TPU v7x, 256 devices: a whole 4x4x8 slice. The times are simulated.
256 devices in a mesh: row: 16 (over z, y_hi), col: 16 (over x, y_lo, core).
Axes of the slice: x: 4, y: 4 (y_hi: 2, y_lo: 2; y = y_hi * 2 + y_lo), z: 8, core: 2. Of those that a mesh axis runs over, the one named last changes fastest.
Arguments:
- grad_out: bfloat16 [16, 4096, 1024], P('row', 'col'), may hold values from -6 to 6
- preact: bfloat16 [16, 4096, 1024], P('row', 'col'), may hold values from -8 to 8
- features: bfloat16 [16, 4096, 1024], P('col', 'row'), may hold values from -6 to 6
- weight: bfloat16 [1024, 1024], replicated, may hold values from -0.1875 to 0.1875
- tile_values: bfloat16 [16, 16, 80, 128, 128], P('row', 'col'), may hold values from -0.125 to 0.125
- tile_row: int32 [16, 16, 80], P('row', 'col'), may hold values from 0 to 31, as said below
- tile_col: int32 [16, 16, 80], P('row', 'col'), may hold values from 0 to 31
- tile_count: int32 [16, 16], P('row', 'col'), may hold values from 1 to 80, as said below
Outputs:
- grad_in: bfloat16 [16, 4096, 1024], P('col', 'row')
- grad_weight: float32 [1024, 1024], replicated
Inputs may be any that keep to these rules, and one draw needn't show every extreme that they name: `tile_count`: some block uses all 80 slots. Within a block, the slots below its count name distinct (tile_row, tile_col) pairs; the other slots are ignored.
All inputs are finite; a program needn't handle non-finite values.
Results may differ from a plain program's by a relative error of at most 0.023.
Values may be sent and summed in bfloat16 or wider, within the bound.
No kernel may reach another device: no remote copies, remote signals or barrier semaphores. Data moves between devices by JAX's collectives and lax.ppermute only.
A program may use at most 128 MiB of HBM per device.

v0:
```python
import functools

import jax
import jax.numpy as jnp
from jax import lax
from jax.experimental import pallas as pl
from jax.experimental.pallas import tpu as pltpu
from jax.sharding import Mesh, PartitionSpec as P

ROW = ("z", "yh")
COL = ("x", "yl", "core")
SIDE = ("yh", "x", "yl")
GROUP = 8
CHUNKS = 2
REACH = 2


def silu_grad(grad_out, preact):
    pre_value = preact.astype(jnp.float32)
    sigmoid_val = jax.nn.sigmoid(pre_value)
    scaled = grad_out.astype(jnp.float32) * sigmoid_val * (1.0 + pre_value * (1.0 - sigmoid_val))
    return scaled.astype(jnp.bfloat16)


def tile_kernel(columns, count_ref, send_ref, row_ref, col_ref, blocks_hbm, panel_hbm, *refs):
    outs, (total, blocks_ref, panel_ref, stage, sems) = refs[:-5], refs[-5:]
    chunks = len(columns)
    _, tiles, size, width = stage.shape
    count = count_ref[0]
    loads = [pltpu.make_async_copy(blocks_hbm, blocks_ref, sems.at[0])]
    for c in range(chunks):
        loads.append(pltpu.make_async_copy(
            panel_hbm.at[:, columns[c]:columns[c] + width], panel_ref.at[c], sems.at[1 + c]
        ))
    for copy in loads:
        copy.start()
    total[...] = jnp.zeros_like(total)
    loads[0].wait()
    leaving = []
    for c in range(chunks):
        loads[1 + c].wait()

        def add_group(step, carry):
            for u in range(GROUP):
                slot = step * GROUP + u
                start = pl.multiple_of(row_ref[slot] * size, size)
                place = jnp.where(slot < count, col_ref[slot], tiles)
                total[place] += lax.dot_general(
                    blocks_ref[slot], panel_ref[c, pl.ds(start, size), :], (((0,), (0,)), ((), ())),
                    preferred_element_type=jnp.float32,
                )
            return carry

        lax.fori_loop(0, (count + GROUP - 1) // GROUP, add_group, 0)

        def store(tile, carry):
            stage[c, tile] = total[tile].astype(stage.dtype)
            if c < chunks - 1:
                total[tile] = jnp.zeros((size, width), jnp.float32)
            return carry

        lax.fori_loop(0, tiles, store, 0)
        whole, *pieces = outs[3 * c:3 * c + 3]
        first = 1 + chunks + 3 * c
        for i, ref in enumerate(pieces):
            start = send_ref[2 * c + i] * ref.shape[0]
            leaving.append(pltpu.make_async_copy(stage.at[c, pl.ds(start, ref.shape[0])], ref, sems.at[first + i]))
        leaving.append(pltpu.make_async_copy(stage.at[c], whole, sems.at[first + 2]))
        for copy in leaving[-3:]:
            copy.start()
    for copy in leaving:
        copy.wait()


def tile_sum(panel, columns, width, blocks, row_ids, col_ids, used_count, col_tiles, send):
    slots, size, _ = blocks.shape
    depth = panel.shape[0]
    chunks = len(columns)
    piece = col_tiles // lax.axis_size("z")
    hbm = pl.BlockSpec(memory_space=pl.ANY)
    outs = pl.pallas_call(
        functools.partial(tile_kernel, columns),
        out_shape=[jax.ShapeDtypeStruct((n, size, width), jnp.bfloat16) for n in (col_tiles, piece, piece)] * chunks,
        in_specs=[pl.BlockSpec(memory_space=pltpu.SMEM)] * 4 + [hbm] * 2,
        out_specs=[hbm] * (3 * chunks),
        scratch_shapes=[
            pltpu.VMEM((col_tiles + 1, size, width), jnp.float32),
            pltpu.VMEM(blocks.shape, jnp.bfloat16),
            pltpu.VMEM((chunks, depth, width), jnp.bfloat16),
            pltpu.VMEM((chunks, col_tiles, size, width), jnp.bfloat16),
            pltpu.SemaphoreType.DMA((1 + 4 * chunks,)),
        ],
        compiler_params=pltpu.CompilerParams(vmem_limit_bytes=56 * 2**20),
        cost_estimate=pl.CostEstimate(
            flops=2 * slots * size * size * width * chunks,
            bytes_accessed=2 * (blocks.size + depth * width * chunks + col_tiles * size * width * chunks),
            transcendentals=0,
        ),
    )(used_count, send, row_ids, col_ids, blocks, panel)
    return [outs[3 * c:3 * c + 3] for c in range(chunks)]


def behind(value, others):
    return lax.optimization_barrier((value, others))[0]


def shift(value, axis, way):
    size = lax.axis_size(axis)
    return lax.ppermute(value, axis, [(i, (i + way) % size) for i in range(size)])


def row_sum(partial, pieces, ways):
    size = lax.axis_size("z")
    here = lax.axis_index("z")

    def own(place):
        return lax.dynamic_index_in_dim(partial, jnp.bitwise_and(place, size - 1), 0, keepdims=False)

    arrived = []
    sent = [[] for _ in range(size // 2)]
    for moving, (way, hops) in zip(pieces, ways):
        for hop in range(hops):
            sent[hop].append(moving)
            moving = shift(moving, "z", way)
            left = hops - 1 - hop
            if left:
                moving = (moving.astype(jnp.float32) + own(here + way * left).astype(jnp.float32)).astype(jnp.bfloat16)
        arrived.append(moving)
    arrived.append(own(here))
    half = lax.axis_index("yh")

    def total(which):
        halves = [lax.dynamic_index_in_dim(t.reshape(2, -1, t.shape[-1]), which, 0, keepdims=False) for t in arrived]
        return sum(t.astype(jnp.float32) for t in halves)

    other = shift(total(1 - half).astype(jnp.bfloat16), "yh", 1)
    mixed = (total(half) + other.astype(jnp.float32)).astype(jnp.bfloat16)
    return mixed, sent


def gather_features(turned, reach):
    found = []
    for start in (turned, shift(turned, "yh", 1)):
        near = {0: start}
        for k in range(1, reach + 1):
            near[k], near[-k] = shift(near[k - 1], "z", -1), shift(near[1 - k], "z", 1)
        found.append(near)
    return found


def term_kernel(chunks, reach, place_ref, *refs):
    partials, refs = refs[:chunks], refs[chunks:]
    passing, refs = refs[:2 * chunks], refs[2 * chunks:]
    features, (out_ref, total, left, nodes, sems) = refs[:-5], refs[-5:]
    z, yh, first = place_ref[0], place_ref[1], place_ref[2]
    rows = out_ref.shape[0]
    count = 2 * reach + 1
    depth = features[0].shape[1]
    width = nodes.shape[2]
    groups = []
    used = 0
    for i in range(count):
        group = []
        for h in range(2):
            b = 2 * i + h
            at = slice(b * depth, (b + 1) * depth)
            source = features[h * count + i].at[pl.ds(pl.multiple_of(first * rows, rows), rows), :]
            group.append(pltpu.make_async_copy(source, left.at[:, at], sems.at[used]))
            used += 1
            half = pl.ds(pl.multiple_of(jnp.bitwise_xor(yh, h) * depth, depth), depth)
            for c in range(chunks):
                if abs(i - reach) == reach:
                    source = passing[2 * c + (i > reach)].at[half, :]
                else:
                    source = partials[c].at[jnp.bitwise_and(z + (i - reach), partials[c].shape[0] - 1), half, :]
                group.append(pltpu.make_async_copy(source, nodes.at[c, at, :], sems.at[used]))
                used += 1
        groups.append(group)
    for group in groups:
        for copy in group:
            copy.start()
    steps = [(0, 1), (1, 3), (3, count)]
    for step, (low, high) in enumerate(steps):
        for group in groups[low:high]:
            for copy in group:
                copy.wait()
        inner = slice(low * 2 * depth, high * 2 * depth)

        for c in range(chunks):
            columns = slice(c * width, (c + 1) * width)
            product = jnp.dot(left[:, inner], nodes[c, inner, :], preferred_element_type=jnp.float32)
            if step:
                product = total[:, columns] + product
            if step < len(steps) - 1:
                total[:, columns] = product
            else:
                out_ref[:, columns] = product.astype(out_ref.dtype)


def weight_terms(features, partials, passing, reach, place):
    distances = list(range(-reach, reach + 1))
    features = [near[k] for near in features for k in distances]
    height, depth = features[0].shape
    width = partials[0].shape[2]
    chunks = len(partials)
    blocks = len(features)
    operands = list(partials) + [p for pair in passing for p in pair] + features
    return pl.pallas_call(
        functools.partial(term_kernel, chunks, reach),
        out_shape=jax.ShapeDtypeStruct((height // 2, chunks * width), jnp.bfloat16),
        in_specs=[pl.BlockSpec(memory_space=pltpu.SMEM)] + [pl.BlockSpec(memory_space=pl.ANY)] * len(operands),
        out_specs=pl.BlockSpec(memory_space=pltpu.VMEM),
        scratch_shapes=[
            pltpu.VMEM((height // 2, chunks * width), jnp.float32),
            pltpu.VMEM((height // 2, blocks * depth), jnp.bfloat16),
            pltpu.VMEM((chunks, blocks * depth, width), jnp.bfloat16),
            pltpu.SemaphoreType.DMA(((1 + chunks) * blocks,)),
        ],
        compiler_params=pltpu.CompilerParams(vmem_limit_bytes=56 * 2**20),
        cost_estimate=pl.CostEstimate(
            flops=height * blocks * depth * chunks * width,
            bytes_accessed=2 * blocks * depth * (height // 2 + chunks * width) + height * chunks * width,
            transcendentals=0,
        ),
    )(place, *operands)


def place_kernel(which_ref, half_ref, *refs):
    out_hbm, stage, sem = refs[-3:]
    rows = stage.shape[0]
    stage[...] = half_ref[...].astype(stage.dtype)
    copy = pltpu.make_async_copy(stage, out_hbm.at[pl.ds(pl.multiple_of(which_ref[0] * rows, rows), rows), :], sem)
    copy.start()
    copy.wait()


def place_half(half, which, whole=()):
    rows, width = half.shape
    whole = [whole] if len(whole) else []
    hbm = pl.BlockSpec(memory_space=pl.ANY)
    return pl.pallas_call(
        place_kernel,
        out_shape=jax.ShapeDtypeStruct((2 * rows, width), jnp.float32),
        in_specs=[pl.BlockSpec(memory_space=pltpu.SMEM), pl.BlockSpec(memory_space=pltpu.VMEM)] + [hbm] * len(whole),
        out_specs=hbm,
        scratch_shapes=[pltpu.VMEM((rows, width), jnp.float32), pltpu.SemaphoreType.DMA],
        input_output_aliases={2: 0} if whole else {},
    )(which.reshape(1), half, *whole)


def sum_everywhere(mine, other, second, third):
    side = lax.axis_size(SIDE)
    depth = lax.axis_size("z")
    core = lax.axis_index("core")
    part = mine.astype(jnp.float32) + shift(other, "core", 1).astype(jnp.float32)
    part = part.astype(jnp.bfloat16).reshape(side, -1, part.shape[-1])
    part = lax.all_to_all(part, SIDE, 0, 0, tiled=True)
    part = jnp.sum(part.astype(jnp.float32), axis=0).astype(jnp.bfloat16)
    part = behind(part, second)
    part = lax.all_to_all(jnp.broadcast_to(part[None], (depth,) + part.shape), "z", 0, 0, tiled=True)
    part = jnp.sum(part.astype(jnp.float32), axis=0).astype(jnp.bfloat16)
    part = behind(part, third)
    half = lax.all_to_all(jnp.broadcast_to(part[None], (side,) + part.shape), SIDE, 0, 0, tiled=True)
    half = half.reshape(-1, half.shape[-1])
    return place_half(shift(half, "core", 1), 1 - core, place_half(half, core))


def per_device(grad_out, preact, features, weight, tile_values, tile_row, tile_col, tile_count):
    size = tile_values.shape[-1]
    width = grad_out.shape[-1] // CHUNKS
    col_tiles = features.shape[1] * lax.axis_size(ROW) // size
    tiles = (tile_values[0, 0], tile_row[0, 0], tile_col[0, 0], tile_count[0], col_tiles)
    z, depth = lax.axis_index("z"), lax.axis_size("z")

    panel = lax.all_gather(silu_grad(grad_out[0], preact[0]), COL, axis=0, tiled=True)
    near = gather_features(features[0].T, REACH)
    ways = (((1, 4), (-1, 3)), ((1, 3), (-1, 4)))
    before = [near_by[k] for near_by in near for k in (REACH, -REACH)]
    partials = []
    passing = []
    mixed = []
    sent = [[] for _ in range(depth // 2)]
    send = jnp.stack([jnp.bitwise_and(z + way * hops, depth - 1) for pair in ways for way, hops in pair])
    columns = tuple(c * width for c in range(CHUNKS))
    chunks = tile_sum(panel, columns, width, *tiles, behind(send, before))
    for (whole, *pieces), pair in zip(chunks, ways):
        partials.append(whole.reshape(depth, -1, width))
        total, moves = row_sum(partials[-1], [p.reshape(-1, width) for p in pieces], pair)
        mixed.append(total)
        for hop, sums in enumerate(moves):
            sent[hop] += sums
        far = {way: moves[hops - REACH][i] for i, (way, hops) in enumerate(pair)}
        passing.append((far[-1], far[1]))
    core = lax.axis_index("core")
    theirs, ours = [jnp.stack([z, lax.axis_index("yh"), half]) for half in (1 - core, core)]
    theirs = weight_terms(near, partials, passing, REACH, theirs)
    ours = weight_terms(near, partials, passing, REACH, behind(ours, theirs))
    grad_weight = sum_everywhere(ours, theirs, sent[3], mixed)
    grad_in = lax.dot_general(
        jnp.concatenate(mixed, axis=1), weight, (((1,), (1,)), ((), ())), preferred_element_type=jnp.float32
    )
    return (grad_in.astype(jnp.bfloat16)[None], grad_weight)


def solution(mesh):
    devices = mesh.devices.reshape(8, 2, 4, 2, 2)
    fine = Mesh(devices, ROW + COL)
    return jax.shard_map(
        per_device,
        mesh=fine,
        in_specs=(
            P(ROW, COL, None),
            P(ROW, COL, None),
            P(COL, ROW, None),
            P(),
            P(ROW, COL, None, None, None),
            P(ROW, COL, None),
            P(ROW, COL, None),
            P(ROW, COL),
        ),
        out_specs=(P(COL, ROW, None), P()),
        check_vma=False,
    )
```

profile of v0, /device:TPU:1, one launch (start us, length us, event | category | flops | bytes accessed | tf_op | source)
XLA Modules:
  0.0 249.9 jit_solution(1716904529166556542)
XLA Ops:
  7.2 2.6 %fusion.6 = bf16[256,1024]{1,0:T(8,128)(2,1)} fusion(bf16[1,256,1024]{2,1,0:T(8,128)(2,1)} %param.8, bf16[1,256,1024]{2,1,0:T(8,128)(2,1)} %param.9), kind=kLoop, calls=%fused_computation.10 | loop fusion | flops 2883584 | bytes 1572864 | tf_op jit(solution)/shard_map/convert_element_type | solution.py:22
  9.8 1.2 copy.12
  11.1 3.8 %collective-permute-start.4 = (bf16[1024,256]{1,0:T(8,128)(2,1)S(1)}, bf16[1024,256]{1,0:T(8,128)(2,1)S(1)}, u32[]{:S(2)}, u32[]{:S(2)}) collective-permute-start(bf16[1024,256]{1,0:T(8,128)(2,1)S(1)} %bitcast.93), channel_id=1, source_target_pairs={{0,16},{16,0},{1,17},{17,1},{2,18},{18,2},{3,19},{19,3},{4,20},{20... | collective-permute-start | bytes 1572872 | tf_op jit(solution)/shard_map/ppermute | solution.py:109
  14.9 5.6 %collective-permute-start = (bf16[1024,256]{1,0:T(8,128)(2,1)S(1)}, bf16[1024,256]{1,0:T(8,128)(2,1)}, u32[]{:S(2)}, u32[]{:S(2)}) collective-permute-start(bf16[1024,256]{1,0:T(8,128)(2,1)S(1)} %bitcast.94), channel_id=1, source_target_pairs={{0,224},{32,0},{64,32},{96,64},{128,96},{160,128},{192,160},{224,1... | collective-permute-start | bytes 1572872 | tf_op jit(solution)/shard_map/ppermute | solution.py:109
  20.5 5.0 %collective-permute-done.4.refs_13_ = bf16[1024,256]{1,0:T(8,128)(2,1)S(1)} collective-permute-done((bf16[1024,256]{1,0:T(8,128)(2,1)S(1)}, bf16[1024,256]{1,0:T(8,128)(2,1)S(1)}, u32[]{:S(2)}, u32[]{:S(2)}) %collective-permute-start.4) | collective-permute-done | bytes 524320 | tf_op jit(solution)/shard_map/ppermute | solution.py:109
  25.5 7.3 %collective-permute-start.5 = (bf16[1024,256]{1,0:T(8,128)(2,1)S(1)}, bf16[1024,256]{1,0:T(8,128)(2,1)}, u32[]{:S(2)}, u32[]{:S(2)}) collective-permute-start(bf16[1024,256]{1,0:T(8,128)(2,1)S(1)} %collective-permute-done.4.refs_13_), channel_id=1, source_target_pairs={{0,224},{32,0},{64,32},{96,64},{128,96},{160,128},{192,160},{224,1... | collective-permute-start | bytes 1572872 | tf_op jit(solution)/shard_map/ppermute | solution.py:109
  32.8 2.7 %collective-permute-start.1 = (bf16[1024,256]{1,0:T(8,128)(2,1)}, bf16[1024,256]{1,0:T(8,128)(2,1)}, u32[]{:S(2)}, u32[]{:S(2)}) collective-permute-start(bf16[1024,256]{1,0:T(8,128)(2,1)} %collective-permute-done.refs_9_), channel_id=1, source_target_pairs={{0,224},{32,0},{64,32},{96,64},{128,96},{160,128},{192,160},{224,1... | collective-permute-start | bytes 1572872 | tf_op jit(solution)/shard_map/ppermute | solution.py:109
  35.4 4.7 %collective-permute-done.5.refs_14_ = bf16[1024,256]{1,0:T(8,128)(2,1)} collective-permute-done((bf16[1024,256]{1,0:T(8,128)(2,1)S(1)}, bf16[1024,256]{1,0:T(8,128)(2,1)}, u32[]{:S(2)}, u32[]{:S(2)}) %collective-permute-start.5) | collective-permute-done | bytes 524320 | tf_op jit(solution)/shard_map/ppermute | solution.py:109
  40.1 3.5 %collective-permute-start.6 = (bf16[1024,256]{1,0:T(8,128)(2,1)}, bf16[1024,256]{1,0:T(8,128)(2,1)}, u32[]{:S(2)}, u32[]{:S(2)}) collective-permute-start(bf16[1024,256]{1,0:T(8,128)(2,1)} %collective-permute-done.5.refs_14_), channel_id=1, source_target_pairs={{0,224},{32,0},{64,32},{96,64},{128,96},{160,128},{192,160},{224,1... | collective-permute-start | bytes 1572872 | tf_op jit(solution)/shard_map/ppermute | solution.py:109
  44.3 0.7 pad_add_fusion.send_ref
  45.0 6.5 %collective-permute-done.1.refs_10_ = bf16[1024,256]{1,0:T(8,128)(2,1)} collective-permute-done((bf16[1024,256]{1,0:T(8,128)(2,1)}, bf16[1024,256]{1,0:T(8,128)(2,1)}, u32[]{:S(2)}, u32[]{:S(2)}) %collective-permute-start.1) | collective-permute-done | bytes 524320 | tf_op jit(solution)/shard_map/ppermute | solution.py:109
  51.5 3.1 %collective-permute-done.3.refs_6_ = bf16[1024,256]{1,0:T(8,128)(2,1)} collective-permute-done((bf16[1024,256]{1,0:T(8,128)(2,1)}, bf16[1024,256]{1,0:T(8,128)(2,1)}, u32[]{:S(2)}, u32[]{:S(2)}) %collective-permute-start.3) | collective-permute-done | bytes 524320 | tf_op jit(solution)/shard_map/ppermute | solution.py:109
  54.6 8.1 %collective-permute-done.6.refs_15_ = bf16[1024,256]{1,0:T(8,128)(2,1)} collective-permute-done((bf16[1024,256]{1,0:T(8,128)(2,1)}, bf16[1024,256]{1,0:T(8,128)(2,1)}, u32[]{:S(2)}, u32[]{:S(2)}) %collective-permute-start.6) | collective-permute-done | bytes 524320 | tf_op jit(solution)/shard_map/ppermute | solution.py:109
  62.7 3.1 %collective-permute-done.8.refs_11_ = bf16[1024,256]{1,0:T(8,128)(2,1)} collective-permute-done((bf16[1024,256]{1,0:T(8,128)(2,1)}, bf16[1024,256]{1,0:T(8,128)(2,1)}, u32[]{:S(2)}, u32[]{:S(2)}) %collective-permute-start.8) | collective-permute-done | bytes 524320 | tf_op jit(solution)/shard_map/ppermute | solution.py:109
  65.8 3.5 %all-gather.2.cloned.1.call-done.panel_hbm = bf16[4096,1024]{1,0:T(8,128)(2,1)} async-done(((bf16[256,1024]{1,0:T(8,128)(2,1)}), bf16[4096,1024]{1,0:T(8,128)(2,1)}) %all-gather.2.cloned.1.call-update) | async-done | bytes 8388624 | tf_op jit(solution)/shard_map/all_gather | solution.py:275
  69.3 11.3 %shard_map.95 = (bf16[32,128,512]{2,1,0:T(8,128)(2,1)}, bf16[4,128,512]{2,1,0:T(8,128)(2,1)}, bf16[4,128,512]{2,1,0:T(8,128)(2,1)}, bf16[32,128,512]{2,1,0:T(8,1...) custom-call(s32[1]{0:T(128)} %bitcast.80.count_ref, s32[4]{0:T(128)} %pad_add_fusion.send_ref, ...), custom_call_target="tpu_custom_call" | custom-call | flops 2684354560 | bytes 19398656 | tf_op jit(solution)/shard_map/pallas_call | solution.py:81
  80.6 6.9 %collective-permute-start.9 = (bf16[512,512]{1,0:T(8,128)(2,1)}, bf16[512,512]{1,0:T(8,128)(2,1)S(1)}, u32[]{:S(2)}, u32[]{:S(2)}) collective-permute-start(bf16[512,512]{1,0:T(8,128)(2,1)} %bitcast.111), channel_id=1, source_target_pairs={{0,32},{32,64},{64,96},{96,128},{128,160},{160,192},{192,224},{224... | collective-permute-start | bytes 1572872 | tf_op jit(solution)/shard_map/ppermute | solution.py:109
  87.5 8.2 %collective-permute-done.9 = bf16[512,512]{1,0:T(8,128)(2,1)S(1)} collective-permute-done((bf16[512,512]{1,0:T(8,128)(2,1)}, bf16[512,512]{1,0:T(8,128)(2,1)S(1)}, u32[]{:S(2)}, u32[]{:S(2)}) %collective-permute-start.9) | collective-permute-done | bytes 524320 | tf_op jit(solution)/shard_map/ppermute | solution.py:109
  95.7 0.8 copy-done.8
  96.5 1.3 fusion.16
  97.8 2.5 collective-permute-start.10
  100.3 0.6 collective-permute-start.17
  100.9 0.8 copy-done.7
  101.7 1.3 fusion.9
  103.0 2.2 collective-permute-start.21
  105.2 0.6 pad_add_fusion.3.place_ref
  105.8 3.6 %collective-permute-done.13 = bf16[512,512]{1,0:T(8,128)(2,1)} collective-permute-done((bf16[512,512]{1,0:T(8,128)(2,1)}, bf16[512,512]{1,0:T(8,128)(2,1)}, u32[]{:S(2)}, u32[]{:S(2)}) %collective-permute-start.13) | collective-permute-done | bytes 524320 | tf_op jit(solution)/shard_map/ppermute | solution.py:109
  109.4 0.9 collective-permute-done.10
  110.3 2.8 %fusion.15 = (bf16[512,512]{1,0:T(8,128)(2,1)}, bf16[512,512]{1,0:T(8,128)(2,1)}) fusion(bf16[512,512]{1,0:T(8,128)(2,1)} %collective-permute-done.10, bf16[8,512,512]{2,1,0:T(8,128)(2,1)} %bitcast.88, s32[]{:T(128)S(6)} %select_n.45, s32[]{:T(128)S(6)} %select_n.48, bf16[512,512]{1,0:T(8,128)(2,1)} %collective-permute-done.13), kind=kLoop, calls=%fused_computation.28 | loop fusion | flops 2097152 | bytes 3145736 | tf_op jit(solution)/shard_map/convert_element_type | solution.py:127
  113.1 8.5 %collective-permute-done.17 = bf16[512,512]{1,0:T(8,128)(2,1)} collective-permute-done((bf16[512,512]{1,0:T(8,128)(2,1)}, bf16[512,512]{1,0:T(8,128)(2,1)}, u32[]{:S(2)}, u32[]{:S(2)}) %collective-permute-start.17) | collective-permute-done | bytes 524320 | tf_op jit(solution)/shard_map/ppermute | solution.py:109
  121.7 2.8 %fusion.11 = (bf16[512,512]{1,0:T(8,128)(2,1)}, bf16[512,512]{1,0:T(8,128)(2,1)}) fusion(bf16[512,512]{1,0:T(8,128)(2,1)} %collective-permute-done.17, bf16[8,512,512]{2,1,0:T(8,128)(2,1)} %bitcast.82, s32[]{:T(128)S(6)} %select_n.45, s32[]{:T(128)S(6)} %select_n.48, bf16[512,512]{1,0:T(8,128)(2,1)} %collective-permute-done.21), kind=kLoop, calls=%fused_computation.20 | loop fusion | flops 2097152 | bytes 3145736 | tf_op jit(solution)/shard_map/convert_element_type | solution.py:127
  124.4 6.6 %shard_map.96 = bf16[512,1024]{1,0:T(8,128)(2,1)} custom-call(s32[3]{0:T(128)} %pad_add_fusion.3.place_ref, bf16[8,512,512]{2,1,0:T(8,128)(2,1)} %bitcast.89, bf16[8,512,512]{2,1,0:T(8,128)(2,1)} %bitcast.83, bf16[512,512]{1,0:T(8,128)(2,1)} %get-tuple-element.25.refs_2_, bf16[512,512]{1,0:T(8,128)(2,1)} %get-tuple-element.24.refs_3_, ...), custom_call_target="tpu_custom_call" | custom-call | flops 2684354560 | bytes 8912896 | tf_op jit(solution)/shard_map/pallas_call | solution.py:208
  131.0 3.4 %collective-permute-start.25 = (bf16[512,1024]{1,0:T(8,128)(2,1)}, bf16[512,1024]{1,0:T(8,128)(2,1)S(1)}, u32[]{:S(2)}, u32[]{:S(2)}) collective-permute-start(bf16[512,1024]{1,0:T(8,128)(2,1)} %shard_map.96), channel_id=1, source_target_pairs={{0,1},{1,0},{2,3},{3,2},{4,5},{5,4},{6,7},{7,6},{8,9},{9,8},{10,11... | collective-permute-start | bytes 3145736 | tf_op jit(solution)/shard_map/ppermute | solution.py:109
  134.5 0.6 pad_add_fusion.1.place_ref
  135.1 1.0 collective-permute-start.11
  136.1 1.7 collective-permute-start.14
  137.8 6.6 %shard_map.97 = bf16[512,1024]{1,0:T(8,128)(2,1)} custom-call(s32[3]{0:T(128)} %pad_add_fusion.1.place_ref, bf16[8,512,512]{2,1,0:T(8,128)(2,1)} %bitcast.90, bf16[8,512,512]{2,1,0:T(8,128)(2,1)} %bitcast.84, bf16[512,512]{1,0:T(8,128)(2,1)} %get-tuple-element.25.refs_2_, bf16[512,512]{1,0:T(8,128)(2,1)} %get-tuple-element.24.refs_3_, ...), custom_call_target="tpu_custom_call" | custom-call | flops 2684354560 | bytes 8912896 | tf_op jit(solution)/shard_map/pallas_call | solution.py:208
  144.4 2.7 %add_convert_fusion = bf16[512,1024]{1,0:T(8,128)(2,1)} fusion(bf16[512,1024]{1,0:T(8,128)(2,1)S(1)} %collective-permute-done.25, bf16[512,1024]{1,0:T(8,128)(2,1)} %shard_map.97), kind=kLoop, calls=%fused_computation | loop fusion | flops 2097152 | bytes 3145728 | tf_op jit(solution)/shard_map/convert_element_type | solution.py:256
  147.1 12.0 %all-to-all-start = ((bf16[16,32,1024]{2,1,0:T(8,128)(2,1)}), bf16[16,32,1024]{2,1,0:T(8,128)(2,1)}, u32[]{:S(2)}, u32[]{:S(2)}) async-start(bf16[16,32,1024]{2,1,0:T(8,128)(2,1)} %bitcast.98), calls=%async_computation | async-start | bytes 2097152 | tf_op jit(solution)/shard_map/all_to_all | solution.py:257
  159.2 2.7 %collective-permute-start.22 = (bf16[512,512]{1,0:T(8,128)(2,1)S(1)}, bf16[512,512]{1,0:T(8,128)(2,1)}, u32[]{:S(2)}, u32[]{:S(2)}) collective-permute-start(bf16[512,512]{1,0:T(8,128)(2,1)S(1)} %copy-done.2), channel_id=1, source_target_pairs={{0,224},{32,0},{64,32},{96,64},{128,96},{160,128},{192,160},{224,1... | collective-permute-start | bytes 1572872 | tf_op jit(solution)/shard_map/ppermute | solution.py:109
  161.9 2.8 %fusion.14 = (bf16[512,512]{1,0:T(8,128)(2,1)}, bf16[512,512]{1,0:T(8,128)(2,1)}) fusion(bf16[512,512]{1,0:T(8,128)(2,1)} %collective-permute-done.11, bf16[8,512,512]{2,1,0:T(8,128)(2,1)} %bitcast.91, s32[]{:T(128)S(6)} %select_n.46, s32[]{:T(128)S(6)} %select_n.49, bf16[512,512]{1,0:T(8,128)(2,1)} %collective-permute-done.14), kind=kLoop, calls=%fused_computation.26 | loop fusion | flops 2097152 | bytes 3145736 | tf_op jit(solution)/shard_map/convert_element_type | solution.py:127
  164.7 2.7 %collective-permute-start.15 = (bf16[512,512]{1,0:T(8,128)(2,1)}, bf16[512,512]{1,0:T(8,128)(2,1)}, u32[]{:S(2)}, u32[]{:S(2)}) collective-permute-start(bf16[512,512]{1,0:T(8,128)(2,1)} %get-tuple-element.23), channel_id=1, source_target_pairs={{0,224},{32,0},{64,32},{96,64},{128,96},{160,128},{192,160},{224,1... | collective-permute-start | bytes 1572872 | tf_op jit(solution)/shard_map/ppermute | solution.py:109
  167.4 5.7 %collective-permute-done.18 = bf16[512,512]{1,0:T(8,128)(2,1)} collective-permute-done((bf16[512,512]{1,0:T(8,128)(2,1)S(1)}, bf16[512,512]{1,0:T(8,128)(2,1)}, u32[]{:S(2)}, u32[]{:S(2)}) %collective-permute-start.18) | collective-permute-done | bytes 524320 | tf_op jit(solution)/shard_map/ppermute | solution.py:109
  173.1 2.8 %fusion.10 = (bf16[512,512]{1,0:T(8,128)(2,1)}, bf16[512,512]{1,0:T(8,128)(2,1)}) fusion(bf16[512,512]{1,0:T(8,128)(2,1)} %collective-permute-done.18, bf16[8,512,512]{2,1,0:T(8,128)(2,1)} %bitcast.85, s32[]{:T(128)S(6)} %select_n.46, s32[]{:T(128)S(6)} %select_n.49, bf16[512,512]{1,0:T(8,128)(2,1)} %collective-permute-done.22), kind=kLoop, calls=%fused_computation.18 | loop fusion | flops 2097152 | bytes 3145736 | tf_op jit(solution)/shard_map/convert_element_type | solution.py:127
  175.9 2.7 %collective-permute-start.23 = (bf16[512,512]{1,0:T(8,128)(2,1)}, bf16[512,512]{1,0:T(8,128)(2,1)}, u32[]{:S(2)}, u32[]{:S(2)}) collective-permute-start(bf16[512,512]{1,0:T(8,128)(2,1)} %get-tuple-element.27), channel_id=1, source_target_pairs={{0,224},{32,0},{64,32},{96,64},{128,96},{160,128},{192,160},{224,1... | collective-permute-start | bytes 1572872 | tf_op jit(solution)/shard_map/ppermute | solution.py:109
  178.6 1.4 reduce_sum.24
  180.0 0.8 broadcast_in_dim.7
  180.8 3.5 %all-to-all-start.1 = ((bf16[8,32,1024]{2,1,0:T(8,128)(2,1)}), bf16[8,32,1024]{2,1,0:T(8,128)(2,1)S(1)}, u32[]{:S(2)}, u32[]{:S(2)}) async-start(bf16[8,32,1024]{2,1,0:T(8,128)(2,1)} %broadcast_in_dim.7), calls=%async_computation.1 | async-start | bytes 1048576 | tf_op jit(solution)/shard_map/all_to_all | solution.py:260
  184.3 1.1 constant_dynamic-slice_fusion.1
  185.4 1.8 fusion.22
  187.3 2.5 %collective-permute-start.16 = (bf16[256,512]{1,0:T(8,128)(2,1)}, bf16[256,512]{1,0:T(8,128)(2,1)S(1)}, u32[]{:S(2)}, u32[]{:S(2)}) collective-permute-start(bf16[256,512]{1,0:T(8,128)(2,1)} %fusion.22), channel_id=1, source_target_pairs={{0,16},{16,0},{1,17},{17,1},{2,18},{18,2},{3,19},{19,3},{4,20},{20... | collective-permute-start | bytes 786440 | tf_op jit(solution)/shard_map/ppermute | solution.py:109
  189.8 1.1 constant_dynamic-slice_fusion
  190.9 5.8 %collective-permute-done.19 = bf16[512,512]{1,0:T(8,128)(2,1)} collective-permute-done((bf16[512,512]{1,0:T(8,128)(2,1)}, bf16[512,512]{1,0:T(8,128)(2,1)}, u32[]{:S(2)}, u32[]{:S(2)}) %collective-permute-start.19) | collective-permute-done | bytes 524320 | tf_op jit(solution)/shard_map/ppermute | solution.py:109
  196.7 1.8 fusion.23
  198.6 2.5 %collective-permute-start.24 = (bf16[256,512]{1,0:T(8,128)(2,1)}, bf16[256,512]{1,0:T(8,128)(2,1)}, u32[]{:S(2)}, u32[]{:S(2)}) collective-permute-start(bf16[256,512]{1,0:T(8,128)(2,1)} %fusion.23), channel_id=1, source_target_pairs={{0,16},{16,0},{1,17},{17,1},{2,18},{18,2},{3,19},{19,3},{4,20},{20... | collective-permute-start | bytes 786440 | tf_op jit(solution)/shard_map/ppermute | solution.py:109
  201.1 1.9 fusion.21
  203.0 2.7 %collective-permute-done.24 = bf16[256,512]{1,0:T(8,128)(2,1)} collective-permute-done((bf16[256,512]{1,0:T(8,128)(2,1)}, bf16[256,512]{1,0:T(8,128)(2,1)}, u32[]{:S(2)}, u32[]{:S(2)}) %collective-permute-start.24) | collective-permute-done | bytes 262176 | tf_op jit(solution)/shard_map/ppermute | solution.py:109
  205.6 2.0 fusion.20
  207.7 0.1 broadcast_in_dim.8
  207.9 18.0 %all_to_all.15 = bf16[16,32,1024]{2,1,0:T(8,128)(2,1)S(1)} all-to-all(bf16[16,32,1024]{2,1,0:T(8,128)(2,1)S(1)} %broadcast_in_dim.8), channel_id=1, replica_groups=mesh['z'=8,'yh'=2,'x'=4,'yl'=2,'core'=2] {'yh','x','yl'}, dimensions={0} | all-to-all | bytes 2097152 | tf_op jit(solution)/shard_map/all_to_all | solution.py:263
  225.9 9.2 %collective-permute-start.26 = (bf16[512,1024]{1,0:T(8,128)(2,1)S(1)}, bf16[512,1024]{1,0:T(8,128)(2,1)}, u32[]{:S(2)}, u32[]{:S(2)}) collective-permute-start(bf16[512,1024]{1,0:T(8,128)(2,1)S(1)} %bitcast.99), channel_id=1, source_target_pairs={{0,1},{1,0},{2,3},{3,2},{4,5},{5,4},{6,7},{7,6},{8,9},{9,8},{10,11... | collective-permute-start | bytes 3145736 | tf_op jit(solution)/shard_map/ppermute | solution.py:109
  235.1 2.5 fusion
  237.6 2.7 %shard_map.98.refs_0_ = f32[1024,1024]{1,0:T(8,128)} custom-call(s32[1]{0:T(128)} %bitcast.44.which_ref, bf16[512,1024]{1,0:T(8,128)(2,1)} %bitcast.100), custom_call_target="tpu_custom_call" | custom-call | tf_op jit(solution)/shard_map/pallas_call | solution.py:241
  240.3 2.7 %shard_map.99 = f32[1024,1024]{1,0:T(8,128)} custom-call(s32[1]{0:T(128)} %bitcast.41.which_ref, bf16[512,1024]{1,0:T(8,128)(2,1)} %collective-permute-done.26.half_ref, f32[1024,1024]{1,0:T(8,128)} %shard_map.98.refs_0_), custom_call_target="tpu_custom_call", output_to_operand_aliasing={{}: (2, {})} | custom-call | tf_op jit(solution)/shard_map/pallas_call | solution.py:241
  (46 shorter events, 0.3 us)
Async XLA Ops:
  7.2 227.9 %copy-start = (bf16[1024,1024]{1,0:T(8,128)(2,1)S(1)}, bf16[1024,1024]{1,0:T(8,128)(2,1)}, u32[]{:S(2)}) copy-start(bf16[1024,1024]{1,0:T(8,128)(2,1)} %param.11) | copy-start | bytes 6291460
  7.2 62.2 %all-gather.2.cloned.1.call-start = ((), (), s32[]{:S(2)}) async-start(), calls=%async_computation.3 | async-start | bytes 8912896 | tf_op jit(solution)/shard_map/all_gather | solution.py:275
  11.1 69.5 %copy-start.1 = (bf16[1,256,1024]{1,2,0:T(8,128)(2,1)}, bf16[1,256,1024]{1,2,0:T(8,128)(2,1)S(1)}, u32[]{:S(2)}) copy-start(bf16[1,256,1024]{1,2,0:T(8,128)(2,1)S(1)} %copy.12) | copy-start | bytes 1572868
  11.1 14.4 %collective-permute-start.4 = (bf16[1024,256]{1,0:T(8,128)(2,1)S(1)}, bf16[1024,256]{1,0:T(8,128)(2,1)S(1)}, u32[]{:S(2)}, u32[]{:S(2)}) collective-permute-start(bf16[1024,256]{1,0:T(8,128)(2,1)S(1)} %bitcast.93), channel_id=1, source_target_pairs={{0,16},{16,0},{1,17},{17,1},{2,18},{18,2},{3,19},{19,3},{4,20},{20... | collective-permute-start | bytes 1572872 | tf_op jit(solution)/shard_map/ppermute | solution.py:109
  14.9 17.9 %collective-permute-start = (bf16[1024,256]{1,0:T(8,128)(2,1)S(1)}, bf16[1024,256]{1,0:T(8,128)(2,1)}, u32[]{:S(2)}, u32[]{:S(2)}) collective-permute-start(bf16[1024,256]{1,0:T(8,128)(2,1)S(1)} %bitcast.94), channel_id=1, source_target_pairs={{0,224},{32,0},{64,32},{96,64},{128,96},{160,128},{192,160},{224,1... | collective-permute-start | bytes 1572872 | tf_op jit(solution)/shard_map/ppermute | solution.py:109
  20.5 15.0 %collective-permute-start.2 = (bf16[1024,256]{1,0:T(8,128)(2,1)S(1)}, bf16[1024,256]{1,0:T(8,128)(2,1)}, u32[]{:S(2)}, u32[]{:S(2)}) collective-permute-start(bf16[1024,256]{1,0:T(8,128)(2,1)S(1)} %bitcast.95), channel_id=1, source_target_pairs={{0,32},{32,64},{64,96},{96,128},{128,160},{160,192},{192,224},{224... | collective-permute-start | bytes 1572872 | tf_op jit(solution)/shard_map/ppermute | solution.py:109
  25.5 55.1 %copy-start.5 = (bf16[1024,256]{1,0:T(8,128)(2,1)}, bf16[1024,256]{1,0:T(8,128)(2,1)S(1)}, u32[]{:S(2)}) copy-start(bf16[1024,256]{1,0:T(8,128)(2,1)S(1)} %collective-permute-done.4.refs_13_) | copy-start | bytes 1572868
  25.5 14.6 %collective-permute-start.5 = (bf16[1024,256]{1,0:T(8,128)(2,1)S(1)}, bf16[1024,256]{1,0:T(8,128)(2,1)}, u32[]{:S(2)}, u32[]{:S(2)}) collective-permute-start(bf16[1024,256]{1,0:T(8,128)(2,1)S(1)} %collective-permute-done.4.refs_13_), channel_id=1, source_target_pairs={{0,224},{32,0},{64,32},{96,64},{128,96},{160,128},{192,160},{224,1... | collective-permute-start | bytes 1572872 | tf_op jit(solution)/shard_map/ppermute | solution.py:109
  32.8 10.9 %collective-permute-start.7 = (bf16[1024,256]{1,0:T(8,128)(2,1)S(1)}, bf16[1024,256]{1,0:T(8,128)(2,1)}, u32[]{:S(2)}, u32[]{:S(2)}) collective-permute-start(bf16[1024,256]{1,0:T(8,128)(2,1)S(1)} %collective-permute-done.4.refs_13_), channel_id=1, source_target_pairs={{0,32},{32,64},{64,96},{96,128},{128,160},{160,192},{192,224},{224... | collective-permute-start | bytes 1572872 | tf_op jit(solution)/shard_map/ppermute | solution.py:109
  32.8 18.7 %collective-permute-start.1 = (bf16[1024,256]{1,0:T(8,128)(2,1)}, bf16[1024,256]{1,0:T(8,128)(2,1)}, u32[]{:S(2)}, u32[]{:S(2)}) collective-permute-start(bf16[1024,256]{1,0:T(8,128)(2,1)} %collective-permute-done.refs_9_), channel_id=1, source_target_pairs={{0,224},{32,0},{64,32},{96,64},{128,96},{160,128},{192,160},{224,1... | collective-permute-start | bytes 1572872 | tf_op jit(solution)/shard_map/ppermute | solution.py:109
  35.4 19.2 %collective-permute-start.3 = (bf16[1024,256]{1,0:T(8,128)(2,1)}, bf16[1024,256]{1,0:T(8,128)(2,1)}, u32[]{:S(2)}, u32[]{:S(2)}) collective-permute-start(bf16[1024,256]{1,0:T(8,128)(2,1)} %collective-permute-done.2.refs_7_), channel_id=1, source_target_pairs={{0,32},{32,64},{64,96},{96,128},{128,160},{160,192},{192,224},{224... | collective-permute-start | bytes 1572872 | tf_op jit(solution)/shard_map/ppermute | solution.py:109
  40.1 22.6 %collective-permute-start.6 = (bf16[1024,256]{1,0:T(8,128)(2,1)}, bf16[1024,256]{1,0:T(8,128)(2,1)}, u32[]{:S(2)}, u32[]{:S(2)}) collective-permute-start(bf16[1024,256]{1,0:T(8,128)(2,1)} %collective-permute-done.5.refs_14_), channel_id=1, source_target_pairs={{0,224},{32,0},{64,32},{96,64},{128,96},{160,128},{192,160},{224,1... | collective-permute-start | bytes 1572872 | tf_op jit(solution)/shard_map/ppermute | solution.py:109
  43.6 22.2 %collective-permute-start.8 = (bf16[1024,256]{1,0:T(8,128)(2,1)}, bf16[1024,256]{1,0:T(8,128)(2,1)}, u32[]{:S(2)}, u32[]{:S(2)}) collective-permute-start(bf16[1024,256]{1,0:T(8,128)(2,1)} %collective-permute-done.7.refs_12_), channel_id=1, source_target_pairs={{0,32},{32,64},{64,96},{96,128},{128,160},{160,192},{192,224},{224... | collective-permute-start | bytes 1572872 | tf_op jit(solution)/shard_map/ppermute | solution.py:109
  80.6 15.1 %collective-permute-start.9 = (bf16[512,512]{1,0:T(8,128)(2,1)}, bf16[512,512]{1,0:T(8,128)(2,1)S(1)}, u32[]{:S(2)}, u32[]{:S(2)}) collective-permute-start(bf16[512,512]{1,0:T(8,128)(2,1)} %bitcast.111), channel_id=1, source_target_pairs={{0,32},{32,64},{64,96},{96,128},{128,160},{160,192},{192,224},{224... | collective-permute-start | bytes 1572872 | tf_op jit(solution)/shard_map/ppermute | solution.py:109
  87.5 13.4 %collective-permute-start.20 = (bf16[512,512]{1,0:T(8,128)(2,1)}, bf16[512,512]{1,0:T(8,128)(2,1)S(1)}, u32[]{:S(2)}, u32[]{:S(2)}) collective-permute-start(bf16[512,512]{1,0:T(8,128)(2,1)} %bitcast.110), channel_id=1, source_target_pairs={{0,224},{32,0},{64,32},{96,64},{128,96},{160,128},{192,160},{224,1... | collective-permute-start | bytes 1572872 | tf_op jit(solution)/shard_map/ppermute | solution.py:109
  87.5 21.9 %collective-permute-start.13 = (bf16[512,512]{1,0:T(8,128)(2,1)}, bf16[512,512]{1,0:T(8,128)(2,1)}, u32[]{:S(2)}, u32[]{:S(2)}) collective-permute-start(bf16[512,512]{1,0:T(8,128)(2,1)} %bitcast.109), channel_id=1, source_target_pairs={{0,224},{32,0},{64,32},{96,64},{128,96},{160,128},{192,160},{224,1... | collective-permute-start | bytes 1572872 | tf_op jit(solution)/shard_map/ppermute | solution.py:109
  95.7 0.8 copy-start.8
  97.8 12.5 %collective-permute-start.10 = (bf16[512,512]{1,0:T(8,128)(2,1)S(1)}, bf16[512,512]{1,0:T(8,128)(2,1)}, u32[]{:S(2)}, u32[]{:S(2)}) collective-permute-start(bf16[512,512]{1,0:T(8,128)(2,1)S(1)} %fusion.16), channel_id=1, source_target_pairs={{0,32},{32,64},{64,96},{96,128},{128,160},{160,192},{192,224},{224... | collective-permute-start | bytes 1572872 | tf_op jit(solution)/shard_map/ppermute | solution.py:109
  100.3 21.4 %collective-permute-start.17 = (bf16[512,512]{1,0:T(8,128)(2,1)}, bf16[512,512]{1,0:T(8,128)(2,1)}, u32[]{:S(2)}, u32[]{:S(2)}) collective-permute-start(bf16[512,512]{1,0:T(8,128)(2,1)} %bitcast.108), channel_id=1, source_target_pairs={{0,32},{32,64},{64,96},{96,128},{128,160},{160,192},{192,224},{224... | collective-permute-start | bytes 1572872 | tf_op jit(solution)/shard_map/ppermute | solution.py:109
  100.9 0.8 copy-start.7
  103.0 18.6 %collective-permute-start.21 = (bf16[512,512]{1,0:T(8,128)(2,1)S(1)}, bf16[512,512]{1,0:T(8,128)(2,1)}, u32[]{:S(2)}, u32[]{:S(2)}) collective-permute-start(bf16[512,512]{1,0:T(8,128)(2,1)S(1)} %fusion.9), channel_id=1, source_target_pairs={{0,224},{32,0},{64,32},{96,64},{128,96},{160,128},{192,160},{224,1... | collective-permute-start | bytes 1572872 | tf_op jit(solution)/shard_map/ppermute | solution.py:109
  131.0 13.4 %collective-permute-start.25 = (bf16[512,1024]{1,0:T(8,128)(2,1)}, bf16[512,1024]{1,0:T(8,128)(2,1)S(1)}, u32[]{:S(2)}, u32[]{:S(2)}) collective-permute-start(bf16[512,1024]{1,0:T(8,128)(2,1)} %shard_map.96), channel_id=1, source_target_pairs={{0,1},{1,0},{2,3},{3,2},{4,5},{5,4},{6,7},{7,6},{8,9},{9,8},{10,11... | collective-permute-start | bytes 3145736 | tf_op jit(solution)/shard_map/ppermute | solution.py:109
  135.1 26.8 %collective-permute-start.11 = (bf16[512,512]{1,0:T(8,128)(2,1)}, bf16[512,512]{1,0:T(8,128)(2,1)}, u32[]{:S(2)}, u32[]{:S(2)}) collective-permute-start(bf16[512,512]{1,0:T(8,128)(2,1)} %get-tuple-element.24.refs_3_), channel_id=1, source_target_pairs={{0,32},{32,64},{64,96},{96,128},{128,160},{160,192},{192,224},{224... | collective-permute-start | bytes 1572872 | tf_op jit(solution)/shard_map/ppermute | solution.py:109
  136.1 25.8 %collective-permute-start.14 = (bf16[512,512]{1,0:T(8,128)(2,1)}, bf16[512,512]{1,0:T(8,128)(2,1)}, u32[]{:S(2)}, u32[]{:S(2)}) collective-permute-start(bf16[512,512]{1,0:T(8,128)(2,1)} %get-tuple-element.25.refs_2_), channel_id=1, source_target_pairs={{0,224},{32,0},{64,32},{96,64},{128,96},{160,128},{192,160},{224,1... | collective-permute-start | bytes 1572872 | tf_op jit(solution)/shard_map/ppermute | solution.py:109
  144.4 14.8 %copy-start.3 = (bf16[512,512]{1,0:T(8,128)(2,1)S(1)}, bf16[512,512]{1,0:T(8,128)(2,1)}, u32[]{:S(2)}) copy-start(bf16[512,512]{1,0:T(8,128)(2,1)} %get-tuple-element.28.refs_5_) | copy-start | bytes 1572868
  144.4 14.9 %copy-start.2 = (bf16[512,512]{1,0:T(8,128)(2,1)S(1)}, bf16[512,512]{1,0:T(8,128)(2,1)}, u32[]{:S(2)}) copy-start(bf16[512,512]{1,0:T(8,128)(2,1)} %get-tuple-element.29.refs_4_) | copy-start | bytes 1572868
  147.1 31.5 %all-to-all-start = ((bf16[16,32,1024]{2,1,0:T(8,128)(2,1)}), bf16[16,32,1024]{2,1,0:T(8,128)(2,1)}, u32[]{:S(2)}, u32[]{:S(2)}) async-start(bf16[16,32,1024]{2,1,0:T(8,128)(2,1)} %bitcast.98), calls=%async_computation | async-start | bytes 2097152 | tf_op jit(solution)/shard_map/all_to_all | solution.py:257
  159.1 14.0 %collective-permute-start.18 = (bf16[512,512]{1,0:T(8,128)(2,1)S(1)}, bf16[512,512]{1,0:T(8,128)(2,1)}, u32[]{:S(2)}, u32[]{:S(2)}) collective-permute-start(bf16[512,512]{1,0:T(8,128)(2,1)S(1)} %copy-done.3), channel_id=1, source_target_pairs={{0,32},{32,64},{64,96},{96,128},{128,160},{160,192},{192,224},{224... | collective-permute-start | bytes 1572872 | tf_op jit(solution)/shard_map/ppermute | solution.py:109
  159.2 13.9 %collective-permute-start.22 = (bf16[512,512]{1,0:T(8,128)(2,1)S(1)}, bf16[512,512]{1,0:T(8,128)(2,1)}, u32[]{:S(2)}, u32[]{:S(2)}) collective-permute-start(bf16[512,512]{1,0:T(8,128)(2,1)S(1)} %copy-done.2), channel_id=1, source_target_pairs={{0,224},{32,0},{64,32},{96,64},{128,96},{160,128},{192,160},{224,1... | collective-permute-start | bytes 1572872 | tf_op jit(solution)/shard_map/ppermute | solution.py:109
  164.7 20.7 %collective-permute-start.12 = (bf16[512,512]{1,0:T(8,128)(2,1)}, bf16[512,512]{1,0:T(8,128)(2,1)}, u32[]{:S(2)}, u32[]{:S(2)}) collective-permute-start(bf16[512,512]{1,0:T(8,128)(2,1)} %get-tuple-element.22), channel_id=1, source_target_pairs={{0,32},{32,64},{64,96},{96,128},{128,160},{160,192},{192,224},{224... | collective-permute-start | bytes 1572872 | tf_op jit(solution)/shard_map/ppermute | solution.py:109
  164.7 20.7 %collective-permute-start.15 = (bf16[512,512]{1,0:T(8,128)(2,1)}, bf16[512,512]{1,0:T(8,128)(2,1)}, u32[]{:S(2)}, u32[]{:S(2)}) collective-permute-start(bf16[512,512]{1,0:T(8,128)(2,1)} %get-tuple-element.23), channel_id=1, source_target_pairs={{0,224},{32,0},{64,32},{96,64},{128,96},{160,128},{192,160},{224,1... | collective-permute-start | bytes 1572872 | tf_op jit(solution)/shard_map/ppermute | solution.py:109
  175.9 20.8 %collective-permute-start.19 = (bf16[512,512]{1,0:T(8,128)(2,1)}, bf16[512,512]{1,0:T(8,128)(2,1)}, u32[]{:S(2)}, u32[]{:S(2)}) collective-permute-start(bf16[512,512]{1,0:T(8,128)(2,1)} %get-tuple-element.26), channel_id=1, source_target_pairs={{0,32},{32,64},{64,96},{96,128},{128,160},{160,192},{192,224},{224... | collective-permute-start | bytes 1572872 | tf_op jit(solution)/shard_map/ppermute | solution.py:109
  175.9 20.8 %collective-permute-start.23 = (bf16[512,512]{1,0:T(8,128)(2,1)}, bf16[512,512]{1,0:T(8,128)(2,1)}, u32[]{:S(2)}, u32[]{:S(2)}) collective-permute-start(bf16[512,512]{1,0:T(8,128)(2,1)} %get-tuple-element.27), channel_id=1, source_target_pairs={{0,224},{32,0},{64,32},{96,64},{128,96},{160,128},{192,160},{224,1... | collective-permute-start | bytes 1572872 | tf_op jit(solution)/shard_map/ppermute | solution.py:109
  180.8 26.8 %all-to-all-start.1 = ((bf16[8,32,1024]{2,1,0:T(8,128)(2,1)}), bf16[8,32,1024]{2,1,0:T(8,128)(2,1)S(1)}, u32[]{:S(2)}, u32[]{:S(2)}) async-start(bf16[8,32,1024]{2,1,0:T(8,128)(2,1)} %broadcast_in_dim.7), calls=%async_computation.1 | async-start | bytes 1048576 | tf_op jit(solution)/shard_map/all_to_all | solution.py:260
  187.3 13.8 %collective-permute-start.16 = (bf16[256,512]{1,0:T(8,128)(2,1)}, bf16[256,512]{1,0:T(8,128)(2,1)S(1)}, u32[]{:S(2)}, u32[]{:S(2)}) collective-permute-start(bf16[256,512]{1,0:T(8,128)(2,1)} %fusion.22), channel_id=1, source_target_pairs={{0,16},{16,0},{1,17},{17,1},{2,18},{18,2},{3,19},{19,3},{4,20},{20... | collective-permute-start | bytes 786440 | tf_op jit(solution)/shard_map/ppermute | solution.py:109
  190.9 5.9 %copy-start.6 = (bf16[1,512,512]{2,1,0:T(8,128)(2,1)}, bf16[1,512,512]{2,1,0:T(8,128)(2,1)S(1)}, u32[]{:S(2)}) copy-start(bf16[1,512,512]{2,1,0:T(8,128)(2,1)S(1)} %constant_dynamic-slice_fusion) | copy-start | bytes 1572868
  198.6 7.0 %collective-permute-start.24 = (bf16[256,512]{1,0:T(8,128)(2,1)}, bf16[256,512]{1,0:T(8,128)(2,1)}, u32[]{:S(2)}, u32[]{:S(2)}) collective-permute-start(bf16[256,512]{1,0:T(8,128)(2,1)} %fusion.23), channel_id=1, source_target_pairs={{0,16},{16,0},{1,17},{17,1},{2,18},{18,2},{3,19},{19,3},{4,20},{20... | collective-permute-start | bytes 786440 | tf_op jit(solution)/shard_map/ppermute | solution.py:109
  203.0 32.1 %copy-start.9 = (bf16[256,512]{1,0:T(8,128)(2,1)S(1)}, bf16[256,512]{1,0:T(8,128)(2,1)}, u32[]{:S(2)}) copy-start(bf16[256,512]{1,0:T(8,128)(2,1)} %fusion.21) | copy-start | bytes 786436
  225.9 11.8 %copy-start.4 = (bf16[16,32,1024]{2,1,0:T(8,128)(2,1)}, bf16[16,32,1024]{2,1,0:T(8,128)(2,1)S(1)}, u32[]{:S(2)}) copy-start(bf16[16,32,1024]{2,1,0:T(8,128)(2,1)S(1)} %all_to_all.15) | copy-start | bytes 3145732
  225.9 14.5 %collective-permute-start.26 = (bf16[512,1024]{1,0:T(8,128)(2,1)S(1)}, bf16[512,1024]{1,0:T(8,128)(2,1)}, u32[]{:S(2)}, u32[]{:S(2)}) collective-permute-start(bf16[512,1024]{1,0:T(8,128)(2,1)S(1)} %bitcast.99), channel_id=1, source_target_pairs={{0,1},{1,0},{2,3},{3,2},{4,5},{5,4},{6,7},{7,6},{8,9},{9,8},{10,11... | collective-permute-start | bytes 3145736 | tf_op jit(solution)/shard_map/ppermute | solution.py:109
Sparse Core Ops, SparseCore 0:
  10.4 58.8 all-gather.1
where the time goes:
time: 251 us; the launch traced here: 250 us
  starting transfers between devices  79 us (31%)
  waiting for transfers between devices  69.6 us (28%)
  other arithmetic  30.1 us (12%)
  Pallas kernels  29.8 us (12%)
  blocking collectives  18 us (7%)
  between operations  14.9 us (6%)
  local copies, waits for them, and re-layouts  5.99 us (2%)
    ppermute x27, waiting for transfers between devices, shift(): lax.ppermute(value, axis, [(i, (i + way) % size) for i in range(size)])  66 us
    ppermute x27, starting transfers between devices, shift(): lax.ppermute(value, axis, [(i, (i + way) % size) for i in range(size)])  63.4 us
    all_to_all x1, blocking collectives, sum_everywhere(): lax.all_to_all(jnp.broadcast_to(part[None], (side,) + part.shape), SIDE,...  18 us
    convert_element_type x6, other arithmetic, row_sum(): (moving.astype(jnp.float32) + own(here + way * left).astype(jnp.float32))...  13.8 us
    pallas_call x2, Pallas kernels, weight_terms(): pl.pallas_call(functools.partial(term_kernel, chunks, reach), out_shape=j...  13.2 us
    all_to_all x1, starting transfers between devices, sum_everywhere(): part = lax.all_to_all(part, SIDE, 0, 0, tiled=True)  12 us
    pallas_call x1, Pallas kernels, tile_sum(): pl.pallas_call(functools.partial(tile_kernel, columns), out_shape=[jax.Sh...  11.3 us
    pallas_call x2, Pallas kernels, place_half(): pl.pallas_call(place_kernel, out_shape=jax.ShapeDtypeStruct((2 * rows, wi...  5.38 us
  transfers between devices with their start and end apart: 30, of which 14 were waited for; matrix products, arithmetic and copies ran while one was open for 13% of the time, Pallas kernels for 4%

commit v1 on v0

--- a/solution.py
+++ b/solution.py
@@ -32,13 +32,15 @@
         loads.append(pltpu.make_async_copy(
             panel_hbm.at[:, columns[c]:columns[c] + width], panel_ref.at[c], sems.at[1 + c]
         ))
-    for copy in loads:
+    for copy in loads[:2]:
         copy.start()
     total[...] = jnp.zeros_like(total)
     loads[0].wait()
     leaving = []
     for c in range(chunks):
         loads[1 + c].wait()
+        for copy in loads[2 + c:3 + c]:
+            copy.start()
 
         def add_group(step, carry):
             for u in range(GROUP):
@@ -59,15 +61,19 @@
                 total[tile] = jnp.zeros((size, width), jnp.float32)
             return carry
 
-        lax.fori_loop(0, tiles, store, 0)
         whole, *pieces = outs[3 * c:3 * c + 3]
-        first = 1 + chunks + 3 * c
+        depth = pieces[0].shape[0]
+        parts = tiles // depth
+        first = 1 + chunks + (parts + 2) * c
+        for i in range(parts):
+            at = pl.ds(i * depth, depth)
+            lax.fori_loop(i * depth, (i + 1) * depth, store, 0)
+            leaving.append(pltpu.make_async_copy(stage.at[c, at], whole.at[at], sems.at[first + i]))
+            leaving[-1].start()
         for i, ref in enumerate(pieces):
-            start = send_ref[2 * c + i] * ref.shape[0]
-            leaving.append(pltpu.make_async_copy(stage.at[c, pl.ds(start, ref.shape[0])], ref, sems.at[first + i]))
-        leaving.append(pltpu.make_async_copy(stage.at[c], whole, sems.at[first + 2]))
-        for copy in leaving[-3:]:
-            copy.start()
+            at = pl.ds(send_ref[2 * c + i] * depth, depth)
+            leaving.append(pltpu.make_async_copy(stage.at[c, at], ref, sems.at[first + parts + i]))
+            leaving[-1].start()
     for copy in leaving:
         copy.wait()
 
@@ -88,7 +94,7 @@
             pltpu.VMEM(blocks.shape, jnp.bfloat16),
             pltpu.VMEM((chunks, depth, width), jnp.bfloat16),
             pltpu.VMEM((chunks, col_tiles, size, width), jnp.bfloat16),
-            pltpu.SemaphoreType.DMA((1 + 4 * chunks,)),
+            pltpu.SemaphoreType.DMA((1 + chunks + (col_tiles // piece + 2) * chunks,)),
         ],
         compiler_params=pltpu.CompilerParams(vmem_limit_bytes=56 * 2**20),
         cost_estimate=pl.CostEstimate(
@@ -109,13 +115,9 @@
     return lax.ppermute(value, axis, [(i, (i + way) % size) for i in range(size)])
 
 
-def row_sum(partial, pieces, ways):
+def row_chains(partial, pieces, ways):
     size = lax.axis_size("z")
     here = lax.axis_index("z")
-
-    def own(place):
-        return lax.dynamic_index_in_dim(partial, jnp.bitwise_and(place, size - 1), 0, keepdims=False)
-
     arrived = []
     sent = [[] for _ in range(size // 2)]
     for moving, (way, hops) in zip(pieces, ways):
@@ -124,18 +126,29 @@
             moving = shift(moving, "z", way)
             left = hops - 1 - hop
             if left:
-                moving = (moving.astype(jnp.float32) + own(here + way * left).astype(jnp.float32)).astype(jnp.bfloat16)
+                place = jnp.bitwise_and(here + way * left, size - 1)
+                own = lax.dynamic_index_in_dim(partial, place, 0, keepdims=False)
+                moving = (moving.astype(jnp.float32) + own.astype(jnp.float32)).astype(jnp.bfloat16)
         arrived.append(moving)
-    arrived.append(own(here))
+    return arrived, sent
+
+
+def row_sum(partials, arrived):
+    here = lax.axis_index("z")
     half = lax.axis_index("yh")
 
     def total(which):
-        halves = [lax.dynamic_index_in_dim(t.reshape(2, -1, t.shape[-1]), which, 0, keepdims=False) for t in arrived]
-        return sum(t.astype(jnp.float32) for t in halves)
+        sums = []
+        for partial, terms in zip(partials, arrived):
+            width = partial.shape[-1]
+            own = partial.reshape(2 * partial.shape[0], -1, width)
+            parts = [lax.dynamic_index_in_dim(own, 2 * here + which, 0, keepdims=False)]
+            parts += [lax.dynamic_index_in_dim(t.reshape(2, -1, width), which, 0, keepdims=False) for t in terms]
+            sums.append(sum(p.astype(jnp.float32) for p in parts))
+        return jnp.concatenate(sums, axis=1)
 
     other = shift(total(1 - half).astype(jnp.bfloat16), "yh", 1)
-    mixed = (total(half) + other.astype(jnp.float32)).astype(jnp.bfloat16)
-    return mixed, sent
+    return (total(half) + other.astype(jnp.float32)).astype(jnp.bfloat16)
 
 
 def gather_features(turned, reach):
@@ -248,7 +261,7 @@
     )(which.reshape(1), half, *whole)
 
 
-def sum_everywhere(mine, other, second, third):
+def sum_everywhere(mine, other, second):
     side = lax.axis_size(SIDE)
     depth = lax.axis_size("z")
     core = lax.axis_index("core")
@@ -259,7 +272,6 @@
     part = behind(part, second)
     part = lax.all_to_all(jnp.broadcast_to(part[None], (depth,) + part.shape), "z", 0, 0, tiled=True)
     part = jnp.sum(part.astype(jnp.float32), axis=0).astype(jnp.bfloat16)
-    part = behind(part, third)
     half = lax.all_to_all(jnp.broadcast_to(part[None], (side,) + part.shape), SIDE, 0, 0, tiled=True)
     half = half.reshape(-1, half.shape[-1])
     return place_half(shift(half, "core", 1), 1 - core, place_half(half, core))
@@ -278,15 +290,15 @@
     before = [near_by[k] for near_by in near for k in (REACH, -REACH)]
     partials = []
     passing = []
-    mixed = []
+    arrived = []
     sent = [[] for _ in range(depth // 2)]
     send = jnp.stack([jnp.bitwise_and(z + way * hops, depth - 1) for pair in ways for way, hops in pair])
     columns = tuple(c * width for c in range(CHUNKS))
     chunks = tile_sum(panel, columns, width, *tiles, behind(send, before))
     for (whole, *pieces), pair in zip(chunks, ways):
         partials.append(whole.reshape(depth, -1, width))
-        total, moves = row_sum(partials[-1], [p.reshape(-1, width) for p in pieces], pair)
-        mixed.append(total)
+        ends, moves = row_chains(partials[-1], [p.reshape(-1, width) for p in pieces], pair)
+        arrived.append(ends)
         for hop, sums in enumerate(moves):
             sent[hop] += sums
         far = {way: moves[hops - REACH][i] for i, (way, hops) in enumerate(pair)}
@@ -295,9 +307,10 @@
     theirs, ours = [jnp.stack([z, lax.axis_index("yh"), half]) for half in (1 - core, core)]
     theirs = weight_terms(near, partials, passing, REACH, theirs)
     ours = weight_terms(near, partials, passing, REACH, behind(ours, theirs))
-    grad_weight = sum_everywhere(ours, theirs, sent[3], mixed)
+    grad_weight = sum_everywhere(ours, theirs, sent[3])
+    mixed = row_sum(partials, arrived)
     grad_in = lax.dot_general(
-        jnp.concatenate(mixed, axis=1), weight, (((1,), (1,)), ((), ())), preferred_element_type=jnp.float32
+        mixed, weight, (((1,), (1,)), ((), ())), preferred_element_type=jnp.float32
     )
     return (grad_in.astype(jnp.bfloat16)[None], grad_weight)
 

time: 251 us -> 257 us (1.024); the launches traced: 250 us -> 253 us
  waiting for transfers between devices: 69.6 us -> 79.9 us
  starting transfers between devices: 79 us -> 74.6 us
  other arithmetic: 30.1 us -> 26.3 us
    ppermute x27 -> x26, waiting for transfers between devices: 66 us -> 75.4 us  [shift(): lax.ppermute(value, axis, [(i, (i + way) % size) for i in range(size)])]
    convert_element_type x10 -> x6, other arithmetic: 21.4 us -> 13.8 us  [row_chains(): (moving.astype(jnp.float32) + own.astype(jnp.float32)).astype(jnp.bfloat16)]
    all_to_all x1, starting transfers between devices: 12 us -> 7.01 us  [sum_everywhere(): part = lax.all_to_all(part, SIDE, 0, 0, tiled=True)]
    add x0 -> x2, other arithmetic: none -> 3.9 us  [total(): sums.append(sum((p.astype(jnp.float32) for p in parts)))]
    ppermute x27 -> x26, starting transfers between devices: 63.4 us -> 63.2 us  [shift(): lax.ppermute(value, axis, [(i, (i + way) % size) for i in range(size)])]
  transfers between devices with their start and end apart: 30 -> 29, of which waited for: 14 -> 15; matrix products, arithmetic and copies ran while one was open for 13% -> 9% of each run, Pallas kernels for 4% -> 4%
where the time goes in v1:
time: 257 us; the launch traced here: 253 us
  waiting for transfers between devices  79.9 us (31%)
  starting transfers between devices  74.6 us (29%)
  Pallas kernels  30.5 us (12%)
  other arithmetic  26.3 us (10%)
  blocking collectives  19.8 us (8%)
  between operations  14.9 us (6%)
  local copies, waits for them, and re-layouts  4.03 us (2%)
  matrix products  2.61 us (1%)
    ppermute x26, waiting for transfers between devices, shift(): lax.ppermute(value, axis, [(i, (i + way) % size) for i in range(size)])  75.4 us
    ppermute x26, starting transfers between devices, shift(): lax.ppermute(value, axis, [(i, (i + way) % size) for i in range(size)])  63.2 us
    all_to_all x1, blocking collectives, sum_everywhere(): lax.all_to_all(jnp.broadcast_to(part[None], (depth,) + part.shape), 'z',...  19.8 us
    convert_element_type x6, other arithmetic, row_chains(): (moving.astype(jnp.float32) + own.astype(jnp.float32)).astype(jnp.bfloat16)  13.8 us
    pallas_call x2, Pallas kernels, weight_terms(): pl.pallas_call(functools.partial(term_kernel, chunks, reach), out_shape=j...  13.3 us
    pallas_call x1, Pallas kernels, tile_sum(): pl.pallas_call(functools.partial(tile_kernel, columns), out_shape=[jax.Sh...  11.8 us
    all_to_all x1, starting transfers between devices, sum_everywhere(): part = lax.all_to_all(part, SIDE, 0, 0, tiled=True)  7.01 us
    pallas_call x2, Pallas kernels, place_half(): pl.pallas_call(place_kernel, out_shape=jax.ShapeDtypeStruct((2 * rows, wi...  5.38 us
  transfers between devices with their start and end apart: 29, of which 15 were waited for; matrix products, arithmetic and copies ran while one was open for 9% of the time, Pallas kernels for 4%

profile of v1, /device:TPU:1, one launch (start us, length us, event | category | flops | bytes accessed | tf_op | source)
XLA Modules:
  0.0 252.8 jit_solution(3630303109642995774)
XLA Ops:
  7.2 2.6 %fusion.6 = bf16[256,1024]{1,0:T(8,128)(2,1)} fusion(bf16[1,256,1024]{2,1,0:T(8,128)(2,1)} %param.8, bf16[1,256,1024]{2,1,0:T(8,128)(2,1)} %param.9), kind=kLoop, calls=%fused_computation.10 | loop fusion | flops 2883584 | bytes 1572864 | tf_op jit(solution)/shard_map/convert_element_type | solution.py:22
  9.8 1.2 copy.12
  11.1 3.8 %collective-permute-start.4 = (bf16[1024,256]{1,0:T(8,128)(2,1)S(1)}, bf16[1024,256]{1,0:T(8,128)(2,1)S(1)}, u32[]{:S(2)}, u32[]{:S(2)}) collective-permute-start(bf16[1024,256]{1,0:T(8,128)(2,1)S(1)} %bitcast.89), channel_id=1, source_target_pairs={{0,16},{16,0},{1,17},{17,1},{2,18},{18,2},{3,19},{19,3},{4,20},{20... | collective-permute-start | bytes 1572872 | tf_op jit(solution)/shard_map/ppermute | solution.py:115
  14.9 5.6 %collective-permute-start = (bf16[1024,256]{1,0:T(8,128)(2,1)S(1)}, bf16[1024,256]{1,0:T(8,128)(2,1)}, u32[]{:S(2)}, u32[]{:S(2)}) collective-permute-start(bf16[1024,256]{1,0:T(8,128)(2,1)S(1)} %bitcast.90), channel_id=1, source_target_pairs={{0,224},{32,0},{64,32},{96,64},{128,96},{160,128},{192,160},{224,1... | collective-permute-start | bytes 1572872 | tf_op jit(solution)/shard_map/ppermute | solution.py:115
  20.5 5.0 %collective-permute-done.4.refs_13_ = bf16[1024,256]{1,0:T(8,128)(2,1)S(1)} collective-permute-done((bf16[1024,256]{1,0:T(8,128)(2,1)S(1)}, bf16[1024,256]{1,0:T(8,128)(2,1)S(1)}, u32[]{:S(2)}, u32[]{:S(2)}) %collective-permute-start.4) | collective-permute-done | bytes 524320 | tf_op jit(solution)/shard_map/ppermute | solution.py:115
  25.5 7.3 %collective-permute-start.5 = (bf16[1024,256]{1,0:T(8,128)(2,1)S(1)}, bf16[1024,256]{1,0:T(8,128)(2,1)}, u32[]{:S(2)}, u32[]{:S(2)}) collective-permute-start(bf16[1024,256]{1,0:T(8,128)(2,1)S(1)} %collective-permute-done.4.refs_13_), channel_id=1, source_target_pairs={{0,224},{32,0},{64,32},{96,64},{128,96},{160,128},{192,160},{224,1... | collective-permute-start | bytes 1572872 | tf_op jit(solution)/shard_map/ppermute | solution.py:115
  32.8 2.7 %collective-permute-start.1 = (bf16[1024,256]{1,0:T(8,128)(2,1)}, bf16[1024,256]{1,0:T(8,128)(2,1)}, u32[]{:S(2)}, u32[]{:S(2)}) collective-permute-start(bf16[1024,256]{1,0:T(8,128)(2,1)} %collective-permute-done.refs_9_), channel_id=1, source_target_pairs={{0,224},{32,0},{64,32},{96,64},{128,96},{160,128},{192,160},{224,1... | collective-permute-start | bytes 1572872 | tf_op jit(solution)/shard_map/ppermute | solution.py:115
  35.4 4.7 %collective-permute-done.5.refs_14_ = bf16[1024,256]{1,0:T(8,128)(2,1)} collective-permute-done((bf16[1024,256]{1,0:T(8,128)(2,1)S(1)}, bf16[1024,256]{1,0:T(8,128)(2,1)}, u32[]{:S(2)}, u32[]{:S(2)}) %collective-permute-start.5) | collective-permute-done | bytes 524320 | tf_op jit(solution)/shard_map/ppermute | solution.py:115
  40.1 3.5 %collective-permute-start.6 = (bf16[1024,256]{1,0:T(8,128)(2,1)}, bf16[1024,256]{1,0:T(8,128)(2,1)}, u32[]{:S(2)}, u32[]{:S(2)}) collective-permute-start(bf16[1024,256]{1,0:T(8,128)(2,1)} %collective-permute-done.5.refs_14_), channel_id=1, source_target_pairs={{0,224},{32,0},{64,32},{96,64},{128,96},{160,128},{192,160},{224,1... | collective-permute-start | bytes 1572872 | tf_op jit(solution)/shard_map/ppermute | solution.py:115
  44.3 0.6 pad_add_fusion.send_ref
  44.9 6.6 %collective-permute-done.1.refs_10_ = bf16[1024,256]{1,0:T(8,128)(2,1)} collective-permute-done((bf16[1024,256]{1,0:T(8,128)(2,1)}, bf16[1024,256]{1,0:T(8,128)(2,1)}, u32[]{:S(2)}, u32[]{:S(2)}) %collective-permute-start.1) | collective-permute-done | bytes 524320 | tf_op jit(solution)/shard_map/ppermute | solution.py:115
  51.5 3.1 %collective-permute-done.3.refs_6_ = bf16[1024,256]{1,0:T(8,128)(2,1)} collective-permute-done((bf16[1024,256]{1,0:T(8,128)(2,1)}, bf16[1024,256]{1,0:T(8,128)(2,1)}, u32[]{:S(2)}, u32[]{:S(2)}) %collective-permute-start.3) | collective-permute-done | bytes 524320 | tf_op jit(solution)/shard_map/ppermute | solution.py:115
  54.6 8.1 %collective-permute-done.6.refs_15_ = bf16[1024,256]{1,0:T(8,128)(2,1)} collective-permute-done((bf16[1024,256]{1,0:T(8,128)(2,1)}, bf16[1024,256]{1,0:T(8,128)(2,1)}, u32[]{:S(2)}, u32[]{:S(2)}) %collective-permute-start.6) | collective-permute-done | bytes 524320 | tf_op jit(solution)/shard_map/ppermute | solution.py:115
  62.7 3.1 %collective-permute-done.8.refs_11_ = bf16[1024,256]{1,0:T(8,128)(2,1)} collective-permute-done((bf16[1024,256]{1,0:T(8,128)(2,1)}, bf16[1024,256]{1,0:T(8,128)(2,1)}, u32[]{:S(2)}, u32[]{:S(2)}) %collective-permute-start.8) | collective-permute-done | bytes 524320 | tf_op jit(solution)/shard_map/ppermute | solution.py:115
  65.8 3.5 %all-gather.2.cloned.1.call-done.panel_hbm = bf16[4096,1024]{1,0:T(8,128)(2,1)} async-done(((bf16[256,1024]{1,0:T(8,128)(2,1)}), bf16[4096,1024]{1,0:T(8,128)(2,1)}) %all-gather.2.cloned.1.call-update) | async-done | bytes 8388624 | tf_op jit(solution)/shard_map/all_gather | solution.py:287
  69.3 11.8 %shard_map.95 = (bf16[32,128,512]{2,1,0:T(8,128)(2,1)}, bf16[4,128,512]{2,1,0:T(8,128)(2,1)}, bf16[4,128,512]{2,1,0:T(8,128)(2,1)}, bf16[32,128,512]{2,1,0:T(8,1...) custom-call(s32[1]{0:T(128)} %bitcast.76.count_ref, s32[4]{0:T(128)} %pad_add_fusion.send_ref, ...), custom_call_target="tpu_custom_call" | custom-call | flops 2684354560 | bytes 19398656 | tf_op jit(solution)/shard_map/pallas_call | solution.py:87
  81.2 1.4 collective-permute-start.9
  82.5 4.0 %collective-permute-start.19 = (bf16[512,512]{1,0:T(8,128)(2,1)}, bf16[512,512]{1,0:T(8,128)(2,1)S(1)}, u32[]{:S(2)}, u32[]{:S(2)}) collective-permute-start(bf16[512,512]{1,0:T(8,128)(2,1)} %bitcast.102), channel_id=1, source_target_pairs={{0,224},{32,0},{64,32},{96,64},{128,96},{160,128},{192,160},{224,1... | collective-permute-start | bytes 1572872 | tf_op jit(solution)/shard_map/ppermute | solution.py:115
  86.5 1.4 collective-permute-start.13
  87.9 7.1 %collective-permute-done.9 = bf16[512,512]{1,0:T(8,128)(2,1)S(1)} collective-permute-done((bf16[512,512]{1,0:T(8,128)(2,1)}, bf16[512,512]{1,0:T(8,128)(2,1)S(1)}, u32[]{:S(2)}, u32[]{:S(2)}) %collective-permute-start.9) | collective-permute-done | bytes 524320 | tf_op jit(solution)/shard_map/ppermute | solution.py:115
  95.0 0.8 copy-done.7
  95.8 1.3 fusion.17
  97.1 2.2 collective-permute-start.10
  99.3 2.1 collective-permute-start.16
  101.4 0.8 copy-done.6
  102.2 1.3 fusion.10
  103.6 1.6 collective-permute-start.20
  105.1 0.6 pad_add_fusion.3.place_ref
  105.7 6.5 %collective-permute-done.13 = bf16[512,512]{1,0:T(8,128)(2,1)} collective-permute-done((bf16[512,512]{1,0:T(8,128)(2,1)}, bf16[512,512]{1,0:T(8,128)(2,1)}, u32[]{:S(2)}, u32[]{:S(2)}) %collective-permute-start.13) | collective-permute-done | bytes 524320 | tf_op jit(solution)/shard_map/ppermute | solution.py:115
  112.2 0.9 collective-permute-done.10
  113.1 2.8 %fusion.16 = (bf16[512,512]{1,0:T(8,128)(2,1)}, bf16[512,512]{1,0:T(8,128)(2,1)}) fusion(bf16[512,512]{1,0:T(8,128)(2,1)} %collective-permute-done.10, bf16[8,512,512]{2,1,0:T(8,128)(2,1)} %bitcast.84, s32[]{:T(128)S(6)} %select_n.47, s32[]{:T(128)S(6)} %select_n.50, bf16[512,512]{1,0:T(8,128)(2,1)} %collective-permute-done.13), kind=kLoop, calls=%fused_computation.30 | loop fusion | flops 2097152 | bytes 3145736 | tf_op jit(solution)/shard_map/convert_element_type | solution.py:131
  115.9 8.4 %collective-permute-done.16 = bf16[512,512]{1,0:T(8,128)(2,1)} collective-permute-done((bf16[512,512]{1,0:T(8,128)(2,1)}, bf16[512,512]{1,0:T(8,128)(2,1)}, u32[]{:S(2)}, u32[]{:S(2)}) %collective-permute-start.16) | collective-permute-done | bytes 524320 | tf_op jit(solution)/shard_map/ppermute | solution.py:115
  124.3 2.8 %fusion.12 = (bf16[512,512]{1,0:T(8,128)(2,1)}, bf16[512,512]{1,0:T(8,128)(2,1)}) fusion(bf16[512,512]{1,0:T(8,128)(2,1)} %collective-permute-done.16, bf16[8,512,512]{2,1,0:T(8,128)(2,1)} %bitcast.78, s32[]{:T(128)S(6)} %select_n.47, s32[]{:T(128)S(6)} %select_n.50, bf16[512,512]{1,0:T(8,128)(2,1)} %collective-permute-done.20), kind=kLoop, calls=%fused_computation.22 | loop fusion | flops 2097152 | bytes 3145736 | tf_op jit(solution)/shard_map/convert_element_type | solution.py:131
  127.1 6.7 %shard_map.96 = bf16[512,1024]{1,0:T(8,128)(2,1)} custom-call(s32[3]{0:T(128)} %pad_add_fusion.3.place_ref, bf16[8,512,512]{2,1,0:T(8,128)(2,1)} %bitcast.85, bf16[8,512,512]{2,1,0:T(8,128)(2,1)} %bitcast.79, bf16[512,512]{1,0:T(8,128)(2,1)} %get-tuple-element.27.refs_2_, bf16[512,512]{1,0:T(8,128)(2,1)} %get-tuple-element.26.refs_3_, ...), custom_call_target="tpu_custom_call" | custom-call | flops 2684354560 | bytes 8912896 | tf_op jit(solution)/shard_map/pallas_call | solution.py:221
  133.8 2.8 %collective-permute-start.24 = (bf16[512,1024]{1,0:T(8,128)(2,1)}, bf16[512,1024]{1,0:T(8,128)(2,1)S(1)}, u32[]{:S(2)}, u32[]{:S(2)}) collective-permute-start(bf16[512,1024]{1,0:T(8,128)(2,1)} %shard_map.96), channel_id=1, source_target_pairs={{0,1},{1,0},{2,3},{3,2},{4,5},{5,4},{6,7},{7,6},{8,9},{9,8},{10,11... | collective-permute-start | bytes 3145736 | tf_op jit(solution)/shard_map/ppermute | solution.py:115
  136.7 0.6 pad_add_fusion.1.place_ref
  137.3 4.5 %collective-permute-start.14 = (bf16[512,512]{1,0:T(8,128)(2,1)S(1)}, bf16[512,512]{1,0:T(8,128)(2,1)}, u32[]{:S(2)}, u32[]{:S(2)}) collective-permute-start(bf16[512,512]{1,0:T(8,128)(2,1)S(1)} %copy-done.2), channel_id=1, source_target_pairs={{0,224},{32,0},{64,32},{96,64},{128,96},{160,128},{192,160},{224,1... | collective-permute-start | bytes 1572872 | tf_op jit(solution)/shard_map/ppermute | solution.py:115
  141.8 6.6 %shard_map.97 = bf16[512,1024]{1,0:T(8,128)(2,1)} custom-call(s32[3]{0:T(128)} %pad_add_fusion.1.place_ref, bf16[8,512,512]{2,1,0:T(8,128)(2,1)} %bitcast.86, bf16[8,512,512]{2,1,0:T(8,128)(2,1)} %bitcast.80, bf16[512,512]{1,0:T(8,128)(2,1)} %get-tuple-element.27.refs_2_, bf16[512,512]{1,0:T(8,128)(2,1)} %get-tuple-element.26.refs_3_, ...), custom_call_target="tpu_custom_call" | custom-call | flops 2684354560 | bytes 8912896 | tf_op jit(solution)/shard_map/pallas_call | solution.py:221
  148.4 2.7 %add_convert_fusion = bf16[512,1024]{1,0:T(8,128)(2,1)} fusion(bf16[512,1024]{1,0:T(8,128)(2,1)S(1)} %collective-permute-done.24, bf16[512,1024]{1,0:T(8,128)(2,1)} %shard_map.97), kind=kLoop, calls=%fused_computation | loop fusion | flops 2097152 | bytes 3145728 | tf_op jit(solution)/shard_map/convert_element_type | solution.py:269
  151.1 7.0 %all-to-all-start = ((bf16[16,32,1024]{2,1,0:T(8,128)(2,1)}), bf16[16,32,1024]{2,1,0:T(8,128)(2,1)}, u32[]{:S(2)}, u32[]{:S(2)}) async-start(bf16[16,32,1024]{2,1,0:T(8,128)(2,1)} %bitcast.94), calls=%async_computation | async-start | bytes 2097152 | tf_op jit(solution)/shard_map/all_to_all | solution.py:270
  158.1 0.1 collective-permute-start.17
  158.2 2.7 %collective-permute-start.21 = (bf16[512,512]{1,0:T(8,128)(2,1)S(1)}, bf16[512,512]{1,0:T(8,128)(2,1)}, u32[]{:S(2)}, u32[]{:S(2)}) collective-permute-start(bf16[512,512]{1,0:T(8,128)(2,1)S(1)} %copy-done.3), channel_id=1, source_target_pairs={{0,224},{32,0},{64,32},{96,64},{128,96},{160,128},{192,160},{224,1... | collective-permute-start | bytes 1572872 | tf_op jit(solution)/shard_map/ppermute | solution.py:115
  160.9 2.8 %fusion.15 = (bf16[512,512]{1,0:T(8,128)(2,1)}, bf16[512,512]{1,0:T(8,128)(2,1)}) fusion(bf16[512,512]{1,0:T(8,128)(2,1)} %collective-permute-done.11, bf16[8,512,512]{2,1,0:T(8,128)(2,1)} %bitcast.87, s32[]{:T(128)S(6)} %select_n.48, s32[]{:T(128)S(6)} %select_n.51, bf16[512,512]{1,0:T(8,128)(2,1)} %collective-permute-done.14), kind=kLoop, calls=%fused_computation.28 | loop fusion | flops 2097152 | bytes 3145736 | tf_op jit(solution)/shard_map/convert_element_type | solution.py:131
  163.7 8.6 %collective-permute-done.17 = bf16[512,512]{1,0:T(8,128)(2,1)} collective-permute-done((bf16[512,512]{1,0:T(8,128)(2,1)}, bf16[512,512]{1,0:T(8,128)(2,1)}, u32[]{:S(2)}, u32[]{:S(2)}) %collective-permute-start.17) | collective-permute-done | bytes 524320 | tf_op jit(solution)/shard_map/ppermute | solution.py:115
  172.3 2.8 %fusion.11 = (bf16[512,512]{1,0:T(8,128)(2,1)}, bf16[512,512]{1,0:T(8,128)(2,1)}) fusion(bf16[512,512]{1,0:T(8,128)(2,1)} %collective-permute-done.17, bf16[8,512,512]{2,1,0:T(8,128)(2,1)} %bitcast.81, s32[]{:T(128)S(6)} %select_n.48, s32[]{:T(128)S(6)} %select_n.51, bf16[512,512]{1,0:T(8,128)(2,1)} %collective-permute-done.21), kind=kLoop, calls=%fused_computation.20 | loop fusion | flops 2097152 | bytes 3145736 | tf_op jit(solution)/shard_map/convert_element_type | solution.py:131
  175.1 1.4 reduce_sum.24
  176.6 19.8 %all_to_all.15 = bf16[8,32,1024]{2,1,0:T(8,128)(2,1)S(1)} all-to-all(bf16[8,32,1024]{2,1,0:T(8,128)(2,1)S(1)} %broadcast_in_dim.7), channel_id=1, replica_groups=mesh['z'=8,'yh'=2,'x'=4,'yl'=2,'core'=2] {'z'}, dimensions={0} | all-to-all | bytes 1048576 | tf_op jit(solution)/shard_map/all_to_all | solution.py:273
  196.4 0.1 reduce_sum.25
  196.5 1.1 broadcast_in_dim.8
  197.6 4.4 %all-to-all-start.2 = ((bf16[16,32,1024]{2,1,0:T(8,128)(2,1)}), bf16[16,32,1024]{2,1,0:T(8,128)(2,1)S(1)}, u32[]{:S(2)}, u32[]{:S(2)}) async-start(bf16[16,32,1024]{2,1,0:T(8,128)(2,1)} %broadcast_in_dim.8), calls=%async_computation.2 | async-start | bytes 2097152 | tf_op jit(solution)/shard_map/all_to_all | solution.py:275
  202.0 0.3 collective-permute-start.12
  202.3 2.7 %collective-permute-start.15 = (bf16[512,512]{1,0:T(8,128)(2,1)}, bf16[512,512]{1,0:T(8,128)(2,1)}, u32[]{:S(2)}, u32[]{:S(2)}) collective-permute-start(bf16[512,512]{1,0:T(8,128)(2,1)} %get-tuple-element.25), channel_id=1, source_target_pairs={{0,224},{32,0},{64,32},{96,64},{128,96},{160,128},{192,160},{224,1... | collective-permute-start | bytes 1572872 | tf_op jit(solution)/shard_map/ppermute | solution.py:115
  205.0 2.7 %collective-permute-start.22 = (bf16[512,512]{1,0:T(8,128)(2,1)}, bf16[512,512]{1,0:T(8,128)(2,1)}, u32[]{:S(2)}, u32[]{:S(2)}) collective-permute-start(bf16[512,512]{1,0:T(8,128)(2,1)} %get-tuple-element.29), channel_id=1, source_target_pairs={{0,224},{32,0},{64,32},{96,64},{128,96},{160,128},{192,160},{224,1... | collective-permute-start | bytes 1572872 | tf_op jit(solution)/shard_map/ppermute | solution.py:115
  207.6 5.3 %collective-permute-done.12 = bf16[512,512]{1,0:T(8,128)(2,1)} collective-permute-done((bf16[512,512]{1,0:T(8,128)(2,1)}, bf16[512,512]{1,0:T(8,128)(2,1)}, u32[]{:S(2)}, u32[]{:S(2)}) %collective-permute-start.12) | collective-permute-done | bytes 524320 | tf_op jit(solution)/shard_map/ppermute | solution.py:115
  213.0 2.4 fusion.19
  215.3 0.9 all-to-all-done.2
  216.3 9.1 %collective-permute-start.25 = (bf16[512,1024]{1,0:T(8,128)(2,1)S(1)}, bf16[512,1024]{1,0:T(8,128)(2,1)}, u32[]{:S(2)}, u32[]{:S(2)}) collective-permute-start(bf16[512,1024]{1,0:T(8,128)(2,1)S(1)} %bitcast.95), channel_id=1, source_target_pairs={{0,1},{1,0},{2,3},{3,2},{4,5},{5,4},{6,7},{7,6},{8,9},{9,8},{10,11... | collective-permute-start | bytes 3145736 | tf_op jit(solution)/shard_map/ppermute | solution.py:115
  225.3 1.5 fusion.20
  226.9 0.1 pad_maximum_fusion
  226.9 2.9 %collective-permute-start.23 = (bf16[256,1024]{1,0:T(8,128)(2,1)S(1)}, bf16[256,1024]{1,0:T(8,128)(2,1)S(1)}, u32[]{:S(2)}, u32[]{:S(2)}) collective-permute-start(bf16[256,1024]{1,0:T(8,128)(2,1)S(1)} %pad_maximum_fusion), channel_id=1, source_target_pairs={{0,16},{16,0},{1,17},{17,1},{2,18},{18,2},{3,19},{19,3},{4,20},{20... | collective-permute-start | bytes 1572872 | tf_op jit(solution)/shard_map/ppermute | solution.py:115
  229.9 8.0 %collective-permute-done.23 = bf16[256,1024]{1,0:T(8,128)(2,1)S(1)} collective-permute-done((bf16[256,1024]{1,0:T(8,128)(2,1)S(1)}, bf16[256,1024]{1,0:T(8,128)(2,1)S(1)}, u32[]{:S(2)}, u32[]{:S(2)}) %collective-permute-start.23) | collective-permute-done | bytes 524320 | tf_op jit(solution)/shard_map/ppermute | solution.py:115
  237.9 2.6 %fusion = bf16[1,256,1024]{2,1,0:T(8,128)(2,1)} fusion(bf16[1024,1024]{1,0:T(8,128)(2,1)S(1)} %copy-done, f32[256,512]{1,0:T(8,128)S(1)} %get-tuple-element.23, f32[256,512]{1,0:T(8,128)} %get-tuple-element.21, bf16[256,1024]{1,0:T(8,128)(2,1)S(1)} %collective-permute-done.23), kind=kOutput, calls=%fused_computation.4 | convolution fusion | flops 538181632 | bytes 4194304 | tf_op jit(solution)/shard_map/dot_general | solution.py:312
  240.5 2.7 %shard_map.98.refs_0_ = f32[1024,1024]{1,0:T(8,128)} custom-call(s32[1]{0:T(128)} %bitcast.44.which_ref, bf16[512,1024]{1,0:T(8,128)(2,1)} %bitcast.96), custom_call_target="tpu_custom_call" | custom-call | tf_op jit(solution)/shard_map/pallas_call | solution.py:254
  243.2 2.7 %shard_map.99 = f32[1024,1024]{1,0:T(8,128)} custom-call(s32[1]{0:T(128)} %bitcast.41.which_ref, bf16[512,1024]{1,0:T(8,128)(2,1)} %collective-permute-done.25.half_ref, f32[1024,1024]{1,0:T(8,128)} %shard_map.98.refs_0_), custom_call_target="tpu_custom_call", output_to_operand_aliasing={{}: (2, {})} | custom-call | tf_op jit(solution)/shard_map/pallas_call | solution.py:254
  (37 shorter events, 0.2 us)
Async XLA Ops:
  7.2 230.7 %copy-start = (bf16[1024,1024]{1,0:T(8,128)(2,1)S(1)}, bf16[1024,1024]{1,0:T(8,128)(2,1)}, u32[]{:S(2)}) copy-start(bf16[1024,1024]{1,0:T(8,128)(2,1)} %param.11) | copy-start | bytes 6291460
  7.2 62.2 %all-gather.2.cloned.1.call-start = ((), (), s32[]{:S(2)}) async-start(), calls=%async_computation.3 | async-start | bytes 8912896 | tf_op jit(solution)/shard_map/all_gather | solution.py:287
  11.1 70.1 %copy-start.1 = (bf16[1,256,1024]{1,2,0:T(8,128)(2,1)}, bf16[1,256,1024]{1,2,0:T(8,128)(2,1)S(1)}, u32[]{:S(2)}) copy-start(bf16[1,256,1024]{1,2,0:T(8,128)(2,1)S(1)} %copy.12) | copy-start | bytes 1572868
  11.1 14.4 %collective-permute-start.4 = (bf16[1024,256]{1,0:T(8,128)(2,1)S(1)}, bf16[1024,256]{1,0:T(8,128)(2,1)S(1)}, u32[]{:S(2)}, u32[]{:S(2)}) collective-permute-start(bf16[1024,256]{1,0:T(8,128)(2,1)S(1)} %bitcast.89), channel_id=1, source_target_pairs={{0,16},{16,0},{1,17},{17,1},{2,18},{18,2},{3,19},{19,3},{4,20},{20... | collective-permute-start | bytes 1572872 | tf_op jit(solution)/shard_map/ppermute | solution.py:115
  14.9 17.9 %collective-permute-start = (bf16[1024,256]{1,0:T(8,128)(2,1)S(1)}, bf16[1024,256]{1,0:T(8,128)(2,1)}, u32[]{:S(2)}, u32[]{:S(2)}) collective-permute-start(bf16[1024,256]{1,0:T(8,128)(2,1)S(1)} %bitcast.90), channel_id=1, source_target_pairs={{0,224},{32,0},{64,32},{96,64},{128,96},{160,128},{192,160},{224,1... | collective-permute-start | bytes 1572872 | tf_op jit(solution)/shard_map/ppermute | solution.py:115
  20.5 15.0 %collective-permute-start.2 = (bf16[1024,256]{1,0:T(8,128)(2,1)S(1)}, bf16[1024,256]{1,0:T(8,128)(2,1)}, u32[]{:S(2)}, u32[]{:S(2)}) collective-permute-start(bf16[1024,256]{1,0:T(8,128)(2,1)S(1)} %bitcast.91), channel_id=1, source_target_pairs={{0,32},{32,64},{64,96},{96,128},{128,160},{160,192},{192,224},{224... | collective-permute-start | bytes 1572872 | tf_op jit(solution)/shard_map/ppermute | solution.py:115
  25.5 55.7 %copy-start.5 = (bf16[1024,256]{1,0:T(8,128)(2,1)}, bf16[1024,256]{1,0:T(8,128)(2,1)S(1)}, u32[]{:S(2)}) copy-start(bf16[1024,256]{1,0:T(8,128)(2,1)S(1)} %collective-permute-done.4.refs_13_) | copy-start | bytes 1572868
  25.5 14.6 %collective-permute-start.5 = (bf16[1024,256]{1,0:T(8,128)(2,1)S(1)}, bf16[1024,256]{1,0:T(8,128)(2,1)}, u32[]{:S(2)}, u32[]{:S(2)}) collective-permute-start(bf16[1024,256]{1,0:T(8,128)(2,1)S(1)} %collective-permute-done.4.refs_13_), channel_id=1, source_target_pairs={{0,224},{32,0},{64,32},{96,64},{128,96},{160,128},{192,160},{224,1... | collective-permute-start | bytes 1572872 | tf_op jit(solution)/shard_map/ppermute | solution.py:115
  32.8 10.9 %collective-permute-start.7 = (bf16[1024,256]{1,0:T(8,128)(2,1)S(1)}, bf16[1024,256]{1,0:T(8,128)(2,1)}, u32[]{:S(2)}, u32[]{:S(2)}) collective-permute-start(bf16[1024,256]{1,0:T(8,128)(2,1)S(1)} %collective-permute-done.4.refs_13_), channel_id=1, source_target_pairs={{0,32},{32,64},{64,96},{96,128},{128,160},{160,192},{192,224},{224... | collective-permute-start | bytes 1572872 | tf_op jit(solution)/shard_map/ppermute | solution.py:115
  32.8 18.7 %collective-permute-start.1 = (bf16[1024,256]{1,0:T(8,128)(2,1)}, bf16[1024,256]{1,0:T(8,128)(2,1)}, u32[]{:S(2)}, u32[]{:S(2)}) collective-permute-start(bf16[1024,256]{1,0:T(8,128)(2,1)} %collective-permute-done.refs_9_), channel_id=1, source_target_pairs={{0,224},{32,0},{64,32},{96,64},{128,96},{160,128},{192,160},{224,1... | collective-permute-start | bytes 1572872 | tf_op jit(solution)/shard_map/ppermute | solution.py:115
  35.4 19.2 %collective-permute-start.3 = (bf16[1024,256]{1,0:T(8,128)(2,1)}, bf16[1024,256]{1,0:T(8,128)(2,1)}, u32[]{:S(2)}, u32[]{:S(2)}) collective-permute-start(bf16[1024,256]{1,0:T(8,128)(2,1)} %collective-permute-done.2.refs_7_), channel_id=1, source_target_pairs={{0,32},{32,64},{64,96},{96,128},{128,160},{160,192},{192,224},{224... | collective-permute-start | bytes 1572872 | tf_op jit(solution)/shard_map/ppermute | solution.py:115
  40.1 22.6 %collective-permute-start.6 = (bf16[1024,256]{1,0:T(8,128)(2,1)}, bf16[1024,256]{1,0:T(8,128)(2,1)}, u32[]{:S(2)}, u32[]{:S(2)}) collective-permute-start(bf16[1024,256]{1,0:T(8,128)(2,1)} %collective-permute-done.5.refs_14_), channel_id=1, source_target_pairs={{0,224},{32,0},{64,32},{96,64},{128,96},{160,128},{192,160},{224,1... | collective-permute-start | bytes 1572872 | tf_op jit(solution)/shard_map/ppermute | solution.py:115
  43.6 22.2 %collective-permute-start.8 = (bf16[1024,256]{1,0:T(8,128)(2,1)}, bf16[1024,256]{1,0:T(8,128)(2,1)}, u32[]{:S(2)}, u32[]{:S(2)}) collective-permute-start(bf16[1024,256]{1,0:T(8,128)(2,1)} %collective-permute-done.7.refs_12_), channel_id=1, source_target_pairs={{0,32},{32,64},{64,96},{96,128},{128,160},{160,192},{192,224},{224... | collective-permute-start | bytes 1572872 | tf_op jit(solution)/shard_map/ppermute | solution.py:115
  81.2 13.8 %collective-permute-start.9 = (bf16[512,512]{1,0:T(8,128)(2,1)}, bf16[512,512]{1,0:T(8,128)(2,1)S(1)}, u32[]{:S(2)}, u32[]{:S(2)}) collective-permute-start(bf16[512,512]{1,0:T(8,128)(2,1)} %bitcast.103), channel_id=1, source_target_pairs={{0,32},{32,64},{64,96},{96,128},{128,160},{160,192},{192,224},{224... | collective-permute-start | bytes 1572872 | tf_op jit(solution)/shard_map/ppermute | solution.py:115
  82.5 18.9 %collective-permute-start.19 = (bf16[512,512]{1,0:T(8,128)(2,1)}, bf16[512,512]{1,0:T(8,128)(2,1)S(1)}, u32[]{:S(2)}, u32[]{:S(2)}) collective-permute-start(bf16[512,512]{1,0:T(8,128)(2,1)} %bitcast.102), channel_id=1, source_target_pairs={{0,224},{32,0},{64,32},{96,64},{128,96},{160,128},{192,160},{224,1... | collective-permute-start | bytes 1572872 | tf_op jit(solution)/shard_map/ppermute | solution.py:115
  86.5 25.6 %collective-permute-start.13 = (bf16[512,512]{1,0:T(8,128)(2,1)}, bf16[512,512]{1,0:T(8,128)(2,1)}, u32[]{:S(2)}, u32[]{:S(2)}) collective-permute-start(bf16[512,512]{1,0:T(8,128)(2,1)} %bitcast.101), channel_id=1, source_target_pairs={{0,224},{32,0},{64,32},{96,64},{128,96},{160,128},{192,160},{224,1... | collective-permute-start | bytes 1572872 | tf_op jit(solution)/shard_map/ppermute | solution.py:115
  95.0 0.8 copy-start.7
  97.1 15.9 %collective-permute-start.10 = (bf16[512,512]{1,0:T(8,128)(2,1)S(1)}, bf16[512,512]{1,0:T(8,128)(2,1)}, u32[]{:S(2)}, u32[]{:S(2)}) collective-permute-start(bf16[512,512]{1,0:T(8,128)(2,1)S(1)} %fusion.17), channel_id=1, source_target_pairs={{0,32},{32,64},{64,96},{96,128},{128,160},{160,192},{192,224},{224... | collective-permute-start | bytes 1572872 | tf_op jit(solution)/shard_map/ppermute | solution.py:115
  99.3 25.0 %collective-permute-start.16 = (bf16[512,512]{1,0:T(8,128)(2,1)}, bf16[512,512]{1,0:T(8,128)(2,1)}, u32[]{:S(2)}, u32[]{:S(2)}) collective-permute-start(bf16[512,512]{1,0:T(8,128)(2,1)} %bitcast.100), channel_id=1, source_target_pairs={{0,32},{32,64},{64,96},{96,128},{128,160},{160,192},{192,224},{224... | collective-permute-start | bytes 1572872 | tf_op jit(solution)/shard_map/ppermute | solution.py:115
  101.4 0.8 copy-start.6
  103.6 20.7 %collective-permute-start.20 = (bf16[512,512]{1,0:T(8,128)(2,1)S(1)}, bf16[512,512]{1,0:T(8,128)(2,1)}, u32[]{:S(2)}, u32[]{:S(2)}) collective-permute-start(bf16[512,512]{1,0:T(8,128)(2,1)S(1)} %fusion.10), channel_id=1, source_target_pairs={{0,224},{32,0},{64,32},{96,64},{128,96},{160,128},{192,160},{224,1... | collective-permute-start | bytes 1572872 | tf_op jit(solution)/shard_map/ppermute | solution.py:115
  127.1 10.2 %copy-start.2 = (bf16[512,512]{1,0:T(8,128)(2,1)S(1)}, bf16[512,512]{1,0:T(8,128)(2,1)}, u32[]{:S(2)}) copy-start(bf16[512,512]{1,0:T(8,128)(2,1)} %get-tuple-element.27.refs_2_) | copy-start | bytes 1572868
  133.8 14.6 %collective-permute-start.24 = (bf16[512,1024]{1,0:T(8,128)(2,1)}, bf16[512,1024]{1,0:T(8,128)(2,1)S(1)}, u32[]{:S(2)}, u32[]{:S(2)}) collective-permute-start(bf16[512,1024]{1,0:T(8,128)(2,1)} %shard_map.96), channel_id=1, source_target_pairs={{0,1},{1,0},{2,3},{3,2},{4,5},{5,4},{6,7},{7,6},{8,9},{9,8},{10,11... | collective-permute-start | bytes 3145736 | tf_op jit(solution)/shard_map/ppermute | solution.py:115
  137.3 23.6 %collective-permute-start.11 = (bf16[512,512]{1,0:T(8,128)(2,1)}, bf16[512,512]{1,0:T(8,128)(2,1)}, u32[]{:S(2)}, u32[]{:S(2)}) collective-permute-start(bf16[512,512]{1,0:T(8,128)(2,1)} %get-tuple-element.26.refs_3_), channel_id=1, source_target_pairs={{0,32},{32,64},{64,96},{96,128},{128,160},{160,192},{192,224},{224... | collective-permute-start | bytes 1572872 | tf_op jit(solution)/shard_map/ppermute | solution.py:115
  137.3 23.6 %collective-permute-start.14 = (bf16[512,512]{1,0:T(8,128)(2,1)S(1)}, bf16[512,512]{1,0:T(8,128)(2,1)}, u32[]{:S(2)}, u32[]{:S(2)}) collective-permute-start(bf16[512,512]{1,0:T(8,128)(2,1)S(1)} %copy-done.2), channel_id=1, source_target_pairs={{0,224},{32,0},{64,32},{96,64},{128,96},{160,128},{192,160},{224,1... | collective-permute-start | bytes 1572872 | tf_op jit(solution)/shard_map/ppermute | solution.py:115
  148.4 9.8 %copy-start.3 = (bf16[512,512]{1,0:T(8,128)(2,1)S(1)}, bf16[512,512]{1,0:T(8,128)(2,1)}, u32[]{:S(2)}) copy-start(bf16[512,512]{1,0:T(8,128)(2,1)} %get-tuple-element.31.refs_4_) | copy-start | bytes 1572868
  151.1 24.0 %all-to-all-start = ((bf16[16,32,1024]{2,1,0:T(8,128)(2,1)}), bf16[16,32,1024]{2,1,0:T(8,128)(2,1)}, u32[]{:S(2)}, u32[]{:S(2)}) async-start(bf16[16,32,1024]{2,1,0:T(8,128)(2,1)} %bitcast.94), calls=%async_computation | async-start | bytes 2097152 | tf_op jit(solution)/shard_map/all_to_all | solution.py:270
  158.1 14.2 %collective-permute-start.17 = (bf16[512,512]{1,0:T(8,128)(2,1)}, bf16[512,512]{1,0:T(8,128)(2,1)}, u32[]{:S(2)}, u32[]{:S(2)}) collective-permute-start(bf16[512,512]{1,0:T(8,128)(2,1)} %get-tuple-element.30.refs_5_), channel_id=1, source_target_pairs={{0,32},{32,64},{64,96},{96,128},{128,160},{160,192},{192,224},{224... | collective-permute-start | bytes 1572872 | tf_op jit(solution)/shard_map/ppermute | solution.py:115
  158.2 14.1 %collective-permute-start.21 = (bf16[512,512]{1,0:T(8,128)(2,1)S(1)}, bf16[512,512]{1,0:T(8,128)(2,1)}, u32[]{:S(2)}, u32[]{:S(2)}) collective-permute-start(bf16[512,512]{1,0:T(8,128)(2,1)S(1)} %copy-done.3), channel_id=1, source_target_pairs={{0,224},{32,0},{64,32},{96,64},{128,96},{160,128},{192,160},{224,1... | collective-permute-start | bytes 1572872 | tf_op jit(solution)/shard_map/ppermute | solution.py:115
  197.6 18.6 %all-to-all-start.2 = ((bf16[16,32,1024]{2,1,0:T(8,128)(2,1)}), bf16[16,32,1024]{2,1,0:T(8,128)(2,1)S(1)}, u32[]{:S(2)}, u32[]{:S(2)}) async-start(bf16[16,32,1024]{2,1,0:T(8,128)(2,1)} %broadcast_in_dim.8), calls=%async_computation.2 | async-start | bytes 2097152 | tf_op jit(solution)/shard_map/all_to_all | solution.py:275
  202.0 11.0 %collective-permute-start.12 = (bf16[512,512]{1,0:T(8,128)(2,1)}, bf16[512,512]{1,0:T(8,128)(2,1)}, u32[]{:S(2)}, u32[]{:S(2)}) collective-permute-start(bf16[512,512]{1,0:T(8,128)(2,1)} %get-tuple-element.24), channel_id=1, source_target_pairs={{0,32},{32,64},{64,96},{96,128},{128,160},{160,192},{192,224},{224... | collective-permute-start | bytes 1572872 | tf_op jit(solution)/shard_map/ppermute | solution.py:115
  202.3 10.6 %collective-permute-start.15 = (bf16[512,512]{1,0:T(8,128)(2,1)}, bf16[512,512]{1,0:T(8,128)(2,1)}, u32[]{:S(2)}, u32[]{:S(2)}) collective-permute-start(bf16[512,512]{1,0:T(8,128)(2,1)} %get-tuple-element.25), channel_id=1, source_target_pairs={{0,224},{32,0},{64,32},{96,64},{128,96},{160,128},{192,160},{224,1... | collective-permute-start | bytes 1572872 | tf_op jit(solution)/shard_map/ppermute | solution.py:115
  205.0 20.4 %collective-permute-start.18 = (bf16[512,512]{1,0:T(8,128)(2,1)}, bf16[512,512]{1,0:T(8,128)(2,1)}, u32[]{:S(2)}, u32[]{:S(2)}) collective-permute-start(bf16[512,512]{1,0:T(8,128)(2,1)} %get-tuple-element.28), channel_id=1, source_target_pairs={{0,32},{32,64},{64,96},{96,128},{128,160},{160,192},{192,224},{224... | collective-permute-start | bytes 1572872 | tf_op jit(solution)/shard_map/ppermute | solution.py:115
  205.0 20.4 %collective-permute-start.22 = (bf16[512,512]{1,0:T(8,128)(2,1)}, bf16[512,512]{1,0:T(8,128)(2,1)}, u32[]{:S(2)}, u32[]{:S(2)}) collective-permute-start(bf16[512,512]{1,0:T(8,128)(2,1)} %get-tuple-element.29), channel_id=1, source_target_pairs={{0,224},{32,0},{64,32},{96,64},{128,96},{160,128},{192,160},{224,1... | collective-permute-start | bytes 1572872 | tf_op jit(solution)/shard_map/ppermute | solution.py:115
  216.3 24.3 %copy-start.4 = (bf16[16,32,1024]{2,1,0:T(8,128)(2,1)}, bf16[16,32,1024]{2,1,0:T(8,128)(2,1)S(1)}, u32[]{:S(2)}) copy-start(bf16[16,32,1024]{2,1,0:T(8,128)(2,1)S(1)} %all-to-all-done.2) | copy-start | bytes 3145732
  216.3 27.0 %collective-permute-start.25 = (bf16[512,1024]{1,0:T(8,128)(2,1)S(1)}, bf16[512,1024]{1,0:T(8,128)(2,1)}, u32[]{:S(2)}, u32[]{:S(2)}) collective-permute-start(bf16[512,1024]{1,0:T(8,128)(2,1)S(1)} %bitcast.95), channel_id=1, source_target_pairs={{0,1},{1,0},{2,3},{3,2},{4,5},{5,4},{6,7},{7,6},{8,9},{9,8},{10,11... | collective-permute-start | bytes 3145736 | tf_op jit(solution)/shard_map/ppermute | solution.py:115
  226.9 10.9 %collective-permute-start.23 = (bf16[256,1024]{1,0:T(8,128)(2,1)S(1)}, bf16[256,1024]{1,0:T(8,128)(2,1)S(1)}, u32[]{:S(2)}, u32[]{:S(2)}) collective-permute-start(bf16[256,1024]{1,0:T(8,128)(2,1)S(1)} %pad_maximum_fusion), channel_id=1, source_target_pairs={{0,16},{16,0},{1,17},{17,1},{2,18},{18,2},{3,19},{19,3},{4,20},{20... | collective-permute-start | bytes 1572872 | tf_op jit(solution)/shard_map/ppermute | solution.py:115
Sparse Core Ops, SparseCore 0:
  10.4 58.8 all-gather.1

commit v2 on v1

--- a/solution.py
+++ b/solution.py
@@ -261,7 +261,7 @@
     )(which.reshape(1), half, *whole)
 
 
-def sum_everywhere(mine, other, second):
+def sum_everywhere(mine, other, second, third):
     side = lax.axis_size(SIDE)
     depth = lax.axis_size("z")
     core = lax.axis_index("core")
@@ -272,6 +272,7 @@
     part = behind(part, second)
     part = lax.all_to_all(jnp.broadcast_to(part[None], (depth,) + part.shape), "z", 0, 0, tiled=True)
     part = jnp.sum(part.astype(jnp.float32), axis=0).astype(jnp.bfloat16)
+    part = behind(part, third)
     half = lax.all_to_all(jnp.broadcast_to(part[None], (side,) + part.shape), SIDE, 0, 0, tiled=True)
     half = half.reshape(-1, half.shape[-1])
     return place_half(shift(half, "core", 1), 1 - core, place_half(half, core))
@@ -307,7 +308,7 @@
     theirs, ours = [jnp.stack([z, lax.axis_index("yh"), half]) for half in (1 - core, core)]
     theirs = weight_terms(near, partials, passing, REACH, theirs)
     ours = weight_terms(near, partials, passing, REACH, behind(ours, theirs))
-    grad_weight = sum_everywhere(ours, theirs, sent[3])
+    grad_weight = sum_everywhere(ours, theirs, sent[3], arrived)
     mixed = row_sum(partials, arrived)
     grad_in = lax.dot_general(
         mixed, weight, (((1,), (1,)), ((), ())), preferred_element_type=jnp.float32

time: 257 us -> 276 us (1.074); the launches traced: 253 us -> 276 us
  waiting for transfers between devices: 79.9 us -> 122 us
  blocking collectives: 19.8 us -> 0 us
    all_to_all x1 -> x0, blocking collectives: 19.8 us -> none  [sum_everywhere(): lax.all_to_all(jnp.broadcast_to(part[None], (depth,) + part.shape), 'z',...]
    ppermute x26, waiting for transfers between devices: 75.4 us -> 94.9 us  [shift(): lax.ppermute(value, axis, [(i, (i + way) % size) for i in range(size)])]
    all_to_all x1, waiting for transfers between devices: 0.94 us -> 13.5 us  [sum_everywhere(): lax.all_to_all(jnp.broadcast_to(part[None], (side,) + part.shape), SIDE,...]
    all_to_all x0 -> x1, waiting for transfers between devices: none -> 10.2 us  [sum_everywhere(): lax.all_to_all(jnp.broadcast_to(part[None], (depth,) + part.shape), 'z',...]
    ppermute x26, starting transfers between devices: 63.2 us -> 56.7 us  [shift(): lax.ppermute(value, axis, [(i, (i + way) % size) for i in range(size)])]
    all_to_all x0 -> x1, starting transfers between devices: none -> 4.98 us  [sum_everywhere(): lax.all_to_all(jnp.broadcast_to(part[None], (depth,) + part.shape), 'z',...]
  transfers between devices with their start and end apart: 29 -> 30, of which waited for: 15 -> 16; matrix products, arithmetic and copies ran while one was open for 9% -> 9% of each run, Pallas kernels for 4% -> 3%
where the time goes in v2:
time: 276 us
  waiting for transfers between devices  122 us (44%)
  starting transfers between devices  76.2 us (28%)
  Pallas kernels  28.6 us (10%)
  other arithmetic  26.5 us (10%)
  between operations  14.9 us (5%)
  local copies, waits for them, and re-layouts  4.89 us (2%)
    ppermute x26, waiting for transfers between devices, shift(): lax.ppermute(value, axis, [(i, (i + way) % size) for i in range(size)])  94.9 us
    ppermute x26, starting transfers between devices, shift(): lax.ppermute(value, axis, [(i, (i + way) % size) for i in range(size)])  56.7 us
    convert_element_type x6, other arithmetic, row_chains(): (moving.astype(jnp.float32) + own.astype(jnp.float32)).astype(jnp.bfloat16)  13.8 us
    all_to_all x1, waiting for transfers between devices, sum_everywhere(): lax.all_to_all(jnp.broadcast_to(part[None], (side,) + part.shape), SIDE,...  13.5 us
    pallas_call x2, Pallas kernels, weight_terms(): pl.pallas_call(functools.partial(term_kernel, chunks, reach), out_shape=j...  13.4 us
    all_to_all x1, waiting for transfers between devices, sum_everywhere(): lax.all_to_all(jnp.broadcast_to(part[None], (depth,) + part.shape), 'z',...  10.2 us
    pallas_call x1, Pallas kernels, tile_sum(): pl.pallas_call(functools.partial(tile_kernel, columns), out_shape=[jax.Sh...  9.85 us
    all_to_all x1, starting transfers between devices, sum_everywhere(): part = lax.all_to_all(part, SIDE, 0, 0, tiled=True)  8.4 us
  transfers between devices with their start and end apart: 30, of which 16 were waited for; matrix products, arithmetic and copies ran while one was open for 9% of the time, Pallas kernels for 3%

profile of v2, /device:TPU:1, one launch (start us, length us, event | category | flops | bytes accessed | tf_op | source)
XLA Modules:
  0.0 275.8 jit_solution(1618153921366877319)
XLA Ops:
  7.2 2.6 fusion.6
  9.8 1.2 copy.12
  11.1 3.8 %collective-permute-start.4 = (bf16[1024,256]{1,0:T(8,128)(2,1)S(1)}, bf16[1024,256]{1,0:T(8,128)(2,1)S(1)}, u32[]{:S(2)}, u32[]{:S(2)}) collective-permute-start(bf16[1024,256]{1,0:T(8,128)(2,1)S(1)} %bitcast.89), channel_id=1, source_target_pairs={{0,16},{16,0},{1,17},{17,1},{2,18},{18,2},{3,19},{19,3},{4,20},{20... | collective-permute-start | bytes 1572872 | tf_op jit(solution)/shard_map/ppermute | solution.py:115
  14.9 5.6 %collective-permute-start = (bf16[1024,256]{1,0:T(8,128)(2,1)S(1)}, bf16[1024,256]{1,0:T(8,128)(2,1)}, u32[]{:S(2)}, u32[]{:S(2)}) collective-permute-start(bf16[1024,256]{1,0:T(8,128)(2,1)S(1)} %bitcast.90), channel_id=1, source_target_pairs={{0,224},{32,0},{64,32},{96,64},{128,96},{160,128},{192,160},{224,1... | collective-permute-start | bytes 1572872 | tf_op jit(solution)/shard_map/ppermute | solution.py:115
  20.5 5.0 %collective-permute-done.4.refs_13_ = bf16[1024,256]{1,0:T(8,128)(2,1)S(1)} collective-permute-done((bf16[1024,256]{1,0:T(8,128)(2,1)S(1)}, bf16[1024,256]{1,0:T(8,128)(2,1)S(1)}, u32[]{:S(2)}, u32[]{:S(2)}) %collective-permute-start.4) | collective-permute-done | bytes 524320 | tf_op jit(solution)/shard_map/ppermute | solution.py:115
  25.5 7.3 %collective-permute-start.5 = (bf16[1024,256]{1,0:T(8,128)(2,1)S(1)}, bf16[1024,256]{1,0:T(8,128)(2,1)}, u32[]{:S(2)}, u32[]{:S(2)}) collective-permute-start(bf16[1024,256]{1,0:T(8,128)(2,1)S(1)} %collective-permute-done.4.refs_13_), channel_id=1, source_target_pairs={{0,224},{32,0},{64,32},{96,64},{128,96},{160,128},{192,160},{224,1... | collective-permute-start | bytes 1572872 | tf_op jit(solution)/shard_map/ppermute | solution.py:115
  32.8 2.7 collective-permute-start.1
  35.4 4.7 %collective-permute-done.5.refs_14_ = bf16[1024,256]{1,0:T(8,128)(2,1)} collective-permute-done((bf16[1024,256]{1,0:T(8,128)(2,1)S(1)}, bf16[1024,256]{1,0:T(8,128)(2,1)}, u32[]{:S(2)}, u32[]{:S(2)}) %collective-permute-start.5) | collective-permute-done | bytes 524320 | tf_op jit(solution)/shard_map/ppermute | solution.py:115
  40.1 3.5 %collective-permute-start.6 = (bf16[1024,256]{1,0:T(8,128)(2,1)}, bf16[1024,256]{1,0:T(8,128)(2,1)}, u32[]{:S(2)}, u32[]{:S(2)}) collective-permute-start(bf16[1024,256]{1,0:T(8,128)(2,1)} %collective-permute-done.5.refs_14_), channel_id=1, source_target_pairs={{0,224},{32,0},{64,32},{96,64},{128,96},{160,128},{192,160},{224,1... | collective-permute-start | bytes 1572872 | tf_op jit(solution)/shard_map/ppermute | solution.py:115
  44.3 0.7 pad_add_fusion.send_ref
  45.0 6.5 %collective-permute-done.1.refs_10_ = bf16[1024,256]{1,0:T(8,128)(2,1)} collective-permute-done((bf16[1024,256]{1,0:T(8,128)(2,1)}, bf16[1024,256]{1,0:T(8,128)(2,1)}, u32[]{:S(2)}, u32[]{:S(2)}) %collective-permute-start.1) | collective-permute-done | bytes 524320 | tf_op jit(solution)/shard_map/ppermute | solution.py:115
  51.5 3.1 %collective-permute-done.3.refs_6_ = bf16[1024,256]{1,0:T(8,128)(2,1)} collective-permute-done((bf16[1024,256]{1,0:T(8,128)(2,1)}, bf16[1024,256]{1,0:T(8,128)(2,1)}, u32[]{:S(2)}, u32[]{:S(2)}) %collective-permute-start.3) | collective-permute-done | bytes 524320 | tf_op jit(solution)/shard_map/ppermute | solution.py:115
  54.6 8.1 %collective-permute-done.6.refs_15_ = bf16[1024,256]{1,0:T(8,128)(2,1)} collective-permute-done((bf16[1024,256]{1,0:T(8,128)(2,1)}, bf16[1024,256]{1,0:T(8,128)(2,1)}, u32[]{:S(2)}, u32[]{:S(2)}) %collective-permute-start.6) | collective-permute-done | bytes 524320 | tf_op jit(solution)/shard_map/ppermute | solution.py:115
  62.7 3.1 %collective-permute-done.8.refs_11_ = bf16[1024,256]{1,0:T(8,128)(2,1)} collective-permute-done((bf16[1024,256]{1,0:T(8,128)(2,1)}, bf16[1024,256]{1,0:T(8,128)(2,1)}, u32[]{:S(2)}, u32[]{:S(2)}) %collective-permute-start.8) | collective-permute-done | bytes 524320 | tf_op jit(solution)/shard_map/ppermute | solution.py:115
  65.8 3.5 %all-gather.2.cloned.1.call-done.panel_hbm = bf16[4096,1024]{1,0:T(8,128)(2,1)} async-done(((bf16[256,1024]{1,0:T(8,128)(2,1)}), bf16[4096,1024]{1,0:T(8,128)(2,1)}) %all-gather.2.cloned.1.call-update) | async-done | bytes 8388624 | tf_op jit(solution)/shard_map/all_gather | solution.py:288
  69.3 9.9 %shard_map.95 = (bf16[32,128,512]{2,1,0:T(8,128)(2,1)}, bf16[4,128,512]{2,1,0:T(8,128)(2,1)}, bf16[4,128,512]{2,1,0:T(8,128)(2,1)}, bf16[32,128,512]{2,1,0:T(8,1...) custom-call(s32[1]{0:T(128)} %bitcast.76.count_ref, s32[4]{0:T(128)} %pad_add_fusion.send_ref, ...), custom_call_target="tpu_custom_call" | custom-call | flops 2684354560 | bytes 19398656 | tf_op jit(solution)/shard_map/pallas_call | solution.py:87
  79.2 1.3 collective-permute-start.9
  80.6 4.0 %collective-permute-start.19 = (bf16[512,512]{1,0:T(8,128)(2,1)}, bf16[512,512]{1,0:T(8,128)(2,1)S(1)}, u32[]{:S(2)}, u32[]{:S(2)}) collective-permute-start(bf16[512,512]{1,0:T(8,128)(2,1)} %bitcast.103), channel_id=1, source_target_pairs={{0,224},{32,0},{64,32},{96,64},{128,96},{160,128},{192,160},{224,1... | collective-permute-start | bytes 1572872 | tf_op jit(solution)/shard_map/ppermute | solution.py:115
  84.6 7.3 %collective-permute-start.13 = (bf16[512,512]{1,0:T(8,128)(2,1)}, bf16[512,512]{1,0:T(8,128)(2,1)}, u32[]{:S(2)}, u32[]{:S(2)}) collective-permute-start(bf16[512,512]{1,0:T(8,128)(2,1)} %bitcast.102), channel_id=1, source_target_pairs={{0,224},{32,0},{64,32},{96,64},{128,96},{160,128},{192,160},{224,1... | collective-permute-start | bytes 1572872 | tf_op jit(solution)/shard_map/ppermute | solution.py:115
  91.9 3.8 %collective-permute-done.9 = bf16[512,512]{1,0:T(8,128)(2,1)S(1)} collective-permute-done((bf16[512,512]{1,0:T(8,128)(2,1)}, bf16[512,512]{1,0:T(8,128)(2,1)S(1)}, u32[]{:S(2)}, u32[]{:S(2)}) %collective-permute-start.9) | collective-permute-done | bytes 524320 | tf_op jit(solution)/shard_map/ppermute | solution.py:115
  95.7 0.8 copy-done.7
  96.5 1.3 fusion.17
  97.8 0.3 collective-permute-start.10
  98.2 0.8 copy-done.6
  99.0 1.3 fusion.10
  100.3 5.9 %collective-permute-start.20 = (bf16[512,512]{1,0:T(8,128)(2,1)S(1)}, bf16[512,512]{1,0:T(8,128)(2,1)}, u32[]{:S(2)}, u32[]{:S(2)}) collective-permute-start(bf16[512,512]{1,0:T(8,128)(2,1)S(1)} %fusion.10), channel_id=1, source_target_pairs={{0,224},{32,0},{64,32},{96,64},{128,96},{160,128},{192,160},{224,1... | collective-permute-start | bytes 1572872 | tf_op jit(solution)/shard_map/ppermute | solution.py:115
  106.2 0.6 pad_add_fusion.3.place_ref
  106.8 8.2 %collective-permute-done.10 = bf16[512,512]{1,0:T(8,128)(2,1)} collective-permute-done((bf16[512,512]{1,0:T(8,128)(2,1)S(1)}, bf16[512,512]{1,0:T(8,128)(2,1)}, u32[]{:S(2)}, u32[]{:S(2)}) %collective-permute-start.10) | collective-permute-done | bytes 524320 | tf_op jit(solution)/shard_map/ppermute | solution.py:115
  115.0 2.8 %fusion.16 = (bf16[512,512]{1,0:T(8,128)(2,1)}, bf16[512,512]{1,0:T(8,128)(2,1)}) fusion(bf16[512,512]{1,0:T(8,128)(2,1)} %collective-permute-done.10, bf16[8,512,512]{2,1,0:T(8,128)(2,1)} %bitcast.84, s32[]{:T(128)S(6)} %select_n.47, s32[]{:T(128)S(6)} %select_n.50, bf16[512,512]{1,0:T(8,128)(2,1)} %collective-permute-done.13), kind=kLoop, calls=%fused_computation.30 | loop fusion | flops 2097152 | bytes 3145736 | tf_op jit(solution)/shard_map/convert_element_type | solution.py:131
  117.8 8.4 %collective-permute-done.16 = bf16[512,512]{1,0:T(8,128)(2,1)} collective-permute-done((bf16[512,512]{1,0:T(8,128)(2,1)}, bf16[512,512]{1,0:T(8,128)(2,1)}, u32[]{:S(2)}, u32[]{:S(2)}) %collective-permute-start.16) | collective-permute-done | bytes 524320 | tf_op jit(solution)/shard_map/ppermute | solution.py:115
  126.3 2.8 %fusion.12 = (bf16[512,512]{1,0:T(8,128)(2,1)}, bf16[512,512]{1,0:T(8,128)(2,1)}) fusion(bf16[512,512]{1,0:T(8,128)(2,1)} %collective-permute-done.16, bf16[8,512,512]{2,1,0:T(8,128)(2,1)} %bitcast.78, s32[]{:T(128)S(6)} %select_n.47, s32[]{:T(128)S(6)} %select_n.50, bf16[512,512]{1,0:T(8,128)(2,1)} %collective-permute-done.20), kind=kLoop, calls=%fused_computation.22 | loop fusion | flops 2097152 | bytes 3145736 | tf_op jit(solution)/shard_map/convert_element_type | solution.py:131
  129.1 6.8 %shard_map.96 = bf16[512,1024]{1,0:T(8,128)(2,1)} custom-call(s32[3]{0:T(128)} %pad_add_fusion.3.place_ref, bf16[8,512,512]{2,1,0:T(8,128)(2,1)} %bitcast.85, bf16[8,512,512]{2,1,0:T(8,128)(2,1)} %bitcast.79, bf16[512,512]{1,0:T(8,128)(2,1)} %get-tuple-element.29.refs_2_, bf16[512,512]{1,0:T(8,128)(2,1)} %get-tuple-element.28.refs_3_, ...), custom_call_target="tpu_custom_call" | custom-call | flops 2684354560 | bytes 8912896 | tf_op jit(solution)/shard_map/pallas_call | solution.py:221
  135.8 0.8 collective-permute-start.24
  136.6 0.6 pad_add_fusion.1.place_ref
  137.3 2.7 collective-permute-start.14
  140.0 6.6 %shard_map.97 = bf16[512,1024]{1,0:T(8,128)(2,1)} custom-call(s32[3]{0:T(128)} %pad_add_fusion.1.place_ref, bf16[8,512,512]{2,1,0:T(8,128)(2,1)} %bitcast.86, bf16[8,512,512]{2,1,0:T(8,128)(2,1)} %bitcast.80, bf16[512,512]{1,0:T(8,128)(2,1)} %get-tuple-element.29.refs_2_, bf16[512,512]{1,0:T(8,128)(2,1)} %get-tuple-element.28.refs_3_, ...), custom_call_target="tpu_custom_call" | custom-call | flops 2684354560 | bytes 8912896 | tf_op jit(solution)/shard_map/pallas_call | solution.py:221
  146.6 2.7 add_convert_fusion
  149.3 8.4 %all-to-all-start = ((bf16[16,32,1024]{2,1,0:T(8,128)(2,1)}), bf16[16,32,1024]{2,1,0:T(8,128)(2,1)}, u32[]{:S(2)}, u32[]{:S(2)}) async-start(bf16[16,32,1024]{2,1,0:T(8,128)(2,1)} %bitcast.94), calls=%async_computation | async-start | bytes 2097152 | tf_op jit(solution)/shard_map/all_to_all | solution.py:270
  157.7 0.1 collective-permute-start.17
  157.8 2.7 collective-permute-start.21
  160.4 2.8 %fusion.15 = (bf16[512,512]{1,0:T(8,128)(2,1)}, bf16[512,512]{1,0:T(8,128)(2,1)}) fusion(bf16[512,512]{1,0:T(8,128)(2,1)} %collective-permute-done.11, bf16[8,512,512]{2,1,0:T(8,128)(2,1)} %bitcast.87, s32[]{:T(128)S(6)} %select_n.48, s32[]{:T(128)S(6)} %select_n.51, bf16[512,512]{1,0:T(8,128)(2,1)} %collective-permute-done.14), kind=kLoop, calls=%fused_computation.28 | loop fusion | flops 2097152 | bytes 3145736 | tf_op jit(solution)/shard_map/convert_element_type | solution.py:131
  163.3 8.6 %collective-permute-done.17 = bf16[512,512]{1,0:T(8,128)(2,1)} collective-permute-done((bf16[512,512]{1,0:T(8,128)(2,1)}, bf16[512,512]{1,0:T(8,128)(2,1)}, u32[]{:S(2)}, u32[]{:S(2)}) %collective-permute-start.17) | collective-permute-done | bytes 524320 | tf_op jit(solution)/shard_map/ppermute | solution.py:115
  171.9 2.8 %fusion.11 = (bf16[512,512]{1,0:T(8,128)(2,1)}, bf16[512,512]{1,0:T(8,128)(2,1)}) fusion(bf16[512,512]{1,0:T(8,128)(2,1)} %collective-permute-done.17, bf16[8,512,512]{2,1,0:T(8,128)(2,1)} %bitcast.81, s32[]{:T(128)S(6)} %select_n.48, s32[]{:T(128)S(6)} %select_n.51, bf16[512,512]{1,0:T(8,128)(2,1)} %collective-permute-done.21), kind=kLoop, calls=%fused_computation.20 | loop fusion | flops 2097152 | bytes 3145736 | tf_op jit(solution)/shard_map/convert_element_type | solution.py:131
  174.6 1.4 reduce_sum.24
  176.0 0.9 broadcast_in_dim.7
  176.9 5.0 %all-to-all-start.1 = ((bf16[8,32,1024]{2,1,0:T(8,128)(2,1)}), bf16[8,32,1024]{2,1,0:T(8,128)(2,1)S(1)}, u32[]{:S(2)}, u32[]{:S(2)}) async-start(bf16[8,32,1024]{2,1,0:T(8,128)(2,1)} %broadcast_in_dim.7), calls=%async_computation.1 | async-start | bytes 1048576 | tf_op jit(solution)/shard_map/all_to_all | solution.py:273
  181.9 1.5 collective-permute-start.12
  183.3 1.2 collective-permute-start.15
  184.6 0.2 collective-permute-start.18
  184.8 2.5 collective-permute-start.22
  187.3 10.2 %all-to-all-done.1 = bf16[8,32,1024]{2,1,0:T(8,128)(2,1)S(1)} async-done(((bf16[8,32,1024]{2,1,0:T(8,128)(2,1)}), bf16[8,32,1024]{2,1,0:T(8,128)(2,1)S(1)}, u32[]{:S(2)}, u32[]{:S(2)}) %all-to-all-start.1) | async-done | bytes 524320 | tf_op jit(solution)/shard_map/all_to_all | solution.py:273
  197.6 9.9 %collective-permute-done.12 = bf16[512,512]{1,0:T(8,128)(2,1)} collective-permute-done((bf16[512,512]{1,0:T(8,128)(2,1)}, bf16[512,512]{1,0:T(8,128)(2,1)}, u32[]{:S(2)}, u32[]{:S(2)}) %collective-permute-start.12) | collective-permute-done | bytes 524320 | tf_op jit(solution)/shard_map/ppermute | solution.py:115
  207.5 11.1 %collective-permute-done.18 = bf16[512,512]{1,0:T(8,128)(2,1)S(1)} collective-permute-done((bf16[512,512]{1,0:T(8,128)(2,1)}, bf16[512,512]{1,0:T(8,128)(2,1)S(1)}, u32[]{:S(2)}, u32[]{:S(2)}) %collective-permute-start.18) | collective-permute-done | bytes 524320 | tf_op jit(solution)/shard_map/ppermute | solution.py:115
  218.7 1.2 broadcast_in_dim.8
  219.8 6.1 %all-to-all-start.2 = ((bf16[16,32,1024]{2,1,0:T(8,128)(2,1)}), bf16[16,32,1024]{2,1,0:T(8,128)(2,1)S(1)}, u32[]{:S(2)}, u32[]{:S(2)}) async-start(bf16[16,32,1024]{2,1,0:T(8,128)(2,1)} %broadcast_in_dim.8), calls=%async_computation.2 | async-start | bytes 2097152 | tf_op jit(solution)/shard_map/all_to_all | solution.py:276
  225.9 2.4 fusion.19
  228.3 13.5 %all-to-all-done.2 = bf16[16,32,1024]{2,1,0:T(8,128)(2,1)S(1)} async-done(((bf16[16,32,1024]{2,1,0:T(8,128)(2,1)}), bf16[16,32,1024]{2,1,0:T(8,128)(2,1)S(1)}, u32[]{:S(2)}, u32[]{:S(2)}) %all-to-all-start.2) | async-done | bytes 1048608 | tf_op jit(solution)/shard_map/all_to_all | solution.py:276
  241.7 2.8 %collective-permute-start.25 = (bf16[512,1024]{1,0:T(8,128)(2,1)S(1)}, bf16[512,1024]{1,0:T(8,128)(2,1)}, u32[]{:S(2)}, u32[]{:S(2)}) collective-permute-start(bf16[512,1024]{1,0:T(8,128)(2,1)S(1)} %bitcast.95), channel_id=1, source_target_pairs={{0,1},{1,0},{2,3},{3,2},{4,5},{5,4},{6,7},{7,6},{8,9},{9,8},{10,11... | collective-permute-start | bytes 3145736 | tf_op jit(solution)/shard_map/ppermute | solution.py:115
  244.6 1.5 fusion.20
  246.2 0.6 collective-permute-start.23
  246.7 14.1 %collective-permute-done.23 = bf16[256,1024]{1,0:T(8,128)(2,1)S(1)} collective-permute-done((bf16[256,1024]{1,0:T(8,128)(2,1)S(1)}, bf16[256,1024]{1,0:T(8,128)(2,1)S(1)}, u32[]{:S(2)}, u32[]{:S(2)}) %collective-permute-start.23) | collective-permute-done | bytes 524320 | tf_op jit(solution)/shard_map/ppermute | solution.py:115
  260.9 2.6 fusion
  263.5 2.7 shard_map.98.refs_0_
  266.2 2.7 shard_map.99
  (40 shorter events, 0.4 us)
Async XLA Ops:
  7.2 253.7 %copy-start = (bf16[1024,1024]{1,0:T(8,128)(2,1)S(1)}, bf16[1024,1024]{1,0:T(8,128)(2,1)}, u32[]{:S(2)}) copy-start(bf16[1024,1024]{1,0:T(8,128)(2,1)} %param.11) | copy-start | bytes 6291460
  7.2 62.2 %all-gather.2.cloned.1.call-start = ((), (), s32[]{:S(2)}) async-start(), calls=%async_computation.3 | async-start | bytes 8912896 | tf_op jit(solution)/shard_map/all_gather | solution.py:288
  11.1 68.1 %copy-start.1 = (bf16[1,256,1024]{1,2,0:T(8,128)(2,1)}, bf16[1,256,1024]{1,2,0:T(8,128)(2,1)S(1)}, u32[]{:S(2)}) copy-start(bf16[1,256,1024]{1,2,0:T(8,128)(2,1)S(1)} %copy.12) | copy-start | bytes 1572868
  11.1 14.4 %collective-permute-start.4 = (bf16[1024,256]{1,0:T(8,128)(2,1)S(1)}, bf16[1024,256]{1,0:T(8,128)(2,1)S(1)}, u32[]{:S(2)}, u32[]{:S(2)}) collective-permute-start(bf16[1024,256]{1,0:T(8,128)(2,1)S(1)} %bitcast.89), channel_id=1, source_target_pairs={{0,16},{16,0},{1,17},{17,1},{2,18},{18,2},{3,19},{19,3},{4,20},{20... | collective-permute-start | bytes 1572872 | tf_op jit(solution)/shard_map/ppermute | solution.py:115
  14.9 17.9 %collective-permute-start = (bf16[1024,256]{1,0:T(8,128)(2,1)S(1)}, bf16[1024,256]{1,0:T(8,128)(2,1)}, u32[]{:S(2)}, u32[]{:S(2)}) collective-permute-start(bf16[1024,256]{1,0:T(8,128)(2,1)S(1)} %bitcast.90), channel_id=1, source_target_pairs={{0,224},{32,0},{64,32},{96,64},{128,96},{160,128},{192,160},{224,1... | collective-permute-start | bytes 1572872 | tf_op jit(solution)/shard_map/ppermute | solution.py:115
  20.5 15.0 %collective-permute-start.2 = (bf16[1024,256]{1,0:T(8,128)(2,1)S(1)}, bf16[1024,256]{1,0:T(8,128)(2,1)}, u32[]{:S(2)}, u32[]{:S(2)}) collective-permute-start(bf16[1024,256]{1,0:T(8,128)(2,1)S(1)} %bitcast.91), channel_id=1, source_target_pairs={{0,32},{32,64},{64,96},{96,128},{128,160},{160,192},{192,224},{224... | collective-permute-start | bytes 1572872 | tf_op jit(solution)/shard_map/ppermute | solution.py:115
  25.5 53.7 %copy-start.5 = (bf16[1024,256]{1,0:T(8,128)(2,1)}, bf16[1024,256]{1,0:T(8,128)(2,1)S(1)}, u32[]{:S(2)}) copy-start(bf16[1024,256]{1,0:T(8,128)(2,1)S(1)} %collective-permute-done.4.refs_13_) | copy-start | bytes 1572868
  25.5 14.6 %collective-permute-start.5 = (bf16[1024,256]{1,0:T(8,128)(2,1)S(1)}, bf16[1024,256]{1,0:T(8,128)(2,1)}, u32[]{:S(2)}, u32[]{:S(2)}) collective-permute-start(bf16[1024,256]{1,0:T(8,128)(2,1)S(1)} %collective-permute-done.4.refs_13_), channel_id=1, source_target_pairs={{0,224},{32,0},{64,32},{96,64},{128,96},{160,128},{192,160},{224,1... | collective-permute-start | bytes 1572872 | tf_op jit(solution)/shard_map/ppermute | solution.py:115
  32.8 10.9 %collective-permute-start.7 = (bf16[1024,256]{1,0:T(8,128)(2,1)S(1)}, bf16[1024,256]{1,0:T(8,128)(2,1)}, u32[]{:S(2)}, u32[]{:S(2)}) collective-permute-start(bf16[1024,256]{1,0:T(8,128)(2,1)S(1)} %collective-permute-done.4.refs_13_), channel_id=1, source_target_pairs={{0,32},{32,64},{64,96},{96,128},{128,160},{160,192},{192,224},{224... | collective-permute-start | bytes 1572872 | tf_op jit(solution)/shard_map/ppermute | solution.py:115
  32.8 18.7 %collective-permute-start.1 = (bf16[1024,256]{1,0:T(8,128)(2,1)}, bf16[1024,256]{1,0:T(8,128)(2,1)}, u32[]{:S(2)}, u32[]{:S(2)}) collective-permute-start(bf16[1024,256]{1,0:T(8,128)(2,1)} %collective-permute-done.refs_9_), channel_id=1, source_target_pairs={{0,224},{32,0},{64,32},{96,64},{128,96},{160,128},{192,160},{224,1... | collective-permute-start | bytes 1572872 | tf_op jit(solution)/shard_map/ppermute | solution.py:115
  35.4 19.2 %collective-permute-start.3 = (bf16[1024,256]{1,0:T(8,128)(2,1)}, bf16[1024,256]{1,0:T(8,128)(2,1)}, u32[]{:S(2)}, u32[]{:S(2)}) collective-permute-start(bf16[1024,256]{1,0:T(8,128)(2,1)} %collective-permute-done.2.refs_7_), channel_id=1, source_target_pairs={{0,32},{32,64},{64,96},{96,128},{128,160},{160,192},{192,224},{224... | collective-permute-start | bytes 1572872 | tf_op jit(solution)/shard_map/ppermute | solution.py:115
  40.1 22.6 %collective-permute-start.6 = (bf16[1024,256]{1,0:T(8,128)(2,1)}, bf16[1024,256]{1,0:T(8,128)(2,1)}, u32[]{:S(2)}, u32[]{:S(2)}) collective-permute-start(bf16[1024,256]{1,0:T(8,128)(2,1)} %collective-permute-done.5.refs_14_), channel_id=1, source_target_pairs={{0,224},{32,0},{64,32},{96,64},{128,96},{160,128},{192,160},{224,1... | collective-permute-start | bytes 1572872 | tf_op jit(solution)/shard_map/ppermute | solution.py:115
  43.6 22.2 %collective-permute-start.8 = (bf16[1024,256]{1,0:T(8,128)(2,1)}, bf16[1024,256]{1,0:T(8,128)(2,1)}, u32[]{:S(2)}, u32[]{:S(2)}) collective-permute-start(bf16[1024,256]{1,0:T(8,128)(2,1)} %collective-permute-done.7.refs_12_), channel_id=1, source_target_pairs={{0,32},{32,64},{64,96},{96,128},{128,160},{160,192},{192,224},{224... | collective-permute-start | bytes 1572872 | tf_op jit(solution)/shard_map/ppermute | solution.py:115
  79.2 16.5 %collective-permute-start.9 = (bf16[512,512]{1,0:T(8,128)(2,1)}, bf16[512,512]{1,0:T(8,128)(2,1)S(1)}, u32[]{:S(2)}, u32[]{:S(2)}) collective-permute-start(bf16[512,512]{1,0:T(8,128)(2,1)} %bitcast.104), channel_id=1, source_target_pairs={{0,32},{32,64},{64,96},{96,128},{128,160},{160,192},{192,224},{224... | collective-permute-start | bytes 1572872 | tf_op jit(solution)/shard_map/ppermute | solution.py:115
  80.6 17.6 %collective-permute-start.19 = (bf16[512,512]{1,0:T(8,128)(2,1)}, bf16[512,512]{1,0:T(8,128)(2,1)S(1)}, u32[]{:S(2)}, u32[]{:S(2)}) collective-permute-start(bf16[512,512]{1,0:T(8,128)(2,1)} %bitcast.103), channel_id=1, source_target_pairs={{0,224},{32,0},{64,32},{96,64},{128,96},{160,128},{192,160},{224,1... | collective-permute-start | bytes 1572872 | tf_op jit(solution)/shard_map/ppermute | solution.py:115
  84.6 22.2 %collective-permute-start.13 = (bf16[512,512]{1,0:T(8,128)(2,1)}, bf16[512,512]{1,0:T(8,128)(2,1)}, u32[]{:S(2)}, u32[]{:S(2)}) collective-permute-start(bf16[512,512]{1,0:T(8,128)(2,1)} %bitcast.102), channel_id=1, source_target_pairs={{0,224},{32,0},{64,32},{96,64},{128,96},{160,128},{192,160},{224,1... | collective-permute-start | bytes 1572872 | tf_op jit(solution)/shard_map/ppermute | solution.py:115
  95.7 0.8 copy-start.7
  97.8 17.2 %collective-permute-start.10 = (bf16[512,512]{1,0:T(8,128)(2,1)S(1)}, bf16[512,512]{1,0:T(8,128)(2,1)}, u32[]{:S(2)}, u32[]{:S(2)}) collective-permute-start(bf16[512,512]{1,0:T(8,128)(2,1)S(1)} %fusion.17), channel_id=1, source_target_pairs={{0,32},{32,64},{64,96},{96,128},{128,160},{160,192},{192,224},{224... | collective-permute-start | bytes 1572872 | tf_op jit(solution)/shard_map/ppermute | solution.py:115
  98.1 28.2 %collective-permute-start.16 = (bf16[512,512]{1,0:T(8,128)(2,1)}, bf16[512,512]{1,0:T(8,128)(2,1)}, u32[]{:S(2)}, u32[]{:S(2)}) collective-permute-start(bf16[512,512]{1,0:T(8,128)(2,1)} %bitcast.101), channel_id=1, source_target_pairs={{0,32},{32,64},{64,96},{96,128},{128,160},{160,192},{192,224},{224... | collective-permute-start | bytes 1572872 | tf_op jit(solution)/shard_map/ppermute | solution.py:115
  98.2 0.8 copy-start.6
  100.3 25.9 %collective-permute-start.20 = (bf16[512,512]{1,0:T(8,128)(2,1)S(1)}, bf16[512,512]{1,0:T(8,128)(2,1)}, u32[]{:S(2)}, u32[]{:S(2)}) collective-permute-start(bf16[512,512]{1,0:T(8,128)(2,1)S(1)} %fusion.10), channel_id=1, source_target_pairs={{0,224},{32,0},{64,32},{96,64},{128,96},{160,128},{192,160},{224,1... | collective-permute-start | bytes 1572872 | tf_op jit(solution)/shard_map/ppermute | solution.py:115
  129.1 8.2 %copy-start.2 = (bf16[512,512]{1,0:T(8,128)(2,1)S(1)}, bf16[512,512]{1,0:T(8,128)(2,1)}, u32[]{:S(2)}) copy-start(bf16[512,512]{1,0:T(8,128)(2,1)} %get-tuple-element.29.refs_2_) | copy-start | bytes 1572868
  135.8 10.8 %collective-permute-start.24 = (bf16[512,1024]{1,0:T(8,128)(2,1)}, bf16[512,1024]{1,0:T(8,128)(2,1)S(1)}, u32[]{:S(2)}, u32[]{:S(2)}) collective-permute-start(bf16[512,1024]{1,0:T(8,128)(2,1)} %shard_map.96), channel_id=1, source_target_pairs={{0,1},{1,0},{2,3},{3,2},{4,5},{5,4},{6,7},{7,6},{8,9},{9,8},{10,11... | collective-permute-start | bytes 3145736 | tf_op jit(solution)/shard_map/ppermute | solution.py:115
  137.3 23.1 %collective-permute-start.11 = (bf16[512,512]{1,0:T(8,128)(2,1)}, bf16[512,512]{1,0:T(8,128)(2,1)}, u32[]{:S(2)}, u32[]{:S(2)}) collective-permute-start(bf16[512,512]{1,0:T(8,128)(2,1)} %get-tuple-element.28.refs_3_), channel_id=1, source_target_pairs={{0,32},{32,64},{64,96},{96,128},{128,160},{160,192},{192,224},{224... | collective-permute-start | bytes 1572872 | tf_op jit(solution)/shard_map/ppermute | solution.py:115
  137.3 23.1 %collective-permute-start.14 = (bf16[512,512]{1,0:T(8,128)(2,1)S(1)}, bf16[512,512]{1,0:T(8,128)(2,1)}, u32[]{:S(2)}, u32[]{:S(2)}) collective-permute-start(bf16[512,512]{1,0:T(8,128)(2,1)S(1)} %copy-done.2), channel_id=1, source_target_pairs={{0,224},{32,0},{64,32},{96,64},{128,96},{160,128},{192,160},{224,1... | collective-permute-start | bytes 1572872 | tf_op jit(solution)/shard_map/ppermute | solution.py:115
  146.6 11.2 %copy-start.3 = (bf16[512,512]{1,0:T(8,128)(2,1)S(1)}, bf16[512,512]{1,0:T(8,128)(2,1)}, u32[]{:S(2)}) copy-start(bf16[512,512]{1,0:T(8,128)(2,1)} %get-tuple-element.33.refs_4_) | copy-start | bytes 1572868
  149.3 25.4 %all-to-all-start = ((bf16[16,32,1024]{2,1,0:T(8,128)(2,1)}), bf16[16,32,1024]{2,1,0:T(8,128)(2,1)}, u32[]{:S(2)}, u32[]{:S(2)}) async-start(bf16[16,32,1024]{2,1,0:T(8,128)(2,1)} %bitcast.94), calls=%async_computation | async-start | bytes 2097152 | tf_op jit(solution)/shard_map/all_to_all | solution.py:270
  157.7 14.2 %collective-permute-start.17 = (bf16[512,512]{1,0:T(8,128)(2,1)}, bf16[512,512]{1,0:T(8,128)(2,1)}, u32[]{:S(2)}, u32[]{:S(2)}) collective-permute-start(bf16[512,512]{1,0:T(8,128)(2,1)} %get-tuple-element.32.refs_5_), channel_id=1, source_target_pairs={{0,32},{32,64},{64,96},{96,128},{128,160},{160,192},{192,224},{224... | collective-permute-start | bytes 1572872 | tf_op jit(solution)/shard_map/ppermute | solution.py:115
  157.8 14.1 %collective-permute-start.21 = (bf16[512,512]{1,0:T(8,128)(2,1)S(1)}, bf16[512,512]{1,0:T(8,128)(2,1)}, u32[]{:S(2)}, u32[]{:S(2)}) collective-permute-start(bf16[512,512]{1,0:T(8,128)(2,1)S(1)} %copy-done.3), channel_id=1, source_target_pairs={{0,224},{32,0},{64,32},{96,64},{128,96},{160,128},{192,160},{224,1... | collective-permute-start | bytes 1572872 | tf_op jit(solution)/shard_map/ppermute | solution.py:115
  176.9 20.6 %all-to-all-start.1 = ((bf16[8,32,1024]{2,1,0:T(8,128)(2,1)}), bf16[8,32,1024]{2,1,0:T(8,128)(2,1)S(1)}, u32[]{:S(2)}, u32[]{:S(2)}) async-start(bf16[8,32,1024]{2,1,0:T(8,128)(2,1)} %broadcast_in_dim.7), calls=%async_computation.1 | async-start | bytes 1048576 | tf_op jit(solution)/shard_map/all_to_all | solution.py:273
  181.9 25.6 %collective-permute-start.12 = (bf16[512,512]{1,0:T(8,128)(2,1)}, bf16[512,512]{1,0:T(8,128)(2,1)}, u32[]{:S(2)}, u32[]{:S(2)}) collective-permute-start(bf16[512,512]{1,0:T(8,128)(2,1)} %get-tuple-element.26), channel_id=1, source_target_pairs={{0,32},{32,64},{64,96},{96,128},{128,160},{160,192},{192,224},{224... | collective-permute-start | bytes 1572872 | tf_op jit(solution)/shard_map/ppermute | solution.py:115
  183.3 24.2 %collective-permute-start.15 = (bf16[512,512]{1,0:T(8,128)(2,1)}, bf16[512,512]{1,0:T(8,128)(2,1)}, u32[]{:S(2)}, u32[]{:S(2)}) collective-permute-start(bf16[512,512]{1,0:T(8,128)(2,1)} %get-tuple-element.27), channel_id=1, source_target_pairs={{0,224},{32,0},{64,32},{96,64},{128,96},{160,128},{192,160},{224,1... | collective-permute-start | bytes 1572872 | tf_op jit(solution)/shard_map/ppermute | solution.py:115
  184.6 34.1 %collective-permute-start.18 = (bf16[512,512]{1,0:T(8,128)(2,1)}, bf16[512,512]{1,0:T(8,128)(2,1)S(1)}, u32[]{:S(2)}, u32[]{:S(2)}) collective-permute-start(bf16[512,512]{1,0:T(8,128)(2,1)} %get-tuple-element.30), channel_id=1, source_target_pairs={{0,32},{32,64},{64,96},{96,128},{128,160},{160,192},{192,224},{224... | collective-permute-start | bytes 1572872 | tf_op jit(solution)/shard_map/ppermute | solution.py:115
  184.8 33.8 %collective-permute-start.22 = (bf16[512,512]{1,0:T(8,128)(2,1)}, bf16[512,512]{1,0:T(8,128)(2,1)}, u32[]{:S(2)}, u32[]{:S(2)}) collective-permute-start(bf16[512,512]{1,0:T(8,128)(2,1)} %get-tuple-element.31), channel_id=1, source_target_pairs={{0,224},{32,0},{64,32},{96,64},{128,96},{160,128},{192,160},{224,1... | collective-permute-start | bytes 1572872 | tf_op jit(solution)/shard_map/ppermute | solution.py:115
  218.7 1.2 copy-start.8
  219.8 21.9 %all-to-all-start.2 = ((bf16[16,32,1024]{2,1,0:T(8,128)(2,1)}), bf16[16,32,1024]{2,1,0:T(8,128)(2,1)S(1)}, u32[]{:S(2)}, u32[]{:S(2)}) async-start(bf16[16,32,1024]{2,1,0:T(8,128)(2,1)} %broadcast_in_dim.8), calls=%async_computation.2 | async-start | bytes 2097152 | tf_op jit(solution)/shard_map/all_to_all | solution.py:276
  241.7 21.8 %copy-start.4 = (bf16[16,32,1024]{2,1,0:T(8,128)(2,1)}, bf16[16,32,1024]{2,1,0:T(8,128)(2,1)S(1)}, u32[]{:S(2)}) copy-start(bf16[16,32,1024]{2,1,0:T(8,128)(2,1)S(1)} %all-to-all-done.2) | copy-start | bytes 3145732
  241.7 24.5 %collective-permute-start.25 = (bf16[512,1024]{1,0:T(8,128)(2,1)S(1)}, bf16[512,1024]{1,0:T(8,128)(2,1)}, u32[]{:S(2)}, u32[]{:S(2)}) collective-permute-start(bf16[512,1024]{1,0:T(8,128)(2,1)S(1)} %bitcast.95), channel_id=1, source_target_pairs={{0,1},{1,0},{2,3},{3,2},{4,5},{5,4},{6,7},{7,6},{8,9},{9,8},{10,11... | collective-permute-start | bytes 3145736 | tf_op jit(solution)/shard_map/ppermute | solution.py:115
  246.2 14.7 %collective-permute-start.23 = (bf16[256,1024]{1,0:T(8,128)(2,1)S(1)}, bf16[256,1024]{1,0:T(8,128)(2,1)S(1)}, u32[]{:S(2)}, u32[]{:S(2)}) collective-permute-start(bf16[256,1024]{1,0:T(8,128)(2,1)S(1)} %pad_maximum_fusion), channel_id=1, source_target_pairs={{0,16},{16,0},{1,17},{17,1},{2,18},{18,2},{3,19},{19,3},{4,20},{20... | collective-permute-start | bytes 1572872 | tf_op jit(solution)/shard_map/ppermute | solution.py:115
Sparse Core Ops, SparseCore 0:
  10.4 58.8 all-gather.1

commit v3 on v2

--- a/solution.py
+++ b/solution.py
@@ -308,8 +308,8 @@
     theirs, ours = [jnp.stack([z, lax.axis_index("yh"), half]) for half in (1 - core, core)]
     theirs = weight_terms(near, partials, passing, REACH, theirs)
     ours = weight_terms(near, partials, passing, REACH, behind(ours, theirs))
-    grad_weight = sum_everywhere(ours, theirs, sent[3], arrived)
     mixed = row_sum(partials, arrived)
+    grad_weight = sum_everywhere(ours, theirs, sent[3], mixed)
     grad_in = lax.dot_general(
         mixed, weight, (((1,), (1,)), ((), ())), preferred_element_type=jnp.float32
     )

time: 276 us -> 250 us (0.906); the launches traced: 276 us -> 246 us
  waiting for transfers between devices: 122 us -> 67.8 us
  blocking collectives: 0 us -> 18.2 us
  starting transfers between devices: 76.2 us -> 82 us
    ppermute x26, waiting for transfers between devices: 94.9 us -> 64.3 us  [shift(): lax.ppermute(value, axis, [(i, (i + way) % size) for i in range(size)])]
    all_to_all x0 -> x1, blocking collectives: none -> 18.2 us  [sum_everywhere(): lax.all_to_all(jnp.broadcast_to(part[None], (side,) + part.shape), SIDE,...]
    all_to_all x1 -> x0, waiting for transfers between devices: 13.5 us -> none  [sum_everywhere(): lax.all_to_all(jnp.broadcast_to(part[None], (side,) + part.shape), SIDE,...]
    all_to_all x1, waiting for transfers between devices: 10.2 us -> 0.01 us  [sum_everywhere(): lax.all_to_all(jnp.broadcast_to(part[None], (depth,) + part.shape), 'z',...]
    ppermute x26, starting transfers between devices: 56.7 us -> 64.4 us  [shift(): lax.ppermute(value, axis, [(i, (i + way) % size) for i in range(size)])]
    all_to_all x1 -> x0, starting transfers between devices: 6.05 us -> none  [sum_everywhere(): lax.all_to_all(jnp.broadcast_to(part[None], (side,) + part.shape), SIDE,...]
    all_to_all x1, starting transfers between devices: 8.4 us -> 13.7 us  [sum_everywhere(): part = lax.all_to_all(part, SIDE, 0, 0, tiled=True)]
  transfers between devices with their start and end apart: 30 -> 29, of which waited for: 16 -> 14; matrix products, arithmetic and copies ran while one was open for 9% -> 11% of each run, Pallas kernels for 3% -> 4%
where the time goes in v3:
time: 250 us; the launch traced here: 246 us
  starting transfers between devices  82 us (33%)
  waiting for transfers between devices  67.8 us (27%)
  Pallas kernels  29.6 us (12%)
  other arithmetic  26.7 us (11%)
  blocking collectives  18.2 us (7%)
  between operations  14.9 us (6%)
  local copies, waits for them, and re-layouts  3.82 us (2%)
  matrix products  2.58 us (1%)
    ppermute x26, starting transfers between devices, shift(): lax.ppermute(value, axis, [(i, (i + way) % size) for i in range(size)])  64.4 us
    ppermute x26, waiting for transfers between devices, shift(): lax.ppermute(value, axis, [(i, (i + way) % size) for i in range(size)])  64.3 us
    all_to_all x1, blocking collectives, sum_everywhere(): lax.all_to_all(jnp.broadcast_to(part[None], (side,) + part.shape), SIDE,...  18.2 us
    convert_element_type x6, other arithmetic, row_chains(): (moving.astype(jnp.float32) + own.astype(jnp.float32)).astype(jnp.bfloat16)  13.8 us
    all_to_all x1, starting transfers between devices, sum_everywhere(): part = lax.all_to_all(part, SIDE, 0, 0, tiled=True)  13.7 us
    pallas_call x2, Pallas kernels, weight_terms(): pl.pallas_call(functools.partial(term_kernel, chunks, reach), out_shape=j...  13.3 us
    pallas_call x1, Pallas kernels, tile_sum(): pl.pallas_call(functools.partial(tile_kernel, columns), out_shape=[jax.Sh...  10.9 us
    pallas_call x2, Pallas kernels, place_half(): pl.pallas_call(place_kernel, out_shape=jax.ShapeDtypeStruct((2 * rows, wi...  5.38 us
  transfers between devices with their start and end apart: 29, of which 14 were waited for; matrix products, arithmetic and copies ran while one was open for 11% of the time, Pallas kernels for 4%

profile of v3, /device:TPU:1, one launch (start us, length us, event | category | flops | bytes accessed | tf_op | source)
XLA Modules:
  0.0 245.6 jit_solution(12731474378276813559)
XLA Ops:
  7.2 0.0 all-gather.2.cloned.1.call-start
  7.2 2.6 %fusion.6 = bf16[256,1024]{1,0:T(8,128)(2,1)} fusion(bf16[1,256,1024]{2,1,0:T(8,128)(2,1)} %param.8, bf16[1,256,1024]{2,1,0:T(8,128)(2,1)} %param.9), kind=kLoop, calls=%fused_computation.10 | loop fusion | flops 2883584 | bytes 1572864 | tf_op jit(solution)/shard_map/convert_element_type | solution.py:22
  9.8 1.2 copy.12
  11.1 3.8 %collective-permute-start.4 = (bf16[1024,256]{1,0:T(8,128)(2,1)S(1)}, bf16[1024,256]{1,0:T(8,128)(2,1)S(1)}, u32[]{:S(2)}, u32[]{:S(2)}) collective-permute-start(bf16[1024,256]{1,0:T(8,128)(2,1)S(1)} %bitcast.90), channel_id=1, source_target_pairs={{0,16},{16,0},{1,17},{17,1},{2,18},{18,2},{3,19},{19,3},{4,20},{20... | collective-permute-start | bytes 1572872 | tf_op jit(solution)/shard_map/ppermute | solution.py:115
  14.9 5.6 %collective-permute-start = (bf16[1024,256]{1,0:T(8,128)(2,1)S(1)}, bf16[1024,256]{1,0:T(8,128)(2,1)S(1)}, u32[]{:S(2)}, u32[]{:S(2)}) collective-permute-start(bf16[1024,256]{1,0:T(8,128)(2,1)S(1)} %bitcast.91), channel_id=1, source_target_pairs={{0,224},{32,0},{64,32},{96,64},{128,96},{160,128},{192,160},{224,1... | collective-permute-start | bytes 1572872 | tf_op jit(solution)/shard_map/ppermute | solution.py:115
  20.5 5.0 %collective-permute-done.4.refs_13_ = bf16[1024,256]{1,0:T(8,128)(2,1)S(1)} collective-permute-done((bf16[1024,256]{1,0:T(8,128)(2,1)S(1)}, bf16[1024,256]{1,0:T(8,128)(2,1)S(1)}, u32[]{:S(2)}, u32[]{:S(2)}) %collective-permute-start.4) | collective-permute-done | bytes 524320 | tf_op jit(solution)/shard_map/ppermute | solution.py:115
  25.5 7.3 %collective-permute-start.5 = (bf16[1024,256]{1,0:T(8,128)(2,1)S(1)}, bf16[1024,256]{1,0:T(8,128)(2,1)}, u32[]{:S(2)}, u32[]{:S(2)}) collective-permute-start(bf16[1024,256]{1,0:T(8,128)(2,1)S(1)} %collective-permute-done.4.refs_13_), channel_id=1, source_target_pairs={{0,224},{32,0},{64,32},{96,64},{128,96},{160,128},{192,160},{224,1... | collective-permute-start | bytes 1572872 | tf_op jit(solution)/shard_map/ppermute | solution.py:115
  32.8 2.7 %collective-permute-start.1 = (bf16[1024,256]{1,0:T(8,128)(2,1)S(1)}, bf16[1024,256]{1,0:T(8,128)(2,1)}, u32[]{:S(2)}, u32[]{:S(2)}) collective-permute-start(bf16[1024,256]{1,0:T(8,128)(2,1)S(1)} %collective-permute-done.refs_9_), channel_id=1, source_target_pairs={{0,224},{32,0},{64,32},{96,64},{128,96},{160,128},{192,160},{224,1... | collective-permute-start | bytes 1572872 | tf_op jit(solution)/shard_map/ppermute | solution.py:115
  35.5 4.7 %collective-permute-done.5.refs_14_ = bf16[1024,256]{1,0:T(8,128)(2,1)} collective-permute-done((bf16[1024,256]{1,0:T(8,128)(2,1)S(1)}, bf16[1024,256]{1,0:T(8,128)(2,1)}, u32[]{:S(2)}, u32[]{:S(2)}) %collective-permute-start.5) | collective-permute-done | bytes 524320 | tf_op jit(solution)/shard_map/ppermute | solution.py:115
  40.1 3.5 %collective-permute-start.6 = (bf16[1024,256]{1,0:T(8,128)(2,1)}, bf16[1024,256]{1,0:T(8,128)(2,1)}, u32[]{:S(2)}, u32[]{:S(2)}) collective-permute-start(bf16[1024,256]{1,0:T(8,128)(2,1)} %collective-permute-done.5.refs_14_), channel_id=1, source_target_pairs={{0,224},{32,0},{64,32},{96,64},{128,96},{160,128},{192,160},{224,1... | collective-permute-start | bytes 1572872 | tf_op jit(solution)/shard_map/ppermute | solution.py:115
  44.3 0.7 pad_add_fusion.send_ref
  45.0 6.4 %collective-permute-done.1.refs_10_ = bf16[1024,256]{1,0:T(8,128)(2,1)} collective-permute-done((bf16[1024,256]{1,0:T(8,128)(2,1)S(1)}, bf16[1024,256]{1,0:T(8,128)(2,1)}, u32[]{:S(2)}, u32[]{:S(2)}) %collective-permute-start.1) | collective-permute-done | bytes 524320 | tf_op jit(solution)/shard_map/ppermute | solution.py:115
  51.4 3.2 %collective-permute-done.3.refs_6_ = bf16[1024,256]{1,0:T(8,128)(2,1)} collective-permute-done((bf16[1024,256]{1,0:T(8,128)(2,1)}, bf16[1024,256]{1,0:T(8,128)(2,1)}, u32[]{:S(2)}, u32[]{:S(2)}) %collective-permute-start.3) | collective-permute-done | bytes 524320 | tf_op jit(solution)/shard_map/ppermute | solution.py:115
  54.6 8.1 %collective-permute-done.6.refs_15_ = bf16[1024,256]{1,0:T(8,128)(2,1)} collective-permute-done((bf16[1024,256]{1,0:T(8,128)(2,1)}, bf16[1024,256]{1,0:T(8,128)(2,1)}, u32[]{:S(2)}, u32[]{:S(2)}) %collective-permute-start.6) | collective-permute-done | bytes 524320 | tf_op jit(solution)/shard_map/ppermute | solution.py:115
  62.7 3.1 %collective-permute-done.8.refs_11_ = bf16[1024,256]{1,0:T(8,128)(2,1)} collective-permute-done((bf16[1024,256]{1,0:T(8,128)(2,1)}, bf16[1024,256]{1,0:T(8,128)(2,1)}, u32[]{:S(2)}, u32[]{:S(2)}) %collective-permute-start.8) | collective-permute-done | bytes 524320 | tf_op jit(solution)/shard_map/ppermute | solution.py:115
  65.8 3.5 %all-gather.2.cloned.1.call-done.panel_hbm = bf16[4096,1024]{1,0:T(8,128)(2,1)} async-done(((bf16[256,1024]{1,0:T(8,128)(2,1)}), bf16[4096,1024]{1,0:T(8,128)(2,1)}) %all-gather.2.cloned.1.call-update) | async-done | bytes 8388624 | tf_op jit(solution)/shard_map/all_gather | solution.py:288
  69.3 10.9 %shard_map.95 = (bf16[32,128,512]{2,1,0:T(8,128)(2,1)}, bf16[4,128,512]{2,1,0:T(8,128)(2,1)}, bf16[4,128,512]{2,1,0:T(8,128)(2,1)}, bf16[32,128,512]{2,1,0:T(8,1...) custom-call(s32[1]{0:T(128)} %bitcast.77.count_ref, s32[4]{0:T(128)} %pad_add_fusion.send_ref, ...), custom_call_target="tpu_custom_call" | custom-call | flops 2684354560 | bytes 19398656 | tf_op jit(solution)/shard_map/pallas_call | solution.py:87
  80.3 1.4 collective-permute-start.9
  81.6 4.9 %collective-permute-start.19 = (bf16[512,512]{1,0:T(8,128)(2,1)}, bf16[512,512]{1,0:T(8,128)(2,1)S(1)}, u32[]{:S(2)}, u32[]{:S(2)}) collective-permute-start(bf16[512,512]{1,0:T(8,128)(2,1)} %bitcast.103), channel_id=1, source_target_pairs={{0,224},{32,0},{64,32},{96,64},{128,96},{160,128},{192,160},{224,1... | collective-permute-start | bytes 1572872 | tf_op jit(solution)/shard_map/ppermute | solution.py:115
  86.5 1.4 collective-permute-start.13
  87.9 6.1 %collective-permute-done.9 = bf16[512,512]{1,0:T(8,128)(2,1)S(1)} collective-permute-done((bf16[512,512]{1,0:T(8,128)(2,1)}, bf16[512,512]{1,0:T(8,128)(2,1)S(1)}, u32[]{:S(2)}, u32[]{:S(2)}) %collective-permute-start.9) | collective-permute-done | bytes 524320 | tf_op jit(solution)/shard_map/ppermute | solution.py:115
  94.0 0.8 copy-done.8
  94.8 1.3 fusion.17
  96.2 0.9 collective-permute-start.10
  97.0 2.1 collective-permute-start.16
  99.1 0.8 copy-done.7
  99.9 1.3 fusion.10
  101.2 0.7 collective-permute-start.20
  101.9 0.6 pad_add_fusion.3.place_ref
  102.5 3.2 %collective-permute-done.13 = bf16[512,512]{1,0:T(8,128)(2,1)} collective-permute-done((bf16[512,512]{1,0:T(8,128)(2,1)}, bf16[512,512]{1,0:T(8,128)(2,1)}, u32[]{:S(2)}, u32[]{:S(2)}) %collective-permute-start.13) | collective-permute-done | bytes 524320 | tf_op jit(solution)/shard_map/ppermute | solution.py:115
  105.6 0.1 collective-permute-done.10
  105.8 2.8 %fusion.16 = (bf16[512,512]{1,0:T(8,128)(2,1)}, bf16[512,512]{1,0:T(8,128)(2,1)}) fusion(bf16[512,512]{1,0:T(8,128)(2,1)} %collective-permute-done.10, bf16[8,512,512]{2,1,0:T(8,128)(2,1)} %bitcast.85, s32[]{:T(128)S(6)} %select_n.47, s32[]{:T(128)S(6)} %select_n.50, bf16[512,512]{1,0:T(8,128)(2,1)} %collective-permute-done.13), kind=kLoop, calls=%fused_computation.30 | loop fusion | flops 2097152 | bytes 3145736 | tf_op jit(solution)/shard_map/convert_element_type | solution.py:131
  108.6 8.3 %collective-permute-done.16 = bf16[512,512]{1,0:T(8,128)(2,1)} collective-permute-done((bf16[512,512]{1,0:T(8,128)(2,1)}, bf16[512,512]{1,0:T(8,128)(2,1)}, u32[]{:S(2)}, u32[]{:S(2)}) %collective-permute-start.16) | collective-permute-done | bytes 524320 | tf_op jit(solution)/shard_map/ppermute | solution.py:115
  116.9 2.8 %fusion.12 = (bf16[512,512]{1,0:T(8,128)(2,1)}, bf16[512,512]{1,0:T(8,128)(2,1)}) fusion(bf16[512,512]{1,0:T(8,128)(2,1)} %collective-permute-done.16, bf16[8,512,512]{2,1,0:T(8,128)(2,1)} %bitcast.79, s32[]{:T(128)S(6)} %select_n.47, s32[]{:T(128)S(6)} %select_n.50, bf16[512,512]{1,0:T(8,128)(2,1)} %collective-permute-done.20), kind=kLoop, calls=%fused_computation.22 | loop fusion | flops 2097152 | bytes 3145736 | tf_op jit(solution)/shard_map/convert_element_type | solution.py:131
  119.6 6.7 %shard_map.96 = bf16[512,1024]{1,0:T(8,128)(2,1)} custom-call(s32[3]{0:T(128)} %pad_add_fusion.3.place_ref, bf16[8,512,512]{2,1,0:T(8,128)(2,1)} %bitcast.86, bf16[8,512,512]{2,1,0:T(8,128)(2,1)} %bitcast.80, bf16[512,512]{1,0:T(8,128)(2,1)} %get-tuple-element.29.refs_2_, bf16[512,512]{1,0:T(8,128)(2,1)} %get-tuple-element.28.refs_3_, ...), custom_call_target="tpu_custom_call" | custom-call | flops 2684354560 | bytes 8912896 | tf_op jit(solution)/shard_map/pallas_call | solution.py:221
  126.4 6.5 %collective-permute-start.24 = (bf16[512,1024]{1,0:T(8,128)(2,1)}, bf16[512,1024]{1,0:T(8,128)(2,1)}, u32[]{:S(2)}, u32[]{:S(2)}) collective-permute-start(bf16[512,1024]{1,0:T(8,128)(2,1)} %shard_map.96), channel_id=1, source_target_pairs={{0,1},{1,0},{2,3},{3,2},{4,5},{5,4},{6,7},{7,6},{8,9},{9,8},{10,11... | collective-permute-start | bytes 3145736 | tf_op jit(solution)/shard_map/ppermute | solution.py:115
  132.9 0.6 pad_add_fusion.1.place_ref
  133.5 3.4 %collective-permute-start.14 = (bf16[512,512]{1,0:T(8,128)(2,1)}, bf16[512,512]{1,0:T(8,128)(2,1)}, u32[]{:S(2)}, u32[]{:S(2)}) collective-permute-start(bf16[512,512]{1,0:T(8,128)(2,1)} %get-tuple-element.29.refs_2_), channel_id=1, source_target_pairs={{0,224},{32,0},{64,32},{96,64},{128,96},{160,128},{192,160},{224,1... | collective-permute-start | bytes 1572872 | tf_op jit(solution)/shard_map/ppermute | solution.py:115
  136.9 2.7 %collective-permute-start.21 = (bf16[512,512]{1,0:T(8,128)(2,1)S(1)}, bf16[512,512]{1,0:T(8,128)(2,1)}, u32[]{:S(2)}, u32[]{:S(2)}) collective-permute-start(bf16[512,512]{1,0:T(8,128)(2,1)S(1)} %copy-done.2), channel_id=1, source_target_pairs={{0,224},{32,0},{64,32},{96,64},{128,96},{160,128},{192,160},{224,1... | collective-permute-start | bytes 1572872 | tf_op jit(solution)/shard_map/ppermute | solution.py:115
  139.6 6.6 %shard_map.97 = bf16[512,1024]{1,0:T(8,128)(2,1)} custom-call(s32[3]{0:T(128)} %pad_add_fusion.1.place_ref, bf16[8,512,512]{2,1,0:T(8,128)(2,1)} %bitcast.87, bf16[8,512,512]{2,1,0:T(8,128)(2,1)} %bitcast.81, bf16[512,512]{1,0:T(8,128)(2,1)} %get-tuple-element.29.refs_2_, bf16[512,512]{1,0:T(8,128)(2,1)} %get-tuple-element.28.refs_3_, ...), custom_call_target="tpu_custom_call" | custom-call | flops 2684354560 | bytes 8912896 | tf_op jit(solution)/shard_map/pallas_call | solution.py:221
  146.2 2.9 %add_convert_fusion = bf16[512,1024]{1,0:T(8,128)(2,1)} fusion(bf16[512,1024]{1,0:T(8,128)(2,1)} %collective-permute-done.24, bf16[512,1024]{1,0:T(8,128)(2,1)} %shard_map.97), kind=kLoop, calls=%fused_computation | loop fusion | flops 2097152 | bytes 3145728 | tf_op jit(solution)/shard_map/convert_element_type | solution.py:269
  149.1 13.7 %all-to-all-start = ((bf16[16,32,1024]{2,1,0:T(8,128)(2,1)}), bf16[16,32,1024]{2,1,0:T(8,128)(2,1)}, u32[]{:S(2)}, u32[]{:S(2)}) async-start(bf16[16,32,1024]{2,1,0:T(8,128)(2,1)} %bitcast.95), calls=%async_computation | async-start | bytes 2097152 | tf_op jit(solution)/shard_map/all_to_all | solution.py:270
  162.9 2.8 %fusion.15 = (bf16[512,512]{1,0:T(8,128)(2,1)}, bf16[512,512]{1,0:T(8,128)(2,1)}) fusion(bf16[512,512]{1,0:T(8,128)(2,1)} %collective-permute-done.11, bf16[8,512,512]{2,1,0:T(8,128)(2,1)} %bitcast.88, s32[]{:T(128)S(6)} %select_n.48, s32[]{:T(128)S(6)} %select_n.51, bf16[512,512]{1,0:T(8,128)(2,1)} %collective-permute-done.14), kind=kLoop, calls=%fused_computation.28 | loop fusion | flops 2097152 | bytes 3145736 | tf_op jit(solution)/shard_map/convert_element_type | solution.py:131
  165.7 2.7 %collective-permute-start.15 = (bf16[512,512]{1,0:T(8,128)(2,1)}, bf16[512,512]{1,0:T(8,128)(2,1)}, u32[]{:S(2)}, u32[]{:S(2)}) collective-permute-start(bf16[512,512]{1,0:T(8,128)(2,1)} %get-tuple-element.27), channel_id=1, source_target_pairs={{0,224},{32,0},{64,32},{96,64},{128,96},{160,128},{192,160},{224,1... | collective-permute-start | bytes 1572872 | tf_op jit(solution)/shard_map/ppermute | solution.py:115
  168.4 2.8 %fusion.11 = (bf16[512,512]{1,0:T(8,128)(2,1)}, bf16[512,512]{1,0:T(8,128)(2,1)}) fusion(bf16[512,512]{1,0:T(8,128)(2,1)} %collective-permute-done.17, bf16[8,512,512]{2,1,0:T(8,128)(2,1)} %bitcast.82, s32[]{:T(128)S(6)} %select_n.48, s32[]{:T(128)S(6)} %select_n.51, bf16[512,512]{1,0:T(8,128)(2,1)} %collective-permute-done.21), kind=kLoop, calls=%fused_computation.20 | loop fusion | flops 2097152 | bytes 3145736 | tf_op jit(solution)/shard_map/convert_element_type | solution.py:131
  171.2 2.7 %collective-permute-start.22 = (bf16[512,512]{1,0:T(8,128)(2,1)}, bf16[512,512]{1,0:T(8,128)(2,1)}, u32[]{:S(2)}, u32[]{:S(2)}) collective-permute-start(bf16[512,512]{1,0:T(8,128)(2,1)} %get-tuple-element.31), channel_id=1, source_target_pairs={{0,224},{32,0},{64,32},{96,64},{128,96},{160,128},{192,160},{224,1... | collective-permute-start | bytes 1572872 | tf_op jit(solution)/shard_map/ppermute | solution.py:115
  173.9 5.4 %collective-permute-done.12 = bf16[512,512]{1,0:T(8,128)(2,1)} collective-permute-done((bf16[512,512]{1,0:T(8,128)(2,1)}, bf16[512,512]{1,0:T(8,128)(2,1)}, u32[]{:S(2)}, u32[]{:S(2)}) %collective-permute-start.12) | collective-permute-done | bytes 524320 | tf_op jit(solution)/shard_map/ppermute | solution.py:115
  179.3 1.5 fusion.18
  180.8 1.4 reduce_sum.24
  182.3 0.8 broadcast_in_dim.7
  183.1 3.8 %all-to-all-start.1 = ((bf16[8,32,1024]{2,1,0:T(8,128)(2,1)}), bf16[8,32,1024]{2,1,0:T(8,128)(2,1)S(1)}, u32[]{:S(2)}, u32[]{:S(2)}) async-start(bf16[8,32,1024]{2,1,0:T(8,128)(2,1)} %broadcast_in_dim.7), calls=%async_computation.1 | async-start | bytes 1048576 | tf_op jit(solution)/shard_map/all_to_all | solution.py:273
  186.9 3.6 %collective-permute-done.18 = bf16[512,512]{1,0:T(8,128)(2,1)} collective-permute-done((bf16[512,512]{1,0:T(8,128)(2,1)}, bf16[512,512]{1,0:T(8,128)(2,1)}, u32[]{:S(2)}, u32[]{:S(2)}) %collective-permute-start.18) | collective-permute-done | bytes 524320 | tf_op jit(solution)/shard_map/ppermute | solution.py:115
  190.5 1.5 fusion.19
  192.1 0.1 pad_maximum_fusion
  192.1 2.6 %collective-permute-start.23 = (bf16[256,1024]{1,0:T(8,128)(2,1)S(1)}, bf16[256,1024]{1,0:T(8,128)(2,1)S(1)}, u32[]{:S(2)}, u32[]{:S(2)}) collective-permute-start(bf16[256,1024]{1,0:T(8,128)(2,1)S(1)} %pad_maximum_fusion), channel_id=1, source_target_pairs={{0,16},{16,0},{1,17},{17,1},{2,18},{18,2},{3,19},{19,3},{4,20},{20... | collective-permute-start | bytes 1572872 | tf_op jit(solution)/shard_map/ppermute | solution.py:115
  194.7 7.0 %collective-permute-done.23 = bf16[256,1024]{1,0:T(8,128)(2,1)S(1)} collective-permute-done((bf16[256,1024]{1,0:T(8,128)(2,1)S(1)}, bf16[256,1024]{1,0:T(8,128)(2,1)S(1)}, u32[]{:S(2)}, u32[]{:S(2)}) %collective-permute-start.23) | collective-permute-done | bytes 524320 | tf_op jit(solution)/shard_map/ppermute | solution.py:115
  201.7 0.9 fusion.7
  202.7 0.1 reduce_sum.25
  202.8 0.1 broadcast_in_dim.8
  202.9 18.2 %all_to_all.15 = bf16[16,32,1024]{2,1,0:T(8,128)(2,1)S(1)} all-to-all(bf16[16,32,1024]{2,1,0:T(8,128)(2,1)S(1)} %broadcast_in_dim.8), channel_id=1, replica_groups=mesh['z'=8,'yh'=2,'x'=4,'yl'=2,'core'=2] {'yh','x','yl'}, dimensions={0} | all-to-all | bytes 2097152 | tf_op jit(solution)/shard_map/all_to_all | solution.py:276
  221.1 9.7 %collective-permute-start.25 = (bf16[512,1024]{1,0:T(8,128)(2,1)S(1)}, bf16[512,1024]{1,0:T(8,128)(2,1)}, u32[]{:S(2)}, u32[]{:S(2)}) collective-permute-start(bf16[512,1024]{1,0:T(8,128)(2,1)S(1)} %bitcast.96), channel_id=1, source_target_pairs={{0,1},{1,0},{2,3},{3,2},{4,5},{5,4},{6,7},{7,6},{8,9},{9,8},{10,11... | collective-permute-start | bytes 3145736 | tf_op jit(solution)/shard_map/ppermute | solution.py:115
  230.8 2.6 %fusion = bf16[1,256,1024]{2,1,0:T(8,128)(2,1)} fusion(bf16[256,1024]{1,0:T(8,128)(2,1)} %fusion.7, bf16[1024,1024]{1,0:T(8,128)(2,1)S(1)} %copy-done), kind=kOutput, calls=%fused_computation.4 | convolution fusion | flops 537133056 | bytes 3145728 | tf_op jit(solution)/shard_map/dot_general | solution.py:313
  233.4 2.7 %shard_map.98.refs_0_ = f32[1024,1024]{1,0:T(8,128)} custom-call(s32[1]{0:T(128)} %bitcast.44.which_ref, bf16[512,1024]{1,0:T(8,128)(2,1)} %bitcast.97), custom_call_target="tpu_custom_call" | custom-call | tf_op jit(solution)/shard_map/pallas_call | solution.py:254
  236.1 2.7 %shard_map.99 = f32[1024,1024]{1,0:T(8,128)} custom-call(s32[1]{0:T(128)} %bitcast.41.which_ref, bf16[512,1024]{1,0:T(8,128)(2,1)} %collective-permute-done.25.half_ref, f32[1024,1024]{1,0:T(8,128)} %shard_map.98.refs_0_), custom_call_target="tpu_custom_call", output_to_operand_aliasing={{}: (2, {})} | custom-call | tf_op jit(solution)/shard_map/pallas_call | solution.py:254
  (40 shorter events, 0.1 us)
Async XLA Ops:
  7.2 223.6 %copy-start = (bf16[1024,1024]{1,0:T(8,128)(2,1)S(1)}, bf16[1024,1024]{1,0:T(8,128)(2,1)}, u32[]{:S(2)}) copy-start(bf16[1024,1024]{1,0:T(8,128)(2,1)} %param.11) | copy-start | bytes 6291460
  7.2 62.2 %all-gather.2.cloned.1.call-start = ((), (), s32[]{:S(2)}) async-start(), calls=%async_computation.3 | async-start | bytes 8912896 | tf_op jit(solution)/shard_map/all_gather | solution.py:288
  11.1 69.2 %copy-start.1 = (bf16[1,256,1024]{1,2,0:T(8,128)(2,1)}, bf16[1,256,1024]{1,2,0:T(8,128)(2,1)S(1)}, u32[]{:S(2)}) copy-start(bf16[1,256,1024]{1,2,0:T(8,128)(2,1)S(1)} %copy.12) | copy-start | bytes 1572868
  11.1 14.4 %collective-permute-start.4 = (bf16[1024,256]{1,0:T(8,128)(2,1)S(1)}, bf16[1024,256]{1,0:T(8,128)(2,1)S(1)}, u32[]{:S(2)}, u32[]{:S(2)}) collective-permute-start(bf16[1024,256]{1,0:T(8,128)(2,1)S(1)} %bitcast.90), channel_id=1, source_target_pairs={{0,16},{16,0},{1,17},{17,1},{2,18},{18,2},{3,19},{19,3},{4,20},{20... | collective-permute-start | bytes 1572872 | tf_op jit(solution)/shard_map/ppermute | solution.py:115
  14.9 17.9 %collective-permute-start = (bf16[1024,256]{1,0:T(8,128)(2,1)S(1)}, bf16[1024,256]{1,0:T(8,128)(2,1)S(1)}, u32[]{:S(2)}, u32[]{:S(2)}) collective-permute-start(bf16[1024,256]{1,0:T(8,128)(2,1)S(1)} %bitcast.91), channel_id=1, source_target_pairs={{0,224},{32,0},{64,32},{96,64},{128,96},{160,128},{192,160},{224,1... | collective-permute-start | bytes 1572872 | tf_op jit(solution)/shard_map/ppermute | solution.py:115
  20.5 15.0 %collective-permute-start.2 = (bf16[1024,256]{1,0:T(8,128)(2,1)S(1)}, bf16[1024,256]{1,0:T(8,128)(2,1)}, u32[]{:S(2)}, u32[]{:S(2)}) collective-permute-start(bf16[1024,256]{1,0:T(8,128)(2,1)S(1)} %bitcast.92), channel_id=1, source_target_pairs={{0,32},{32,64},{64,96},{96,128},{128,160},{160,192},{192,224},{224... | collective-permute-start | bytes 1572872 | tf_op jit(solution)/shard_map/ppermute | solution.py:115
  25.5 9.9 %copy-start.5 = (bf16[1024,256]{1,0:T(8,128)(2,1)}, bf16[1024,256]{1,0:T(8,128)(2,1)S(1)}, u32[]{:S(2)}) copy-start(bf16[1024,256]{1,0:T(8,128)(2,1)S(1)} %collective-permute-done.4.refs_13_) | copy-start | bytes 1572868
  25.5 14.6 %collective-permute-start.5 = (bf16[1024,256]{1,0:T(8,128)(2,1)S(1)}, bf16[1024,256]{1,0:T(8,128)(2,1)}, u32[]{:S(2)}, u32[]{:S(2)}) collective-permute-start(bf16[1024,256]{1,0:T(8,128)(2,1)S(1)} %collective-permute-done.4.refs_13_), channel_id=1, source_target_pairs={{0,224},{32,0},{64,32},{96,64},{128,96},{160,128},{192,160},{224,1... | collective-permute-start | bytes 1572872 | tf_op jit(solution)/shard_map/ppermute | solution.py:115
  32.8 10.9 %collective-permute-start.7 = (bf16[1024,256]{1,0:T(8,128)(2,1)S(1)}, bf16[1024,256]{1,0:T(8,128)(2,1)}, u32[]{:S(2)}, u32[]{:S(2)}) collective-permute-start(bf16[1024,256]{1,0:T(8,128)(2,1)S(1)} %collective-permute-done.4.refs_13_), channel_id=1, source_target_pairs={{0,32},{32,64},{64,96},{96,128},{128,160},{160,192},{192,224},{224... | collective-permute-start | bytes 1572872 | tf_op jit(solution)/shard_map/ppermute | solution.py:115
  32.8 47.5 %copy-start.6 = (bf16[1024,256]{1,0:T(8,128)(2,1)}, bf16[1024,256]{1,0:T(8,128)(2,1)S(1)}, u32[]{:S(2)}) copy-start(bf16[1024,256]{1,0:T(8,128)(2,1)S(1)} %collective-permute-done.refs_9_) | copy-start | bytes 1572868
  32.8 18.6 %collective-permute-start.1 = (bf16[1024,256]{1,0:T(8,128)(2,1)S(1)}, bf16[1024,256]{1,0:T(8,128)(2,1)}, u32[]{:S(2)}, u32[]{:S(2)}) collective-permute-start(bf16[1024,256]{1,0:T(8,128)(2,1)S(1)} %collective-permute-done.refs_9_), channel_id=1, source_target_pairs={{0,224},{32,0},{64,32},{96,64},{128,96},{160,128},{192,160},{224,1... | collective-permute-start | bytes 1572872 | tf_op jit(solution)/shard_map/ppermute | solution.py:115
  35.4 19.1 %collective-permute-start.3 = (bf16[1024,256]{1,0:T(8,128)(2,1)}, bf16[1024,256]{1,0:T(8,128)(2,1)}, u32[]{:S(2)}, u32[]{:S(2)}) collective-permute-start(bf16[1024,256]{1,0:T(8,128)(2,1)} %collective-permute-done.2.refs_7_), channel_id=1, source_target_pairs={{0,32},{32,64},{64,96},{96,128},{128,160},{160,192},{192,224},{224... | collective-permute-start | bytes 1572872 | tf_op jit(solution)/shard_map/ppermute | solution.py:115
  40.1 22.6 %collective-permute-start.6 = (bf16[1024,256]{1,0:T(8,128)(2,1)}, bf16[1024,256]{1,0:T(8,128)(2,1)}, u32[]{:S(2)}, u32[]{:S(2)}) collective-permute-start(bf16[1024,256]{1,0:T(8,128)(2,1)} %collective-permute-done.5.refs_14_), channel_id=1, source_target_pairs={{0,224},{32,0},{64,32},{96,64},{128,96},{160,128},{192,160},{224,1... | collective-permute-start | bytes 1572872 | tf_op jit(solution)/shard_map/ppermute | solution.py:115
  43.6 22.2 %collective-permute-start.8 = (bf16[1024,256]{1,0:T(8,128)(2,1)}, bf16[1024,256]{1,0:T(8,128)(2,1)}, u32[]{:S(2)}, u32[]{:S(2)}) collective-permute-start(bf16[1024,256]{1,0:T(8,128)(2,1)} %collective-permute-done.7.refs_12_), channel_id=1, source_target_pairs={{0,32},{32,64},{64,96},{96,128},{128,160},{160,192},{192,224},{224... | collective-permute-start | bytes 1572872 | tf_op jit(solution)/shard_map/ppermute | solution.py:115
  80.3 13.8 %collective-permute-start.9 = (bf16[512,512]{1,0:T(8,128)(2,1)}, bf16[512,512]{1,0:T(8,128)(2,1)S(1)}, u32[]{:S(2)}, u32[]{:S(2)}) collective-permute-start(bf16[512,512]{1,0:T(8,128)(2,1)} %bitcast.104), channel_id=1, source_target_pairs={{0,32},{32,64},{64,96},{96,128},{128,160},{160,192},{192,224},{224... | collective-permute-start | bytes 1572872 | tf_op jit(solution)/shard_map/ppermute | solution.py:115
  81.6 17.5 %collective-permute-start.19 = (bf16[512,512]{1,0:T(8,128)(2,1)}, bf16[512,512]{1,0:T(8,128)(2,1)S(1)}, u32[]{:S(2)}, u32[]{:S(2)}) collective-permute-start(bf16[512,512]{1,0:T(8,128)(2,1)} %bitcast.103), channel_id=1, source_target_pairs={{0,224},{32,0},{64,32},{96,64},{128,96},{160,128},{192,160},{224,1... | collective-permute-start | bytes 1572872 | tf_op jit(solution)/shard_map/ppermute | solution.py:115
  86.5 19.1 %collective-permute-start.13 = (bf16[512,512]{1,0:T(8,128)(2,1)}, bf16[512,512]{1,0:T(8,128)(2,1)}, u32[]{:S(2)}, u32[]{:S(2)}) collective-permute-start(bf16[512,512]{1,0:T(8,128)(2,1)} %bitcast.102), channel_id=1, source_target_pairs={{0,224},{32,0},{64,32},{96,64},{128,96},{160,128},{192,160},{224,1... | collective-permute-start | bytes 1572872 | tf_op jit(solution)/shard_map/ppermute | solution.py:115
  94.0 0.8 copy-start.8
  96.2 9.6 %collective-permute-start.10 = (bf16[512,512]{1,0:T(8,128)(2,1)S(1)}, bf16[512,512]{1,0:T(8,128)(2,1)}, u32[]{:S(2)}, u32[]{:S(2)}) collective-permute-start(bf16[512,512]{1,0:T(8,128)(2,1)S(1)} %fusion.17), channel_id=1, source_target_pairs={{0,32},{32,64},{64,96},{96,128},{128,160},{160,192},{192,224},{224... | collective-permute-start | bytes 1572872 | tf_op jit(solution)/shard_map/ppermute | solution.py:115
  97.0 19.9 %collective-permute-start.16 = (bf16[512,512]{1,0:T(8,128)(2,1)}, bf16[512,512]{1,0:T(8,128)(2,1)}, u32[]{:S(2)}, u32[]{:S(2)}) collective-permute-start(bf16[512,512]{1,0:T(8,128)(2,1)} %bitcast.101), channel_id=1, source_target_pairs={{0,32},{32,64},{64,96},{96,128},{128,160},{160,192},{192,224},{224... | collective-permute-start | bytes 1572872 | tf_op jit(solution)/shard_map/ppermute | solution.py:115
  99.1 0.8 copy-start.7
  101.2 15.6 %collective-permute-start.20 = (bf16[512,512]{1,0:T(8,128)(2,1)S(1)}, bf16[512,512]{1,0:T(8,128)(2,1)}, u32[]{:S(2)}, u32[]{:S(2)}) collective-permute-start(bf16[512,512]{1,0:T(8,128)(2,1)S(1)} %fusion.10), channel_id=1, source_target_pairs={{0,224},{32,0},{64,32},{96,64},{128,96},{160,128},{192,160},{224,1... | collective-permute-start | bytes 1572872 | tf_op jit(solution)/shard_map/ppermute | solution.py:115
  119.6 17.2 %copy-start.3 = (bf16[512,512]{1,0:T(8,128)(2,1)S(1)}, bf16[512,512]{1,0:T(8,128)(2,1)}, u32[]{:S(2)}) copy-start(bf16[512,512]{1,0:T(8,128)(2,1)} %get-tuple-element.32.refs_5_) | copy-start | bytes 1572868
  119.6 17.2 %copy-start.2 = (bf16[512,512]{1,0:T(8,128)(2,1)S(1)}, bf16[512,512]{1,0:T(8,128)(2,1)}, u32[]{:S(2)}) copy-start(bf16[512,512]{1,0:T(8,128)(2,1)} %get-tuple-element.33.refs_4_) | copy-start | bytes 1572868
  126.4 19.8 %collective-permute-start.24 = (bf16[512,1024]{1,0:T(8,128)(2,1)}, bf16[512,1024]{1,0:T(8,128)(2,1)}, u32[]{:S(2)}, u32[]{:S(2)}) collective-permute-start(bf16[512,1024]{1,0:T(8,128)(2,1)} %shard_map.96), channel_id=1, source_target_pairs={{0,1},{1,0},{2,3},{3,2},{4,5},{5,4},{6,7},{7,6},{8,9},{9,8},{10,11... | collective-permute-start | bytes 3145736 | tf_op jit(solution)/shard_map/ppermute | solution.py:115
  133.5 29.4 %collective-permute-start.11 = (bf16[512,512]{1,0:T(8,128)(2,1)}, bf16[512,512]{1,0:T(8,128)(2,1)}, u32[]{:S(2)}, u32[]{:S(2)}) collective-permute-start(bf16[512,512]{1,0:T(8,128)(2,1)} %get-tuple-element.28.refs_3_), channel_id=1, source_target_pairs={{0,32},{32,64},{64,96},{96,128},{128,160},{160,192},{192,224},{224... | collective-permute-start | bytes 1572872 | tf_op jit(solution)/shard_map/ppermute | solution.py:115
  133.5 29.4 %collective-permute-start.14 = (bf16[512,512]{1,0:T(8,128)(2,1)}, bf16[512,512]{1,0:T(8,128)(2,1)}, u32[]{:S(2)}, u32[]{:S(2)}) collective-permute-start(bf16[512,512]{1,0:T(8,128)(2,1)} %get-tuple-element.29.refs_2_), channel_id=1, source_target_pairs={{0,224},{32,0},{64,32},{96,64},{128,96},{160,128},{192,160},{224,1... | collective-permute-start | bytes 1572872 | tf_op jit(solution)/shard_map/ppermute | solution.py:115
  136.9 31.5 %collective-permute-start.17 = (bf16[512,512]{1,0:T(8,128)(2,1)S(1)}, bf16[512,512]{1,0:T(8,128)(2,1)}, u32[]{:S(2)}, u32[]{:S(2)}) collective-permute-start(bf16[512,512]{1,0:T(8,128)(2,1)S(1)} %copy-done.3), channel_id=1, source_target_pairs={{0,32},{32,64},{64,96},{96,128},{128,160},{160,192},{192,224},{224... | collective-permute-start | bytes 1572872 | tf_op jit(solution)/shard_map/ppermute | solution.py:115
  136.9 31.5 %collective-permute-start.21 = (bf16[512,512]{1,0:T(8,128)(2,1)S(1)}, bf16[512,512]{1,0:T(8,128)(2,1)}, u32[]{:S(2)}, u32[]{:S(2)}) collective-permute-start(bf16[512,512]{1,0:T(8,128)(2,1)S(1)} %copy-done.2), channel_id=1, source_target_pairs={{0,224},{32,0},{64,32},{96,64},{128,96},{160,128},{192,160},{224,1... | collective-permute-start | bytes 1572872 | tf_op jit(solution)/shard_map/ppermute | solution.py:115
  149.1 31.7 %all-to-all-start = ((bf16[16,32,1024]{2,1,0:T(8,128)(2,1)}), bf16[16,32,1024]{2,1,0:T(8,128)(2,1)}, u32[]{:S(2)}, u32[]{:S(2)}) async-start(bf16[16,32,1024]{2,1,0:T(8,128)(2,1)} %bitcast.95), calls=%async_computation | async-start | bytes 2097152 | tf_op jit(solution)/shard_map/all_to_all | solution.py:270
  165.7 13.5 %collective-permute-start.12 = (bf16[512,512]{1,0:T(8,128)(2,1)}, bf16[512,512]{1,0:T(8,128)(2,1)}, u32[]{:S(2)}, u32[]{:S(2)}) collective-permute-start(bf16[512,512]{1,0:T(8,128)(2,1)} %get-tuple-element.26), channel_id=1, source_target_pairs={{0,32},{32,64},{64,96},{96,128},{128,160},{160,192},{192,224},{224... | collective-permute-start | bytes 1572872 | tf_op jit(solution)/shard_map/ppermute | solution.py:115
  165.7 13.5 %collective-permute-start.15 = (bf16[512,512]{1,0:T(8,128)(2,1)}, bf16[512,512]{1,0:T(8,128)(2,1)}, u32[]{:S(2)}, u32[]{:S(2)}) collective-permute-start(bf16[512,512]{1,0:T(8,128)(2,1)} %get-tuple-element.27), channel_id=1, source_target_pairs={{0,224},{32,0},{64,32},{96,64},{128,96},{160,128},{192,160},{224,1... | collective-permute-start | bytes 1572872 | tf_op jit(solution)/shard_map/ppermute | solution.py:115
  171.2 19.3 %collective-permute-start.18 = (bf16[512,512]{1,0:T(8,128)(2,1)}, bf16[512,512]{1,0:T(8,128)(2,1)}, u32[]{:S(2)}, u32[]{:S(2)}) collective-permute-start(bf16[512,512]{1,0:T(8,128)(2,1)} %get-tuple-element.30), channel_id=1, source_target_pairs={{0,32},{32,64},{64,96},{96,128},{128,160},{160,192},{192,224},{224... | collective-permute-start | bytes 1572872 | tf_op jit(solution)/shard_map/ppermute | solution.py:115
  171.2 19.3 %collective-permute-start.22 = (bf16[512,512]{1,0:T(8,128)(2,1)}, bf16[512,512]{1,0:T(8,128)(2,1)}, u32[]{:S(2)}, u32[]{:S(2)}) collective-permute-start(bf16[512,512]{1,0:T(8,128)(2,1)} %get-tuple-element.31), channel_id=1, source_target_pairs={{0,224},{32,0},{64,32},{96,64},{128,96},{160,128},{192,160},{224,1... | collective-permute-start | bytes 1572872 | tf_op jit(solution)/shard_map/ppermute | solution.py:115
  183.1 19.6 %all-to-all-start.1 = ((bf16[8,32,1024]{2,1,0:T(8,128)(2,1)}), bf16[8,32,1024]{2,1,0:T(8,128)(2,1)S(1)}, u32[]{:S(2)}, u32[]{:S(2)}) async-start(bf16[8,32,1024]{2,1,0:T(8,128)(2,1)} %broadcast_in_dim.7), calls=%async_computation.1 | async-start | bytes 1048576 | tf_op jit(solution)/shard_map/all_to_all | solution.py:273
  192.1 9.6 %collective-permute-start.23 = (bf16[256,1024]{1,0:T(8,128)(2,1)S(1)}, bf16[256,1024]{1,0:T(8,128)(2,1)S(1)}, u32[]{:S(2)}, u32[]{:S(2)}) collective-permute-start(bf16[256,1024]{1,0:T(8,128)(2,1)S(1)} %pad_maximum_fusion), channel_id=1, source_target_pairs={{0,16},{16,0},{1,17},{17,1},{2,18},{18,2},{3,19},{19,3},{4,20},{20... | collective-permute-start | bytes 1572872 | tf_op jit(solution)/shard_map/ppermute | solution.py:115
  221.1 12.3 %copy-start.4 = (bf16[16,32,1024]{2,1,0:T(8,128)(2,1)}, bf16[16,32,1024]{2,1,0:T(8,128)(2,1)S(1)}, u32[]{:S(2)}) copy-start(bf16[16,32,1024]{2,1,0:T(8,128)(2,1)S(1)} %all_to_all.15) | copy-start | bytes 3145732
  221.1 15.0 %collective-permute-start.25 = (bf16[512,1024]{1,0:T(8,128)(2,1)S(1)}, bf16[512,1024]{1,0:T(8,128)(2,1)}, u32[]{:S(2)}, u32[]{:S(2)}) collective-permute-start(bf16[512,1024]{1,0:T(8,128)(2,1)S(1)} %bitcast.96), channel_id=1, source_target_pairs={{0,1},{1,0},{2,3},{3,2},{4,5},{5,4},{6,7},{7,6},{8,9},{9,8},{10,11... | collective-permute-start | bytes 3145736 | tf_op jit(solution)/shard_map/ppermute | solution.py:115
Sparse Core Ops, SparseCore 0:
  10.4 58.8 all-gather.1
